TPU v7x, 32 devices: a whole 2x2x4 slice. The times are simulated.
32 devices in a mesh: ep: 8 (over z, y), tp: 4 (over x, core).
Axes of the slice: x: 2, y: 2, z: 4, core: 2. Of those that a mesh axis runs over, the one named last changes fastest.
Arguments:
- hidden_in: bfloat16 [4096, 1280], P(('ep', 'tp')), may hold values from -6 to 6
- seq_lengths: int32 [8, 3], P('ep'), may hold values from 16 to 480, as said below
- expert_ids: int32 [4096, 7], P(('ep', 'tp')), may hold values from 0 to 15, all different within a row; in each aligned block of 128 rows (0 to 127, 128 to 255, ...) at most 96 rows name the same one
- attn_gain: bfloat16 [1280], P(('ep', 'tp')), may hold values from 0.5 to 1.5
- w_query: bfloat16 [1280, 1280], P(('ep', 'tp')), may hold values from -0.15625 to 0.15625
- w_key: bfloat16 [1280, 1280], P(('ep', 'tp')), may hold values from -0.15625 to 0.15625
- w_value: bfloat16 [1280, 1280], P(('ep', 'tp')), may hold values from -0.15625 to 0.15625
- w_out: bfloat16 [1280, 1280], P(('ep', 'tp')), may hold values from -2 to 2
- ffn_gain: bfloat16 [1280], P(('ep', 'tp')), may hold values from 0.5 to 1.5
- shared_gate: bfloat16 [1280, 1792], P(('ep', 'tp')), may hold values from -0.15625 to 0.15625
- shared_up: bfloat16 [1280, 1792], P(('ep', 'tp')), may hold values from -0.15625 to 0.15625
- shared_down: bfloat16 [1792, 1280], P(('ep', 'tp')), may hold values from -0.125 to 0.125
- router: bfloat16 [1280, 16], P(('ep', 'tp')), may hold values from -0.078125 to 0.078125
- expert_gate: bfloat16 [16, 896, 1280], P('ep', 'tp'), may hold values from -0.15625 to 0.15625
- expert_up: bfloat16 [16, 896, 1280], P('ep', 'tp'), may hold values from -0.15625 to 0.15625
- expert_down: bfloat16 [16, 896, 1280], P('ep', 'tp'), may hold values from -6 to 6
- cotangent: bfloat16 [4096, 1280], P(('ep', 'tp')), may hold values from -6 to 6
Outputs:
- layer_output: bfloat16 [4096, 1280], P(('ep', 'tp'))
- input_grad: float32 [4096, 1280], P(('ep', 'tp'))
- attn_gain_grad: float32 [1280], P(('ep', 'tp'))
- query_grad: float32 [1280, 1280], P(('ep', 'tp'))
- key_grad: float32 [1280, 1280], P(('ep', 'tp'))
- value_grad: float32 [1280, 1280], P(('ep', 'tp'))
- out_proj_grad: float32 [1280, 1280], P(('ep', 'tp'))
- ffn_gain_grad: float32 [1280], P(('ep', 'tp'))
- shared_gate_grad: float32 [1280, 1792], P(('ep', 'tp'))
- shared_up_grad: float32 [1280, 1792], P(('ep', 'tp'))
- shared_down_grad: float32 [1792, 1280], P(('ep', 'tp'))
- router_grad: float32 [1280, 16], P(('ep', 'tp'))
- expert_gate_grad: float32 [16, 896, 1280], P('ep', 'tp')
- expert_up_grad: float32 [16, 896, 1280], P('ep', 'tp')
- expert_down_grad: float32 [16, 896, 1280], P('ep', 'tp')
Inputs may be any that keep to these rules, and one draw needn't show every extreme that they name: `seq_lengths`: each row holds, in order, the lengths of the three sequences of one group; they sum to 512. `expert_ids`: each token names 7 different experts; among the 128 tokens of one device no expert is named by more than 96 tokens.
All inputs are finite; a program needn't handle non-finite values.
Results may differ from a plain program's by a relative error of at most 0.019.
Values may be sent and summed in bfloat16 or wider, within the bound.
A program may use at most 384 MiB of HBM per device.

v0:
```python
import jax
import jax.numpy as jnp
from jax import lax
from jax.sharding import PartitionSpec as P

HEADS = 10


epsilon = 1e-06


def documents(positions, lengths):
    seq_ends = jnp.cumsum(lengths)
    doc_index = (positions >= seq_ends[0]).astype(jnp.int32) + (positions >= seq_ends[1]).astype(
        jnp.int32
    )
    seq_starts = jnp.where(doc_index == 0, 0, jnp.where(doc_index == 1, seq_ends[0], seq_ends[1]))
    return (doc_index, positions - seq_starts)


def rotary_tables(offsets, head_dim):
    half_dim = head_dim // 2
    frequency = 10000.0 ** (-2.0 * jnp.arange(half_dim, dtype=jnp.float32) / head_dim)
    angles = offsets.astype(jnp.float32)[:, None] * frequency[None, :]
    return (jnp.cos(angles)[:, None, :], jnp.sin(angles)[:, None, :])


def rotate(values, cosine, sine_table):
    half_dim = values.shape[-1] // 2
    first_half = values[..., :half_dim]
    second_half = values[..., half_dim:]
    return jnp.concatenate(
        [
            first_half * cosine - second_half * sine_table,
            first_half * sine_table + second_half * cosine,
        ],
        axis=-1,
    )


def swiglu_grads(grad_hidden, gate_pre, up_pre):
    sigma = jax.nn.sigmoid(gate_pre)
    grad_gate = grad_hidden * up_pre * sigma * (1.0 + gate_pre * (1.0 - sigma))
    grad_up = grad_hidden * (gate_pre * sigma)
    return (grad_gate.astype(jnp.bfloat16), grad_up.astype(jnp.bfloat16))


def norm_back(grad_normed, unit_rows, inverse, gain):
    scaled = grad_normed * gain
    return inverse * (scaled - unit_rows * jnp.mean(scaled * unit_rows, axis=-1, keepdims=True))


def dense_dot(left_side, right_side):
    return jnp.dot(left_side, right_side, preferred_element_type=jnp.float32)


def on_device(
    hidden_in,
    seq_lengths,
    expert_ids,
    attn_gain,
    w_query,
    w_key,
    w_value,
    w_out,
    ffn_gain,
    shared_gate,
    shared_up,
    shared_down,
    router,
    expert_gate,
    expert_up,
    expert_down,
    cotangent,
):
    highest = lax.Precision.HIGHEST
    tok_count = hidden_in.shape[0]
    model_width = hidden_in.shape[1]
    top_count = expert_ids.shape[1]
    exp_local = expert_gate.shape[0]
    experts = exp_local * lax.axis_size("ep")
    capacity = min(12 * tok_count // experts, tok_count)
    group_len = lax.axis_size("tp") * tok_count
    (
        gain_attn,
        full_query,
        full_key,
        full_value,
        full_out,
        gain_ffn,
        full_sgate,
        full_sup,
        full_sdown,
        full_router,
    ) = (
        lax.all_gather(attn_gain, ("ep", "tp"), axis=0, tiled=True),
        lax.all_gather(w_query, ("ep", "tp"), axis=0, tiled=True),
        lax.all_gather(w_key, ("ep", "tp"), axis=0, tiled=True),
        lax.all_gather(w_value, ("ep", "tp"), axis=0, tiled=True),
        lax.all_gather(w_out, ("ep", "tp"), axis=0, tiled=True),
        lax.all_gather(ffn_gain, ("ep", "tp"), axis=0, tiled=True),
        lax.all_gather(shared_gate, ("ep", "tp"), axis=0, tiled=True),
        lax.all_gather(shared_up, ("ep", "tp"), axis=0, tiled=True),
        lax.all_gather(shared_down, ("ep", "tp"), axis=0, tiled=True),
        lax.all_gather(router, ("ep", "tp"), axis=0, tiled=True),
    )
    query_width = full_query.shape[1]
    head_count = HEADS
    head_dim = query_width // head_count
    attn_scale = head_dim ** (-0.5)
    lengths = seq_lengths[0]
    own_pos = lax.axis_index("tp") * tok_count + jnp.arange(tok_count, dtype=jnp.int32)
    all_pos = jnp.arange(group_len, dtype=jnp.int32)
    own_doc, own_offset = documents(own_pos, lengths)
    all_doc, all_offset = documents(all_pos, lengths)
    allowed = (own_doc[:, None] == all_doc[None, :]) & (own_pos[:, None] >= all_pos[None, :])
    cosine, sine_table = rotary_tables(own_offset, head_dim)
    inputs = hidden_in.astype(jnp.float32)
    inverse_one = lax.rsqrt(jnp.mean(inputs * inputs, axis=-1, keepdims=True) + epsilon)
    unit_one = inputs * inverse_one
    gain_one = gain_attn.astype(jnp.float32)
    normed = (unit_one * gain_one).astype(jnp.bfloat16)
    queries = rotate(
        dense_dot(normed, full_query).reshape(tok_count, head_count, head_dim), cosine, sine_table
    ).astype(jnp.bfloat16)
    key_own = (
        rotate(
            dense_dot(normed, full_key).reshape(tok_count, head_count, head_dim), cosine, sine_table
        )
        .astype(jnp.bfloat16)
        .reshape(tok_count, query_width)
    )
    value_own = dense_dot(normed, full_value).astype(jnp.bfloat16)
    key_group, value_group = (
        lax.all_gather(key_own, "tp", axis=0, tiled=True),
        lax.all_gather(value_own, "tp", axis=0, tiled=True),
    )
    key_rows = key_group.reshape(group_len, head_count, head_dim)
    value_rows = value_group.reshape(group_len, head_count, head_dim)

    def masked_scores():
        raw_scores = (
            jnp.einsum("qhd,khd->hqk", queries, key_rows, preferred_element_type=jnp.float32)
            * attn_scale
        )
        return jnp.where(allowed[None], raw_scores, -1e30)

    scores = masked_scores()
    row_peak = jnp.max(scores, axis=-1, keepdims=True)
    row_total = jnp.sum(jnp.exp(scores - row_peak), axis=-1, keepdims=True)
    softmaxed = jnp.exp(scores - row_peak) / row_total
    attended = (
        jnp.einsum(
            "hqk,khd->qhd",
            softmaxed.astype(jnp.bfloat16),
            value_rows,
            preferred_element_type=jnp.float32,
        )
        .reshape(tok_count, query_width)
        .astype(jnp.bfloat16)
    )
    residual = inputs + dense_dot(attended, full_out)
    inverse_two = lax.rsqrt(jnp.mean(residual * residual, axis=-1, keepdims=True) + epsilon)
    unit_two = residual * inverse_two
    gain_two = gain_ffn.astype(jnp.float32)
    normed_two = (unit_two * gain_two).astype(jnp.bfloat16)
    shared_gate_pre = dense_dot(normed_two, full_sgate)
    shared_up_pre = dense_dot(normed_two, full_sup)
    shared_act = (jax.nn.silu(shared_gate_pre) * shared_up_pre).astype(jnp.bfloat16)
    shared_out = dense_dot(shared_act, full_sdown)
    logits = dense_dot(normed_two, full_router)
    affinity = jax.nn.softmax(logits, axis=-1)
    expert_range = jnp.arange(experts, dtype=jnp.int32)
    choose = (expert_ids[:, :, None] == expert_range[None, None, :]).astype(jnp.float32)
    gate_values = jnp.einsum("tje,te->tj", choose, affinity, precision=highest)
    flat_ids = expert_ids.reshape(-1)
    route_hits = (flat_ids[:, None] == expert_range[None, :]).astype(jnp.int32)
    route_rank = jnp.sum(jnp.cumsum(route_hits, axis=0) * route_hits, axis=1) - 1
    slot_index = route_rank * experts + flat_ids
    route_rows = jnp.broadcast_to(
        normed_two[:, None, :], (tok_count, top_count, model_width)
    ).reshape(tok_count * top_count, model_width)
    send_rows = (
        jnp.zeros((capacity * experts, model_width), jnp.bfloat16)
        .at[slot_index]
        .set(route_rows)
        .reshape(capacity, experts, model_width)
    )
    received = lax.all_to_all(send_rows, "ep", split_axis=1, concat_axis=0, tiled=True)
    group_rows = lax.all_gather(received, "tp", axis=0, tiled=True)
    gate_pre = jnp.einsum(
        "rek,efk->ref", group_rows, expert_gate, preferred_element_type=jnp.float32
    )
    up_pre = jnp.einsum("rek,efk->ref", group_rows, expert_up, preferred_element_type=jnp.float32)
    expert_act = (jax.nn.silu(gate_pre) * up_pre).astype(jnp.bfloat16)
    expert_out = lax.psum_scatter(
        jnp.einsum("ref,efk->rek", expert_act, expert_down, preferred_element_type=jnp.float32),
        "tp",
        scatter_dimension=0,
        tiled=True,
    )
    returned = lax.all_to_all(
        expert_out.astype(jnp.bfloat16), "ep", split_axis=0, concat_axis=1, tiled=True
    )
    routed = (
        returned.reshape(capacity * experts, model_width)[slot_index]
        .reshape(tok_count, top_count, model_width)
        .astype(jnp.float32)
    )
    routed_sum = jnp.einsum("tj,tjd->td", gate_values, routed, precision=highest)
    layer_output = (residual + shared_out + routed_sum).astype(jnp.bfloat16)
    grad_out = cotangent.astype(jnp.float32)
    grad_gates = jnp.einsum("tjd,td->tj", routed, grad_out, precision=highest)
    grad_affinity = jnp.einsum("tj,tje->te", grad_gates, choose, precision=highest)
    grad_logits = affinity * (
        grad_affinity - jnp.sum(affinity * grad_affinity, axis=-1, keepdims=True)
    )
    route_grads = (
        (gate_values[:, :, None] * grad_out[:, None, :])
        .astype(jnp.bfloat16)
        .reshape(tok_count * top_count, model_width)
    )
    send_grads = (
        jnp.zeros((capacity * experts, model_width), jnp.bfloat16)
        .at[slot_index]
        .set(route_grads)
        .reshape(capacity, experts, model_width)
    )
    grad_received = lax.all_to_all(send_grads, "ep", split_axis=1, concat_axis=0, tiled=True)
    grad_rows = lax.all_gather(grad_received, "tp", axis=0, tiled=True)
    grad_hidden = jnp.einsum(
        "rek,efk->ref", grad_rows, expert_down, preferred_element_type=jnp.float32
    )
    grad_down_w = jnp.einsum(
        "ref,rek->efk", expert_act, grad_rows, preferred_element_type=jnp.float32
    )
    grad_gate_pre, grad_up_pre = swiglu_grads(grad_hidden, gate_pre, up_pre)
    grad_gate_w = jnp.einsum(
        "ref,rek->efk", grad_gate_pre, group_rows, preferred_element_type=jnp.float32
    )
    grad_up_w = jnp.einsum(
        "ref,rek->efk", grad_up_pre, group_rows, preferred_element_type=jnp.float32
    )
    grad_inputs = lax.psum_scatter(
        jnp.einsum("ref,efk->rek", grad_gate_pre, expert_gate, preferred_element_type=jnp.float32)
        + jnp.einsum("ref,efk->rek", grad_up_pre, expert_up, preferred_element_type=jnp.float32),
        "tp",
        scatter_dimension=0,
        tiled=True,
    )
    grad_back = lax.all_to_all(
        grad_inputs.astype(jnp.bfloat16), "ep", split_axis=0, concat_axis=1, tiled=True
    )
    routed_back = (
        grad_back.reshape(capacity * experts, model_width)[slot_index]
        .reshape(tok_count, top_count, model_width)
        .astype(jnp.float32)
    )
    grad_shared_hidden = dense_dot(cotangent, full_sdown.T)
    grad_sdown = dense_dot(shared_act.T, cotangent)
    grad_sgate_pre, grad_sup_pre = swiglu_grads(grad_shared_hidden, shared_gate_pre, shared_up_pre)
    grad_sgate = dense_dot(normed_two.T, grad_sgate_pre)
    grad_sup = dense_dot(normed_two.T, grad_sup_pre)
    router_full = full_router.astype(jnp.float32)
    grad_normed_two = (
        jnp.sum(routed_back, axis=1)
        + dense_dot(grad_sgate_pre, full_sgate.T)
        + dense_dot(grad_sup_pre, full_sup.T)
        + jnp.dot(grad_logits, router_full.T, precision=highest)
    )
    grad_router = jnp.dot(normed_two.astype(jnp.float32).T, grad_logits, precision=highest)
    grad_gain_two = jnp.sum(grad_normed_two * unit_two, axis=0)
    grad_resid = grad_out + norm_back(grad_normed_two, unit_two, inverse_two, gain_two)
    grad_resid_low = grad_resid.astype(jnp.bfloat16)
    grad_wout = dense_dot(attended.T, grad_resid_low)
    grad_att = (
        dense_dot(grad_resid_low, full_out.T)
        .astype(jnp.bfloat16)
        .reshape(tok_count, head_count, head_dim)
    )
    scores_again = masked_scores()
    softmax_again = jnp.exp(scores_again - row_peak) / row_total
    grad_soft = jnp.einsum("qhd,khd->hqk", grad_att, value_rows, preferred_element_type=jnp.float32)
    grad_scores = (
        softmax_again * (grad_soft - jnp.sum(softmax_again * grad_soft, axis=-1, keepdims=True))
    ).astype(jnp.bfloat16)
    grad_queries = (
        jnp.einsum("hqk,khd->qhd", grad_scores, key_rows, preferred_element_type=jnp.float32)
        * attn_scale
    )
    grad_key_rows = (
        jnp.einsum("hqk,qhd->khd", grad_scores, queries, preferred_element_type=jnp.float32)
        * attn_scale
    )
    grad_value_rows = jnp.einsum(
        "hqk,qhd->khd",
        softmax_again.astype(jnp.bfloat16),
        grad_att,
        preferred_element_type=jnp.float32,
    )
    grad_key_own, grad_value_own = (
        lax.psum_scatter(
            grad_key_rows.reshape(group_len, query_width), "tp", scatter_dimension=0, tiled=True
        ),
        lax.psum_scatter(
            grad_value_rows.reshape(group_len, query_width), "tp", scatter_dimension=0, tiled=True
        ),
    )
    grad_q_pre = (
        rotate(grad_queries, cosine, -sine_table)
        .reshape(tok_count, query_width)
        .astype(jnp.bfloat16)
    )
    grad_k_pre = (
        rotate(grad_key_own.reshape(tok_count, head_count, head_dim), cosine, -sine_table)
        .reshape(tok_count, query_width)
        .astype(jnp.bfloat16)
    )
    grad_v_pre = grad_value_own.astype(jnp.bfloat16)
    grad_wq = dense_dot(normed.T, grad_q_pre)
    grad_wk = dense_dot(normed.T, grad_k_pre)
    grad_wv = dense_dot(normed.T, grad_v_pre)
    grad_normed = (
        dense_dot(grad_q_pre, full_query.T)
        + dense_dot(grad_k_pre, full_key.T)
        + dense_dot(grad_v_pre, full_value.T)
    )
    grad_gain_one = jnp.sum(grad_normed * unit_one, axis=0)
    input_grad = grad_resid + norm_back(grad_normed, unit_one, inverse_one, gain_one)
    (
        grad_attn_gain,
        grad_query,
        grad_key,
        grad_value,
        grad_outproj,
        grad_ffn_gain,
        grad_shared_gate,
        grad_shared_up,
        grad_shared_down,
        grad_router_w,
    ) = (
        lax.psum_scatter(grad_gain_one, ("ep", "tp"), scatter_dimension=0, tiled=True),
        lax.psum_scatter(grad_wq, ("ep", "tp"), scatter_dimension=0, tiled=True),
        lax.psum_scatter(grad_wk, ("ep", "tp"), scatter_dimension=0, tiled=True),
        lax.psum_scatter(grad_wv, ("ep", "tp"), scatter_dimension=0, tiled=True),
        lax.psum_scatter(grad_wout, ("ep", "tp"), scatter_dimension=0, tiled=True),
        lax.psum_scatter(grad_gain_two, ("ep", "tp"), scatter_dimension=0, tiled=True),
        lax.psum_scatter(grad_sgate, ("ep", "tp"), scatter_dimension=0, tiled=True),
        lax.psum_scatter(grad_sup, ("ep", "tp"), scatter_dimension=0, tiled=True),
        lax.psum_scatter(grad_sdown, ("ep", "tp"), scatter_dimension=0, tiled=True),
        lax.psum_scatter(grad_router, ("ep", "tp"), scatter_dimension=0, tiled=True),
    )
    return (
        layer_output,
        input_grad,
        grad_attn_gain,
        grad_query,
        grad_key,
        grad_value,
        grad_outproj,
        grad_ffn_gain,
        grad_shared_gate,
        grad_shared_up,
        grad_shared_down,
        grad_router_w,
        grad_gate_w,
        grad_up_w,
        grad_down_w,
    )


def solution(mesh):
    placed = (
        P(("ep", "tp"), None),
        P("ep", None),
        P(("ep", "tp"), None),
        P(("ep", "tp")),
        P(("ep", "tp"), None),
        P(("ep", "tp"), None),
        P(("ep", "tp"), None),
        P(("ep", "tp"), None),
        P(("ep", "tp")),
        P(("ep", "tp"), None),
        P(("ep", "tp"), None),
        P(("ep", "tp"), None),
        P(("ep", "tp"), None),
        P("ep", "tp", None),
        P("ep", "tp", None),
        P("ep", "tp", None),
        P(("ep", "tp"), None),
    )
    return jax.shard_map(
        on_device,
        mesh=mesh,
        in_specs=placed,
        out_specs=(
            P(("ep", "tp"), None),
            P(("ep", "tp"), None),
            P(("ep", "tp")),
            P(("ep", "tp"), None),
            P(("ep", "tp"), None),
            P(("ep", "tp"), None),
            P(("ep", "tp"), None),
            P(("ep", "tp")),
            P(("ep", "tp"), None),
            P(("ep", "tp"), None),
            P(("ep", "tp"), None),
            P(("ep", "tp"), None),
            P("ep", "tp", None),
            P("ep", "tp", None),
            P("ep", "tp", None),
        ),
        check_vma=False,
    )
```

profile of v0, /device:TPU:0, one launch (start us, length us, event | category | flops | bytes accessed | tf_op | source)
XLA Modules:
  0.0 2744.6 jit_solution(11377397632742083975)
XLA Ops:
  11.2 42.2 %all-reduce.6 = (bf16[1280]{0:T(1024)(128)(2,1)S(1)}, bf16[1280]{0:T(1024)(128)(2,1)S(1)}) all-reduce(bf16[1280]{0:T(1024)(128)(2,1)S(1)} %dynamic-update-slice, bf16[1280]{0:T(1024)(128)(2,1)S(1)} %dynamic-update-slice.1), channel_id=1, replica_groups=mesh['ep'=8,'tp'=4] {'ep','tp'}, use_global_device_ids=true, to_apply=%add | all-reduce | flops 2560 | bytes 10240
  55.9 17.0 all-gather.13.cloned.1.call-done
  78.7 55.3 %all-gather.17.cloned.1.call-done = bf16[1280,1280]{1,0:T(8,128)(2,1)} async-done(((bf16[40,1280]{1,0:T(8,128)(2,1)}), bf16[1280,1280]{1,0:T(8,128)(2,1)}) %all-gather.17.cloned.1.call-update) | async-done | bytes 3276816 | tf_op jit(solution)/shard_map/all_gather | solution.py:97
  137.8 57.1 %all-gather.19.cloned.1.call-done = bf16[1280,1280]{1,0:T(8,128)(2,1)} async-done(((bf16[40,1280]{1,0:T(8,128)(2,1)}), bf16[1280,1280]{1,0:T(8,128)(2,1)}) %all-gather.19.cloned.1.call-update) | async-done | bytes 3276816 | tf_op jit(solution)/shard_map/all_gather | solution.py:98
  215.7 18.7 all-gather.21.cloned.1.call-done
  234.4 4.1 fusion.87
  240.9 55.5 %all-gather.23.cloned.1.call-done = bf16[1280,1280]{1,0:T(8,128)(2,1)} async-done(((bf16[40,1280]{1,0:T(8,128)(2,1)}), bf16[1280,1280]{1,0:T(8,128)(2,1)}) %all-gather.23.cloned.1.call-update) | async-done | bytes 3276816 | tf_op jit(solution)/shard_map/all_gather | solution.py:100
  301.8 4.2 reshape.377
  306.1 9.1 scatter_custom_fusion
  318.5 92.1 %all_to_all.66 = bf16[96,16,1280]{2,0,1:T(8,128)(2,1)S(1)} all-to-all(bf16[96,16,1280]{2,0,1:T(8,128)(2,1)S(1)} %copy.119), channel_id=1, replica_groups=mesh['ep'=8,'tp'=4] {'ep'}, dimensions={1} | all-to-all | bytes 7864320 | tf_op jit(solution)/shard_map/all_to_all | solution.py:189
  413.6 39.8 %all-gather = bf16[32,40,16]{1,2,0:T(8,128)(2,1)S(1)} all-gather(bf16[1,40,16]{1,2,0:T(8,128)(2,1)S(1)} %bitcast.232), channel_id=1, replica_groups=mesh['ep'=8,'tp'=4] {'ep','tp'}, dimensions={0}, use_global_device_ids=true | all-gather | bytes 42240 | tf_op jit(solution)/shard_map/all_gather | solution.py:105
  456.3 5.3 mul.372
  463.3 13.0 scatter_custom_fusion.1
  479.6 90.8 %all_to_all.67 = bf16[96,16,1280]{2,0,1:T(8,128)(2,1)S(1)} all-to-all(bf16[96,16,1280]{2,0,1:T(8,128)(2,1)S(1)} %copy.123), channel_id=1, replica_groups=mesh['ep'=8,'tp'=4] {'ep'}, dimensions={1} | all-to-all | bytes 7864320 | tf_op jit(solution)/shard_map/all_to_all | solution.py:229
  573.8 11.0 fusion.92
  584.8 11.5 fusion.91
  596.2 74.5 %all-gather.33.cloned.1.call-done = bf16[3072,2,1280]{2,0,1:T(8,128)(2,1)} async-done(((bf16[768,2,1280]{2,0,1:T(8,128)(2,1)}), bf16[3072,2,1280]{2,0,1:T(8,128)(2,1)}) %all-gather.33.cloned.1.call-update) | async-done | bytes 15728656 | tf_op jit(solution)/shard_map/all_gather | solution.py:230
  670.8 13.7 fusion.4
  684.5 17.0 fusion.93
  701.5 23.0 add_bitcast_fusion
  724.7 22.5 convolution_bitcast_fusion
  748.5 197.6 %reduce-scatter.15.cloned.1.call-done = f32[768,2,1280]{2,0,1:T(8,128)} async-done(((f32[3072,2,1280]{2,0,1:T(8,128)}), f32[768,2,1280]{2,0,1:T(8,128)}) %reduce-scatter.15.cloned.1.call-update) | async-done | bytes 7864336 | tf_op jit(solution)/shard_map/reduce_scatter | solution.py:244
  949.8 6.0 copy.125
  955.8 5.9 all-to-all-start.3
  962.5 207.9 %reduce-scatter.13.cloned.1.call-done = f32[768,2,1280]{2,0,1:T(8,128)} async-done(((f32[3072,2,1280]{2,0,1:T(8,128)}), f32[768,2,1280]{2,0,1:T(8,128)}) %reduce-scatter.13.cloned.1.call-update) | async-done | bytes 7864336 | tf_op jit(solution)/shard_map/reduce_scatter | solution.py:196
  1174.0 6.1 copy.121
  1180.1 5.5 all-to-all-start.1
  1185.7 110.7 %all-gather.27.cloned.1.call-done = bf16[1280,1792]{1,0:T(8,128)(2,1)} async-done(((bf16[40,1792]{1,0:T(8,128)(2,1)}), bf16[1280,1792]{1,0:T(8,128)(2,1)}) %all-gather.27.cloned.1.call-update) | async-done | bytes 4587536 | tf_op jit(solution)/shard_map/all_gather | solution.py:103
  1296.4 4.0 fusion.90
  1300.4 59.7 %all-gather.25.cloned.1.call-done = bf16[1280,1792]{1,0:T(8,128)(2,1)} async-done(((bf16[40,1792]{1,0:T(8,128)(2,1)}), bf16[1280,1792]{1,0:T(8,128)(2,1)}) %all-gather.25.cloned.1.call-update) | async-done | bytes 4587536 | tf_op jit(solution)/shard_map/all_gather | solution.py:102
  1360.1 4.0 fusion.89
  1364.1 60.8 %all-gather.29.cloned.1.call-done = bf16[1792,1280]{1,0:T(8,128)(2,1)} async-done(((bf16[56,1280]{1,0:T(8,128)(2,1)}), bf16[1792,1280]{1,0:T(8,128)(2,1)}) %all-gather.29.cloned.1.call-update) | async-done | bytes 4587536 | tf_op jit(solution)/shard_map/all_gather | solution.py:104
  1424.9 4.5 multiply_convert_fusion.3
  1429.4 7.2 copy.166
  1436.6 9.4 reshape.351
  1446.0 9.0 gather_fusion.1
  1455.0 4.7 reshape.356
  1459.7 6.8 copy.167
  1466.5 9.0 reshape.348
  1475.6 9.0 gather_fusion
  1484.5 4.3 reshape.349
  1492.9 4.0 reduce_sum.113
  1496.9 3.9 convolution_add_fusion.5
  1500.9 4.0 convolution_add_fusion.4
  1509.0 4.1 fusion.35
  1520.1 6.0 fusion.96
  1526.2 6.0 fusion.95
  1533.1 5.0 fusion.97
  1546.2 4.9 fusion.43
  1553.8 29.6 %reduce-scatter.17.cloned.1.call-done = f32[128,1280]{0,1:T(8,128)} async-done(((f32[512,1280]{0,1:T(8,128)}), f32[128,1280]{0,1:T(8,128)}) %reduce-scatter.17.cloned.1.call-update) | async-done | bytes 655376 | tf_op jit(solution)/shard_map/reduce_scatter | solution.py:302
  1590.2 3.9 fusion.74
  1595.6 3.9 fusion.76
  1599.5 11.6 fusion.100
  1611.1 9.3 fusion.99
  1620.5 9.0 fusion.98
  1633.3 75.0 %all-reduce.9.cloned.1.call-done = f32[1280,16]{0,1:T(8,128)} async-done(((f32[1280,16]{0,1:T(8,128)}), f32[1280,16]{0,1:T(8,128)}) %all-reduce.9.cloned.1.call-update) | async-done | bytes 81936
  1717.2 44.7 %all-reduce.5 = (f32[1280]{0:T(1024)S(1)}, f32[1280]{0:T(1024)S(1)}) all-reduce(f32[1280]{0:T(1024)S(1)} %get-tuple-element.17, f32[1280]{0:T(1024)S(1)} %get-tuple-element.15), channel_id=6, replica_groups=mesh['ep'=8,'tp'=4] {'ep','tp'}, use_global_device_ids=true, to_apply=%region_22.23.clone | all-reduce | flops 2560 | bytes 20480
  1765.2 98.2 %reduce-scatter.31.cloned.1.call-done = f32[40,1792]{1,0:T(8,128)} async-done(((f32[1280,1792]{1,0:T(8,128)}), f32[40,1792]{1,0:T(8,128)}) %reduce-scatter.31.cloned.1.call-update) | async-done | bytes 286736 | tf_op jit(solution)/shard_map/reduce_scatter | solution.py:349
  1863.4 148.9 %reduce-scatter.29.cloned.1.call-done = f32[40,1792]{1,0:T(8,128)} async-done(((f32[1280,1792]{1,0:T(8,128)}), f32[40,1792]{1,0:T(8,128)}) %reduce-scatter.29.cloned.1.call-update) | async-done | bytes 286736 | tf_op jit(solution)/shard_map/reduce_scatter | solution.py:348
  2012.3 149.0 %reduce-scatter.33.cloned.1.call-done = f32[56,1280]{1,0:T(8,128)} async-done(((f32[1792,1280]{1,0:T(8,128)}), f32[56,1280]{1,0:T(8,128)}) %reduce-scatter.33.cloned.1.call-update) | async-done | bytes 286736 | tf_op jit(solution)/shard_map/reduce_scatter | solution.py:350
  2161.3 143.7 %reduce-scatter.27.cloned.1.call-done = f32[40,1280]{1,0:T(8,128)} async-done(((f32[1280,1280]{1,0:T(8,128)}), f32[40,1280]{1,0:T(8,128)}) %reduce-scatter.27.cloned.1.call-update) | async-done | bytes 204816 | tf_op jit(solution)/shard_map/reduce_scatter | solution.py:346
  2305.0 144.1 %reduce-scatter.25.cloned.1.call-done = f32[40,1280]{1,0:T(8,128)} async-done(((f32[1280,1280]{1,0:T(8,128)}), f32[40,1280]{1,0:T(8,128)}) %reduce-scatter.25.cloned.1.call-update) | async-done | bytes 204816 | tf_op jit(solution)/shard_map/reduce_scatter | solution.py:345
  2449.1 144.2 %reduce-scatter.23.cloned.1.call-done = f32[40,1280]{1,0:T(8,128)} async-done(((f32[1280,1280]{1,0:T(8,128)}), f32[40,1280]{1,0:T(8,128)}) %reduce-scatter.23.cloned.1.call-update) | async-done | bytes 204816 | tf_op jit(solution)/shard_map/reduce_scatter | solution.py:344
  2593.3 144.3 %reduce-scatter.21.cloned.1.call-done = f32[40,1280]{1,0:T(8,128)} async-done(((f32[1280,1280]{1,0:T(8,128)}), f32[40,1280]{1,0:T(8,128)}) %reduce-scatter.21.cloned.1.call-update) | async-done | bytes 204816 | tf_op jit(solution)/shard_map/reduce_scatter | solution.py:343
  (272 shorter events, 122.5 us)
Async XLA Ops:
  7.2 663.6 %copy-start = (bf16[2,224,1280]{2,1,0:T(8,128)(2,1)S(1)}, bf16[2,224,1280]{2,1,0:T(8,128)(2,1)}, u32[]{:S(2)}) copy-start(bf16[2,224,1280]{2,1,0:T(8,128)(2,1)} %param.32) | copy-start | bytes 3440644
  7.2 126.7 %copy-start.2 = (bf16[128,1280]{1,0:T(8,128)(2,1)S(1)}, bf16[128,1280]{1,0:T(8,128)(2,1)}, u32[]{:S(2)}) copy-start(bf16[128,1280]{1,0:T(8,128)(2,1)} %param.17) | copy-start | bytes 983044
  7.2 65.7 %all-gather.13.cloned.1.call-start = ((), (), s32[]{:S(2)}) async-start(), calls=%async_computation.15 | async-start | bytes 3379200 | tf_op jit(solution)/shard_map/all_gather | solution.py:99
  7.9 126.0 %all-gather.17.cloned.1.call-start = ((), (), s32[]{:S(2)}) async-start(), calls=%async_computation.17 | async-start | bytes 3379200 | tf_op jit(solution)/shard_map/all_gather | solution.py:97
  8.7 186.3 %all-gather.19.cloned.1.call-start = ((), (), s32[]{:S(2)}) async-start(), calls=%async_computation.18 | async-start | bytes 3379200 | tf_op jit(solution)/shard_map/all_gather | solution.py:98
  9.4 204.6 %all-gather.15.cloned.1.call-start = ((), (), s32[]{:S(2)}) async-start(), calls=%async_computation.16 | async-start | bytes 1638400 | tf_op jit(solution)/shard_map/all_gather | solution.py:136
  53.4 141.6 %copy-start.32 = (f32[1280]{0:T(1024)}, f32[1280]{0:T(1024)S(1)}, u32[]{:S(2)}) copy-start(f32[1280]{0:T(1024)S(1)} %convert_element_type.148) | copy-start | bytes 15364
  55.9 139.1 %copy-start.49 = (f32[128]{0:T(128)}, f32[128]{0:T(128)S(1)}, u32[]{:S(2)}) copy-start(f32[128]{0:T(128)S(1)} %add_rsqrt_fusion.1) | copy-start | bytes 1540
  76.3 158.1 %all-gather.21.cloned.1.call-start = ((), (), s32[]{:S(2)}) async-start(), calls=%async_computation.19 | async-start | bytes 1638400 | tf_op jit(solution)/shard_map/all_gather | solution.py:135
  78.7 123.8 %copy-start.38 = (f32[128,64]{1,0:T(8,128)}, f32[128,64]{1,0:T(8,128)S(1)}, u32[]{:S(2)}) copy-start(f32[128,64]{1,0:T(8,128)S(1)} %get-tuple-element.49) | copy-start | bytes 98308
  202.5 4.3 copy-start.59
  204.8 29.6 %copy-start.24 = (bf16[128,10,64]{2,0,1:T(8,128)(2,1)S(1)}, bf16[128,10,64]{2,0,1:T(8,128)(2,1)}, u32[]{:S(2)}) copy-start(bf16[128,10,64]{2,0,1:T(8,128)(2,1)} %get-tuple-element.31) | copy-start | bytes 491524
  204.8 29.6 %copy-start.26 = (bf16[128,10,64]{2,0,1:T(8,128)(2,1)S(1)}, bf16[128,10,64]{2,0,1:T(8,128)(2,1)}, u32[]{:S(2)}) copy-start(bf16[128,10,64]{2,0,1:T(8,128)(2,1)} %get-tuple-element.32) | copy-start | bytes 491524
  205.9 90.5 %all-gather.23.cloned.1.call-start = ((), (), s32[]{:S(2)}) async-start(), calls=%async_computation.20 | async-start | bytes 3379200 | tf_op jit(solution)/shard_map/all_gather | solution.py:100
  206.5 366.5 %all-gather.31.cloned.1.call-start = ((), (), s32[]{:S(2)}) async-start(), calls=%async_computation.24 | async-start | bytes 19660800 | tf_op jit(solution)/shard_map/all_gather | solution.py:190
  206.8 255.6 %copy-start.36 = (s32[128,7]{1,0:T(8,128)}, s32[128,7]{1,0:T(8,128)S(1)}, u32[]{:S(2)}) copy-start(s32[128,7]{1,0:T(8,128)S(1)} %copy.113) | copy-start | bytes 10756
  207.5 91.6 %copy-start.47 = (f32[1280]{0:T(1024)}, f32[1280]{0:T(1024)S(1)}, u32[]{:S(2)}) copy-start(f32[1280]{0:T(1024)S(1)} %convert_element_type.161) | copy-start | bytes 15364
  215.7 25.2 copy-start.28
  240.9 61.0 %copy-start.20 = (bf16[10,128,128]{2,1,0:T(8,128)(2,1)}, bf16[10,128,128]{2,1,0:T(8,128)(2,1)S(1)}, u32[]{:S(2)}) copy-start(bf16[10,128,128]{2,1,0:T(8,128)(2,1)S(1)} %convolution_convert_fusion.2) | copy-start | bytes 983044
  299.1 7.0 copy-start.57
  412.9 40.7 %copy-start.11 = (bf16[128,1280]{1,0:T(8,128)(2,1)S(1)}, bf16[128,1280]{1,0:T(8,128)(2,1)}, u32[]{:S(2)}) copy-start(bf16[128,1280]{1,0:T(8,128)(2,1)} %param.33) | copy-start | bytes 983044
  412.9 257.8 %all-gather.33.cloned.1.call-start = ((), (), s32[]{:S(2)}) async-start(), calls=%async_computation.26 | async-start | bytes 19660800 | tf_op jit(solution)/shard_map/all_gather | solution.py:230
  453.6 8.0 copy-start.40
  461.8 14.4 copy-start.42
  461.9 14.4 copy-start.53
  463.1 13.2 copy-start.45
  572.5 373.7 %reduce-scatter.15.cloned.1.call-start = ((), (), s32[]{:S(2)}) async-start(), calls=%async_computation.27 | async-start | bytes 39321600 | tf_op jit(solution)/shard_map/reduce_scatter | solution.py:244
  573.7 11.0 copy-start.35
  684.5 17.0 copy-start.13
  724.4 446.0 %reduce-scatter.13.cloned.1.call-start = ((), (), s32[]{:S(2)}) async-start(), calls=%async_computation.25 | async-start | bytes 39321600 | tf_op jit(solution)/shard_map/reduce_scatter | solution.py:196
  747.2 549.2 %all-gather.27.cloned.1.call-start = ((), (), s32[]{:S(2)}) async-start(), calls=%async_computation.22 | async-start | bytes 4730880 | tf_op jit(solution)/shard_map/all_gather | solution.py:103
  747.9 612.2 %all-gather.25.cloned.1.call-start = ((), (), s32[]{:S(2)}) async-start(), calls=%async_computation.21 | async-start | bytes 4730880 | tf_op jit(solution)/shard_map/all_gather | solution.py:102
  955.8 224.3 %all-to-all-start.3 = ((bf16[768,2,1280]{2,1,0:T(2,128)(2,1)}), bf16[768,2,1280]{2,1,0:T(2,128)(2,1)}, u32[]{:S(2)}, u32[]{:S(2)}) async-start(bf16[768,2,1280]{2,1,0:T(2,128)(2,1)} %copy.125), calls=%async_computation.5 | async-start | bytes 7864320 | tf_op jit(solution)/shard_map/all_to_all | solution.py:251
  961.7 463.2 %all-gather.29.cloned.1.call-start = ((), (), s32[]{:S(2)}) async-start(), calls=%async_computation.23 | async-start | bytes 4730880 | tf_op jit(solution)/shard_map/all_gather | solution.py:104
  1180.1 279.6 %all-to-all-start.1 = ((bf16[768,2,1280]{2,1,0:T(2,128)(2,1)}), bf16[768,2,1280]{2,1,0:T(2,128)(2,1)}, u32[]{:S(2)}, u32[]{:S(2)}) async-start(bf16[768,2,1280]{2,1,0:T(2,128)(2,1)} %copy.121), calls=%async_computation.2 | async-start | bytes 7864320 | tf_op jit(solution)/shard_map/all_to_all | solution.py:202
  1185.6 360.5 %reduce-scatter.19.cloned.1.call-start = ((), (), s32[]{:S(2)}) async-start(), calls=%async_computation.29 | async-start | bytes 3276800 | tf_op jit(solution)/shard_map/reduce_scatter | solution.py:305
  1429.4 67.6 %copy-start.22 = (bf16[128,1792]{1,0:T(8,128)(2,1)}, bf16[128,1792]{1,0:T(8,128)(2,1)S(1)}, u32[]{:S(2)}) copy-start(bf16[128,1792]{1,0:T(8,128)(2,1)S(1)} %get-tuple-element.27) | copy-start | bytes 1376260
  1429.4 71.5 %copy-start.23 = (bf16[128,1792]{1,0:T(8,128)(2,1)}, bf16[128,1792]{1,0:T(8,128)(2,1)S(1)}, u32[]{:S(2)}) copy-start(bf16[128,1792]{1,0:T(8,128)(2,1)S(1)} %get-tuple-element.26) | copy-start | bytes 1376260
  1429.4 103.0 %copy-start.16 = (bf16[128,1792]{1,0:T(8,128)(2,1)}, bf16[128,1792]{1,0:T(8,128)(2,1)S(1)}, u32[]{:S(2)}) copy-start(bf16[128,1792]{1,0:T(8,128)(2,1)S(1)} %get-tuple-element.28) | copy-start | bytes 1376260
  1500.8 4.0 copy-start.5
  1500.9 4.0 copy-start.41
  1500.9 4.0 copy-start.48
  1500.9 4.0 copy-start.58
  1509.0 4.1 copy-start.29
  1513.0 70.4 %reduce-scatter.17.cloned.1.call-start = ((), (), s32[]{:S(2)}) async-start(), calls=%async_computation.28 | async-start | bytes 3276800 | tf_op jit(solution)/shard_map/reduce_scatter | solution.py:302
  1519.1 189.2 %all-reduce.9.cloned.1.call-start = ((), (), s32[]{:S(2)}) async-start(), calls=%async_computation.37 | async-start | bytes 163840
  1520.0 343.4 %reduce-scatter.31.cloned.1.call-start = ((), (), s32[]{:S(2)}) async-start(), calls=%async_computation.35 | async-start | bytes 9461760 | tf_op jit(solution)/shard_map/reduce_scatter | solution.py:349
  1526.1 486.2 %reduce-scatter.29.cloned.1.call-start = ((), (), s32[]{:S(2)}) async-start(), calls=%async_computation.34 | async-start | bytes 9461760 | tf_op jit(solution)/shard_map/reduce_scatter | solution.py:348
  1532.2 629.1 %reduce-scatter.33.cloned.1.call-start = ((), (), s32[]{:S(2)}) async-start(), calls=%async_computation.36 | async-start | bytes 9461760 | tf_op jit(solution)/shard_map/reduce_scatter | solution.py:350
  1538.2 766.8 %reduce-scatter.27.cloned.1.call-start = ((), (), s32[]{:S(2)}) async-start(), calls=%async_computation.33 | async-start | bytes 6758400 | tf_op jit(solution)/shard_map/reduce_scatter | solution.py:346
  1542.9 906.2 %reduce-scatter.25.cloned.1.call-start = ((), (), s32[]{:S(2)}) async-start(), calls=%async_computation.32 | async-start | bytes 6758400 | tf_op jit(solution)/shard_map/reduce_scatter | solution.py:345
  1551.1 36.5 %copy-start.39 = (f32[128,64]{1,0:T(8,128)S(1)}, f32[128,64]{1,0:T(8,128)}, u32[]{:S(2)}) copy-start(f32[128,64]{1,0:T(8,128)} %copy-done.38) | copy-start | bytes 98308
  1551.1 36.5 %copy-start.44 = (f32[128,64]{1,0:T(8,128)S(1)}, f32[128,64]{1,0:T(8,128)}, u32[]{:S(2)}) copy-start(f32[128,64]{1,0:T(8,128)} %get-tuple-element.47) | copy-start | bytes 98308
  1551.1 1042.2 %reduce-scatter.23.cloned.1.call-start = ((), (), s32[]{:S(2)}) async-start(), calls=%async_computation.31 | async-start | bytes 6758400 | tf_op jit(solution)/shard_map/reduce_scatter | solution.py:344
  1553.8 33.8 %copy-start.10 = (f32[128,10,128]{2,0,1:T(8,128)S(1)}, f32[128,10,128]{2,0,1:T(8,128)}, u32[]{:S(2)}) copy-start(f32[128,10,128]{2,0,1:T(8,128)} %fusion.21) | copy-start | bytes 1966084
  1594.1 1143.5 %reduce-scatter.21.cloned.1.call-start = ((), (), s32[]{:S(2)}) async-start(), calls=%async_computation.30 | async-start | bytes 6758400 | tf_op jit(solution)/shard_map/reduce_scatter | solution.py:343
  1599.5 11.6 copy-start.14
  1611.1 9.3 copy-start.15
  1611.1 20.6 slice-start
  1620.5 9.0 copy-start.9
  1620.5 9.0 copy-start.46
  1620.5 11.3 slice-start.1
  1708.3 4.7 copy-start.7
  1713.0 1024.6 %copy-start.1 = (bf16[2,224,1280]{2,1,0:T(8,128)(2,1)S(1)}, bf16[2,224,1280]{2,1,0:T(8,128)(2,1)}, u32[]{:S(2)}) copy-start(bf16[2,224,1280]{2,1,0:T(8,128)(2,1)} %param.32) | copy-start | bytes 3440644
  (24 other events, 51.0 us)
Sparse Core Ops, SparseCore 0:
  10.9 61.9 all-gather.12
  75.8 58.1 all-gather.16
  136.8 58.1 all-gather.18
  197.0 17.0 all-gather.14
  216.0 18.3 all-gather.20
  237.1 59.2 all-gather.22
  413.0 98.9 all-gather.30
  572.6 98.0 all-gather.32
  724.6 221.5 reduce-scatter.14
  948.8 221.5 reduce-scatter.12
  1173.2 123.1 all-gather.26
  1299.1 60.9 all-gather.24
  1362.9 61.8 all-gather.28
  1513.2 32.9 reduce-scatter.18
  1548.7 34.6 reduce-scatter.16
  1588.8 119.3 all-reduce.8
  1711.0 152.3 reduce-scatter.30
  1866.2 146.0 reduce-scatter.28
  2015.2 146.0 reduce-scatter.32
  2164.0 140.9 reduce-scatter.26
  2307.8 141.1 reduce-scatter.24
  2452.0 141.3 reduce-scatter.22
  2596.2 141.3 reduce-scatter.20
where the time goes:
time: 2750 us; the launch traced here: 2740 us
  waiting for transfers between devices  2000 us (73%)
  blocking collectives  310 us (11%)
  matrix products  231 us (8%)
  local copies, waits for them, and re-layouts  133 us (5%)
  other arithmetic  42.2 us (2%)
    reduce_scatter x1, waiting for transfers between devices, on_device(): lax.psum_scatter(jnp.einsum('ref,efk->rek', expert_act, expert_down, pref...  208 us
    reduce_scatter x1, waiting for transfers between devices, on_device(): lax.psum_scatter(jnp.einsum('ref,efk->rek', grad_gate_pre, expert_gate, p...  198 us
    reduce_scatter x1, waiting for transfers between devices, on_device(): lax.psum_scatter(grad_sdown, ('ep', 'tp'), scatter_dimension=0, tiled=True)  149 us
    reduce_scatter x1, waiting for transfers between devices, on_device(): lax.psum_scatter(grad_sgate, ('ep', 'tp'), scatter_dimension=0, tiled=True)  149 us
    reduce_scatter x1, waiting for transfers between devices, on_device(): lax.psum_scatter(grad_wq, ('ep', 'tp'), scatter_dimension=0, tiled=True)  144 us
    reduce_scatter x1, waiting for transfers between devices, on_device(): lax.psum_scatter(grad_wk, ('ep', 'tp'), scatter_dimension=0, tiled=True)  144 us
    reduce_scatter x1, waiting for transfers between devices, on_device(): lax.psum_scatter(grad_wv, ('ep', 'tp'), scatter_dimension=0, tiled=True)  144 us
    reduce_scatter x1, waiting for transfers between devices, on_device(): lax.psum_scatter(grad_wout, ('ep', 'tp'), scatter_dimension=0, tiled=True)  144 us
  transfers between devices with their start and end apart: 25, of which 22 were waited for; matrix products, arithmetic and copies ran while one was open for 10% of the time, Pallas kernels for 0%

commit v1 on v0

v1 whole, which is shorter than its diff:
```python
import functools

import jax
import jax.numpy as jnp
from jax import lax
from jax.experimental import pallas as pl
from jax.experimental.pallas import tpu as pltpu
from jax.sharding import PartitionSpec as P

HEADS = 10
AXES = ("ep", "tp")
MESH = pl.DeviceIdType.MESH
VMEM_BUDGET = 56 * 2**20

epsilon = 1e-06

bf16 = jnp.bfloat16
f32 = jnp.float32


def place():
    ep, tp = lax.axis_index("ep"), lax.axis_index("tp")
    return ep // 2, ep % 2, tp // 2, tp % 2


def device(line, a, b, c):
    return (line * 2 + a, b * 2 + c)


def number(line, a, b, c):
    return ((line * 2 + a) * 2 + b) * 2 + c


def halves(shape):
    rows, cols = shape
    if cols % 256 == 0:
        return (
            (pl.ds(0, rows), pl.ds(0, cols // 2)),
            (pl.ds(0, rows), pl.ds(cols // 2, cols // 2)),
        )
    return ((pl.ds(0, rows // 2), pl.ds(0, cols)), (pl.ds(rows // 2, rows // 2), pl.ds(0, cols)))


def greet(partners):
    barrier = pltpu.get_barrier_semaphore()
    for partner in partners:
        pl.semaphore_signal(barrier, inc=1, device_id=partner, device_id_type=MESH)
    pl.semaphore_wait(barrier, len(partners))


def gather_kernel(lines, n_all, n_group, *refs):
    n = n_all + n_group
    ins, outs = refs[:n], refs[n : 2 * n]
    send_sem, recv_sem, group_send, group_recv, local_sem = refs[2 * n :]
    z, a, b, c = place()
    oa, ob, oc = 1 - a, 1 - b, 1 - c
    to_b, to_a, to_c = device(z, a, ob, c), device(z, oa, b, c), device(z, a, b, oc)
    to_line = [None] + [device(lax.rem(z + s, lines), a, b, c) for s in range(1, lines)]
    greet([to_b, to_a, to_c] + to_line[1:])

    back = [lax.rem(z + lines - s, lines) for s in range(lines)]
    started = []

    def slot(kind, step=0):
        return {"z": 0, "x": 1, "y": 2, "p": 3, "q": 4, "sz": 5, "sx": 6, "sy": 7, "sp": 8, "sq": 9}[
            kind
        ] * lines + step

    def send(i, kind, step, src, dst, to):
        copy = pltpu.make_async_remote_copy(
            src, dst, send_sem.at[i, slot(kind, step)], recv_sem.at[i, slot(kind, step)],
            device_id=to, device_id_type=MESH,
        )
        copy.start()
        started.append(copy)

    def arrived(i, kind, step, dst):
        pltpu.make_async_remote_copy(
            dst, dst, send_sem.at[i, slot(kind, step)], recv_sem.at[i, slot(kind, step)],
            device_id=to_c, device_id_type=MESH,
        ).wait_recv()

    locals_ = []
    group_copies = []
    for g in range(n_group):
        src, out = ins[n_all + g], outs[n_all + g]
        dst = out.at[b * 2 + c]
        keep = pltpu.make_async_copy(src, dst, local_sem.at[n_all + g])
        keep.start()
        locals_.append(keep)
        for k, to in enumerate((to_c, to_b)):
            copy = pltpu.make_async_remote_copy(
                src, dst, group_send.at[g, k], group_recv.at[g, k], device_id=to, device_id_type=MESH
            )
            copy.start()
            group_copies.append(copy)
    for i in range(n_all):
        src, own = ins[i], outs[i].at[number(z, a, b, c)]
        keep = pltpu.make_async_copy(src, own, local_sem.at[i])
        keep.start()
        locals_.append(keep)
        send(i, "x", 0, src, own, to_b)
        send(i, "y", 0, src, own, to_a)
        for s in range(1, lines):
            send(i, "z", s, src, own, to_line[s])
        send(i, "sz", 0, src, own, to_c)
    for g in range(n_group):
        out = outs[n_all + g]
        got = out.at[ob * 2 + c]
        pltpu.make_async_remote_copy(
            got, got, group_send.at[g, 1], group_recv.at[g, 1], device_id=to_b, device_id_type=MESH
        ).wait_recv()
        copy = pltpu.make_async_remote_copy(
            got, got, group_send.at[g, 2], group_recv.at[g, 2], device_id=to_c, device_id_type=MESH
        )
        copy.start()
        group_copies.append(copy)
    for s in range(lines):
        for i in range(n_all):
            out = outs[i]
            first, second = halves(out.shape[1:])
            at = back[s]
            if s > 0:
                got = out.at[number(at, a, b, c)]
                arrived(i, "z", s, got)
                send(i, "x", s, got, got, to_b)
                send(i, "y", s, got, got, to_a)
                send(i, "sz", s, got, got, to_c)
        for i in range(n_all):
            out = outs[i]
            first, second = halves(out.shape[1:])
            at = back[s]
            got = out.at[number(at, a, ob, c)]
            arrived(i, "x", s, got)
            half = out.at[(number(at, a, ob, c),) + first]
            send(i, "p", s, half, half, to_a)
            send(i, "sx", s, got, got, to_c)
            got = out.at[number(at, oa, b, c)]
            arrived(i, "y", s, got)
            half = out.at[(number(at, oa, b, c),) + second]
            send(i, "q", s, half, half, to_b)
            send(i, "sy", s, got, got, to_c)
    for s in range(lines):
        for i in range(n_all):
            out = outs[i]
            first, second = halves(out.shape[1:])
            at = back[s]
            for kind, part in (("p", first), ("q", second)):
                half = out.at[(number(at, oa, ob, c),) + part]
                arrived(i, kind, s, half)
                send(i, "s" + kind, s, half, half, to_c)
    for s in range(lines):
        for i in range(n_all):
            out = outs[i]
            first, second = halves(out.shape[1:])
            at = back[s]
            arrived(i, "sz", s, out.at[number(at, a, b, oc)])
            arrived(i, "sx", s, out.at[number(at, a, ob, oc)])
            arrived(i, "sy", s, out.at[number(at, oa, b, oc)])
            arrived(i, "sp", s, out.at[(number(at, oa, ob, oc),) + first])
            arrived(i, "sq", s, out.at[(number(at, oa, ob, oc),) + second])
    for g in range(n_group):
        out = outs[n_all + g]
        for k, t in ((0, b * 2 + oc), (2, ob * 2 + oc)):
            pltpu.make_async_remote_copy(
                out.at[t], out.at[t], group_send.at[g, k], group_recv.at[g, k],
                device_id=to_c, device_id_type=MESH,
            ).wait_recv()
    for copy in started + group_copies:
        copy.wait_send()
    for keep in locals_:
        keep.wait()


def gather(everyone, group, collective_id, name):
    eps, tps = lax.axis_size("ep"), lax.axis_size("tp")
    if eps % 2 or tps != 4 or eps * tps > 64:
        return [lax.all_gather(v, AXES, axis=0) for v in everyone], [
            lax.all_gather(v, "tp", axis=0) for v in group
        ]
    lines = eps // 2
    n_all, n_group = len(everyone), len(group)
    shapes = [jax.ShapeDtypeStruct((eps * tps,) + v.shape, v.dtype) for v in everyone] + [
        jax.ShapeDtypeStruct((tps,) + v.shape, v.dtype) for v in group
    ]
    anywhere = pl.BlockSpec(memory_space=pl.ANY)
    outs = pl.pallas_call(
        functools.partial(gather_kernel, lines, n_all, n_group),
        out_shape=shapes,
        in_specs=[anywhere] * (n_all + n_group),
        out_specs=[anywhere] * (n_all + n_group),
        scratch_shapes=[
            pltpu.SemaphoreType.DMA((n_all, 10 * lines)),
            pltpu.SemaphoreType.DMA((n_all, 10 * lines)),
            pltpu.SemaphoreType.DMA((max(n_group, 1), 3)),
            pltpu.SemaphoreType.DMA((max(n_group, 1), 3)),
            pltpu.SemaphoreType.DMA((n_all + n_group,)),
        ],
        compiler_params=pltpu.CompilerParams(collective_id=collective_id, has_side_effects=True),
        name=name,
    )(*everyone, *group)
    return outs[:n_all], outs[n_all:]


def add_into(dst, src, rows, first, cols, dst_at=(), src_at=()):
    step = 256 if cols % 256 == 0 else 128

    def body(k, carry):
        there = pl.ds(pl.multiple_of(first + k * step, 128), step)
        here = pl.ds(pl.multiple_of(k * step, 128), step)
        total = dst[dst_at + (slice(None), there)].astype(f32) + src[
            src_at + (slice(None), here)
        ].astype(f32)
        dst[dst_at + (slice(None), there)] = total.astype(bf16)
        return carry

    lax.fori_loop(0, cols // step, body, 0)


def reduce_kernel(lines, n_all, n_group, *refs):
    n = n_all + n_group
    ins, outs = refs[:n], refs[n : 2 * n]
    rest = list(refs[2 * n :])
    per_all = [[rest.pop(0) for _ in range(7)] for _ in range(n_all)]
    per_group = [[rest.pop(0) for _ in range(3)] for _ in range(n_group)]
    send_sem, recv_sem, group_send, group_recv, local_sem = rest
    z, a, b, c = place()
    oa, ob, oc = 1 - a, 1 - b, 1 - c
    to_b, to_a, to_c = device(z, a, ob, c), device(z, oa, b, c), device(z, a, b, oc)
    to_line = [None] + [device(lax.rem(z + s, lines), a, b, c) for s in range(1, lines)]
    greet([to_b, to_a, to_c] + to_line[1:])
    order = list(range(1, lines)) + [0]
    goal = [lax.rem(z + s, lines) for s in range(lines)]
    started = []
    kinds = {"s": 0, "p": 1, "q": 2, "x": 3, "y": 4, "z": 5}

    def sems(i, kind, step):
        k = kinds[kind] * lines + step
        return send_sem.at[i, k], recv_sem.at[i, k]

    def send(i, kind, step, src, dst, to):
        copy = pltpu.make_async_remote_copy(
            src, dst, *sems(i, kind, step), device_id=to, device_id_type=MESH
        )
        copy.start()
        started.append(copy)

    def arrived(i, kind, step, dst):
        pltpu.make_async_remote_copy(
            dst, dst, *sems(i, kind, step), device_id=to_c, device_id_type=MESH
        ).wait_recv()

    loads = {}
    for s in order:
        for i in range(n_all):
            acc, sib = per_all[i][:2]
            send(i, "s", s, ins[i].at[goal[s], :, :, oc], sib.at[s], to_c)
            load = pltpu.make_async_copy(
                ins[i].at[goal[s], :, :, c], acc.at[s], local_sem.at[i, s]
            )
            load.start()
            loads[i, s] = load
    group_copies, group_loads = [], []
    for g in range(n_group):
        acc, sib, far = per_group[g]
        src = ins[n_all + g]
        copy = pltpu.make_async_remote_copy(
            src.at[:, oc], sib, group_send.at[g, 0], group_recv.at[g, 0],
            device_id=to_c, device_id_type=MESH,
        )
        copy.start()
        group_copies.append(copy)
        load = pltpu.make_async_copy(src.at[:, c], acc, local_sem.at[n_all + g, 0])
        load.start()
        group_loads.append(load)
    for s in order:
        for i in range(n_all):
            acc, sib, p, q, x, y, line = per_all[i]
            rows, cols = acc.shape[-2:]
            first, second = halves((rows, cols))
            loads[i, s].wait()
            arrived(i, "s", s, sib.at[s])
            for u, v in ((oa, ob), (a, ob), (oa, b), (a, b)):
                add_into(acc, sib, rows, 0, cols, (s, u, v), (s, u, v))
                if (u is oa) and (v is ob):
                    send(i, "p", s, acc.at[(s, oa, ob) + first], p.at[s], to_a)
                    send(i, "q", s, acc.at[(s, oa, ob) + second], q.at[s], to_b)
    for g in range(n_group):
        acc, sib, far = per_group[g]
        rows, cols = acc.shape[-2:]
        group_loads[g].wait()
        pltpu.make_async_remote_copy(
            sib, sib, group_send.at[g, 0], group_recv.at[g, 0], device_id=to_c, device_id_type=MESH
        ).wait_recv()
        for u in (ob, b):
            add_into(acc, sib, rows, 0, cols, (u,), (u,))
            if u is ob:
                copy = pltpu.make_async_remote_copy(
                    acc.at[ob], far, group_send.at[g, 1], group_recv.at[g, 1],
                    device_id=to_b, device_id_type=MESH,
                )
                copy.start()
                group_copies.append(copy)
    for s in order:
        for i in range(n_all):
            acc, sib, p, q, x, y, line = per_all[i]
            rows, cols = acc.shape[-2:]
            arrived(i, "p", s, p.at[s])
            add_into(acc, p, rows, 0, cols // 2, (s, a, ob), (s,))
            send(i, "x", s, acc.at[s, a, ob], x.at[s], to_b)
            arrived(i, "q", s, q.at[s])
            add_into(acc, q, rows, cols // 2, cols // 2, (s, oa, b), (s,))
            send(i, "y", s, acc.at[s, oa, b], y.at[s], to_a)
    for s in order:
        for i in range(n_all):
            acc, sib, p, q, x, y, line = per_all[i]
            rows, cols = acc.shape[-2:]
            arrived(i, "x", s, x.at[s])
            add_into(acc, x, rows, 0, cols, (s, a, b), (s,))
            arrived(i, "y", s, y.at[s])
            add_into(acc, y, rows, 0, cols, (s, a, b), (s,))
            if s > 0:
                send(i, "z", s, acc.at[s, a, b], line.at[s - 1], to_line[s])
    for g in range(n_group):
        acc, sib, far = per_group[g]
        pltpu.make_async_remote_copy(
            far, far, group_send.at[g, 1], group_recv.at[g, 1], device_id=to_b, device_id_type=MESH
        ).wait_recv()
        outs[n_all + g][...] = acc[b].astype(f32) + far[...].astype(f32)
    for i in range(n_all):
        acc, sib, p, q, x, y, line = per_all[i]
        for s in range(1, lines):
            arrived(i, "z", s, line.at[s - 1])
        total = acc[0, a, b].astype(f32)
        for s in range(1, lines):
            total = total + line[s - 1].astype(f32)
        outs[i][...] = total
    for copy in started + group_copies:
        copy.wait_send()


def reduce_scatter(everyone, group, collective_id, name):
    eps, tps = lax.axis_size("ep"), lax.axis_size("tp")
    need = sum(v.size * 2 * 3 // 2 + v.size // v.shape[0] * 8 for v in everyone) + sum(
        v.size * 4 for v in group
    )
    if eps % 2 or tps != 4 or need > VMEM_BUDGET:
        return [
            lax.psum_scatter(v, AXES, scatter_dimension=0).astype(f32) for v in everyone
        ], [lax.psum_scatter(v, "tp", scatter_dimension=0).astype(f32) for v in group]
    lines = eps // 2
    n_all, n_group = len(everyone), len(group)
    anywhere = pl.BlockSpec(memory_space=pl.ANY)
    vmem = pl.BlockSpec(memory_space=pltpu.VMEM)
    scratch = []
    for v in everyone:
        rows, cols = v.shape[1:]
        scratch += [
            pltpu.VMEM((lines, 2, 2, rows, cols), bf16),
            pltpu.VMEM((lines, 2, 2, rows, cols), bf16),
            pltpu.VMEM((lines, rows, cols // 2), bf16),
            pltpu.VMEM((lines, rows, cols // 2), bf16),
            pltpu.VMEM((lines, rows, cols), bf16),
            pltpu.VMEM((lines, rows, cols), bf16),
            pltpu.VMEM((lines - 1, rows, cols), bf16),
        ]
    for v in group:
        rows, cols = v.shape[1:]
        scratch += [
            pltpu.VMEM((2, rows, cols), bf16),
            pltpu.VMEM((2, rows, cols), bf16),
            pltpu.VMEM((rows, cols), bf16),
        ]
    scratch += [
        pltpu.SemaphoreType.DMA((n_all, 6 * lines)),
        pltpu.SemaphoreType.DMA((n_all, 6 * lines)),
        pltpu.SemaphoreType.DMA((max(n_group, 1), 2)),
        pltpu.SemaphoreType.DMA((max(n_group, 1), 2)),
        pltpu.SemaphoreType.DMA((n_all + n_group, lines)),
    ]
    outs = pl.pallas_call(
        functools.partial(reduce_kernel, lines, n_all, n_group),
        out_shape=[jax.ShapeDtypeStruct(v.shape[1:], f32) for v in list(everyone) + list(group)],
        in_specs=[anywhere] * (n_all + n_group),
        out_specs=[vmem] * (n_all + n_group),
        scratch_shapes=scratch,
        compiler_params=pltpu.CompilerParams(
            collective_id=collective_id, has_side_effects=True, vmem_limit_bytes=VMEM_BUDGET
        ),
        name=name,
    )(
        *[v.reshape((lines, 2, 2, 2) + v.shape[1:]) for v in everyone],
        *[v.reshape((2, 2) + v.shape[1:]) for v in group],
    )
    return outs[:n_all], outs[n_all:]


def documents(positions, lengths):
    seq_ends = jnp.cumsum(lengths)
    doc_index = (positions >= seq_ends[0]).astype(jnp.int32) + (positions >= seq_ends[1]).astype(
        jnp.int32
    )
    seq_starts = jnp.where(doc_index == 0, 0, jnp.where(doc_index == 1, seq_ends[0], seq_ends[1]))
    return (doc_index, positions - seq_starts)


def rotary_tables(offsets, head_dim):
    half_dim = head_dim // 2
    frequency = 10000.0 ** (-2.0 * jnp.arange(half_dim, dtype=f32) / head_dim)
    angles = offsets.astype(f32)[:, None] * frequency[None, :]
    return (jnp.cos(angles)[:, None, :], jnp.sin(angles)[:, None, :])


def rotate(values, cosine, sine_table):
    half_dim = values.shape[-1] // 2
    first_half = values[..., :half_dim]
    second_half = values[..., half_dim:]
    return jnp.concatenate(
        [
            first_half * cosine - second_half * sine_table,
            first_half * sine_table + second_half * cosine,
        ],
        axis=-1,
    )


def norm_back(grad_normed, unit_rows, inverse, gain):
    scaled = grad_normed * gain
    return inverse * (scaled - unit_rows * jnp.mean(scaled * unit_rows, axis=-1, keepdims=True))


def dot(left, right, contract):
    return lax.dot_general(left, right, ((contract[0], contract[1]), ((), ())), preferred_element_type=f32)


def dense_dot(left, right):
    return dot(left, right, ((1,), (0,)))


def dot_nt(left, right):
    return dot(left, right, ((1,), (1,)))


def dot_tn(left, right):
    return dot(left, right, ((0,), (0,)))


def on_device(
    hidden_in,
    seq_lengths,
    expert_ids,
    attn_gain,
    w_query,
    w_key,
    w_value,
    w_out,
    ffn_gain,
    shared_gate,
    shared_up,
    shared_down,
    router,
    expert_gate,
    expert_up,
    expert_down,
    cotangent,
):
    tok_count, model_width = hidden_in.shape
    eps, tps = lax.axis_size("ep"), lax.axis_size("tp")
    devices = eps * tps
    exp_local, exp_hidden = expert_gate.shape[:2]
    experts = exp_local * eps
    group_len = tps * tok_count
    tokens = devices * tok_count
    d_rows = w_query.shape[0]
    width = w_query.shape[1]
    sh_rows = shared_down.shape[0]
    head_dim = width // HEADS
    attn_scale = head_dim ** (-0.5)

    flat = jnp.concatenate([router.reshape(-1), attn_gain, ffn_gain])
    small_len = -(-flat.shape[0] // model_width) * model_width
    small = jnp.pad(flat, (0, small_len - flat.shape[0])).reshape(-1, model_width)
    small = jnp.pad(small, ((0, -small.shape[0] % 16), (0, 0)))
    weights = jnp.concatenate([w_query, w_key, w_value, w_out], axis=1)

    (all_weights, all_small, all_cot), (group_hidden,) = gather(
        [weights, small, cotangent], [hidden_in], 0, "gather_weights"
    )
    all_weights = all_weights.reshape(devices * d_rows, 4 * width)
    full_query = all_weights[:, :width]
    full_key = all_weights[:, width : 2 * width]
    full_value = all_weights[:, 2 * width : 3 * width]
    full_out = all_weights[:, 3 * width :]
    all_small = all_small.reshape(devices, -1)
    n_router = d_rows * experts
    full_router = all_small[:, :n_router].reshape(devices * d_rows, experts)
    gain_one = all_small[:, n_router : n_router + d_rows].reshape(-1).astype(f32)
    gain_two = all_small[:, n_router + d_rows : n_router + 2 * d_rows].reshape(-1).astype(f32)
    cot_all = all_cot.reshape(tokens, model_width)

    shared_cols = jnp.stack([shared_gate, shared_up], axis=1).reshape(d_rows, 2, devices, sh_rows)
    shared_cols = lax.all_to_all(
        shared_cols.transpose(2, 1, 3, 0), AXES, split_axis=0, concat_axis=0, tiled=True
    )
    shared_t = shared_cols.transpose(1, 2, 0, 3).reshape(2, sh_rows, model_width)

    lengths = seq_lengths[0]
    tp_index = lax.axis_index("tp")
    own_pos = tp_index * tok_count + jnp.arange(tok_count, dtype=jnp.int32)
    all_pos = jnp.arange(group_len, dtype=jnp.int32)
    own_doc, own_offset = documents(own_pos, lengths)
    all_doc, all_offset = documents(all_pos, lengths)
    allowed = (own_doc[:, None] == all_doc[None, :]) & (own_pos[:, None] >= all_pos[None, :])
    cosine, sine_table = rotary_tables(own_offset, head_dim)
    cosine_all, sine_all = rotary_tables(all_offset, head_dim)

    inputs = hidden_in.astype(f32)
    inverse_one = lax.rsqrt(jnp.mean(inputs * inputs, axis=-1, keepdims=True) + epsilon)
    unit_one = inputs * inverse_one
    normed = (unit_one * gain_one).astype(bf16)
    group_in = group_hidden.reshape(group_len, model_width).astype(f32)
    group_unit = group_in * lax.rsqrt(jnp.mean(group_in * group_in, axis=-1, keepdims=True) + epsilon)
    group_normed = (group_unit * gain_one).astype(bf16)

    queries = rotate(
        dense_dot(normed, full_query).reshape(tok_count, HEADS, head_dim), cosine, sine_table
    ).astype(bf16)
    key_rows = rotate(
        dense_dot(group_normed, full_key).reshape(group_len, HEADS, head_dim), cosine_all, sine_all
    ).astype(bf16)
    value_rows = dense_dot(group_normed, full_value).astype(bf16).reshape(group_len, HEADS, head_dim)

    def masked_scores():
        raw_scores = (
            jnp.einsum("qhd,khd->hqk", queries, key_rows, preferred_element_type=f32) * attn_scale
        )
        return jnp.where(allowed[None], raw_scores, -1e30)

    scores = masked_scores()
    row_peak = jnp.max(scores, axis=-1, keepdims=True)
    row_total = jnp.sum(jnp.exp(scores - row_peak), axis=-1, keepdims=True)
    softmaxed = jnp.exp(scores - row_peak) / row_total
    attended = (
        jnp.einsum("hqk,khd->qhd", softmaxed.astype(bf16), value_rows, preferred_element_type=f32)
        .reshape(tok_count, width)
        .astype(bf16)
    )
    residual = inputs + dense_dot(attended, full_out)
    inverse_two = lax.rsqrt(jnp.mean(residual * residual, axis=-1, keepdims=True) + epsilon)
    unit_two = residual * inverse_two
    normed_two = (unit_two * gain_two).astype(bf16)

    affinity = jax.nn.softmax(dense_dot(normed_two, full_router), axis=-1)
    expert_range = jnp.arange(experts, dtype=jnp.int32)
    named = jnp.any(expert_ids[:, :, None] == expert_range[None, None, :], axis=1)
    signed = jnp.where(named, affinity, -affinity)

    (all_normed, all_signed), _ = gather([normed_two, signed.T], [], 1, "gather_tokens")
    rows = all_normed.reshape(tokens, model_width)
    signed = all_signed.transpose(0, 2, 1).reshape(tokens, experts)

    first_expert = lax.axis_index("ep") * exp_local
    n_routed = exp_local * exp_hidden
    hidden = n_routed + sh_rows
    gate_w = jnp.concatenate([expert_gate.reshape(n_routed, model_width), shared_t[0]])
    up_w = jnp.concatenate([expert_up.reshape(n_routed, model_width), shared_t[1]])
    down_w = jnp.concatenate([expert_down.reshape(n_routed, model_width), shared_down])

    def mixture(rows, cot_rows, signed):
        count = rows.shape[0]
        mine = lax.dynamic_slice_in_dim(signed, first_expert, exp_local, axis=1)
        mine_named = mine > 0
        gates = jnp.where(mine_named, mine, 0.0)
        scale = jnp.concatenate(
            [jnp.repeat(gates, exp_hidden, axis=1), jnp.ones((count, sh_rows), f32)], axis=1
        )
        gate_pre = dot_nt(rows, gate_w)
        up_pre = dot_nt(rows, up_w)
        sigma = jax.nn.sigmoid(gate_pre)
        silu = gate_pre * sigma
        act = silu * up_pre
        act_scaled = (act * scale).astype(bf16)
        out_part = dense_dot(act_scaled, down_w).astype(bf16)
        grad_hidden = dot_nt(cot_rows, down_w)
        grad_gates = jnp.sum(
            (act * grad_hidden)[:, :n_routed].reshape(count, exp_local, exp_hidden), axis=-1
        )
        grad_gates = jnp.where(mine_named, grad_gates, 0.0)
        grad_hidden = grad_hidden * scale
        grad_gate_pre = (grad_hidden * up_pre * sigma * (1.0 + gate_pre * (1.0 - sigma))).astype(
            bf16
        )
        grad_up_pre = (grad_hidden * silu).astype(bf16)
        affinity_all = jnp.abs(signed)
        grad_aff = lax.dynamic_update_slice_in_dim(
            jnp.zeros((count, experts), f32), grad_gates, first_expert, axis=1
        )
        grad_logits = (
            affinity_all * (grad_aff - jnp.sum(affinity_all * grad_aff, axis=-1, keepdims=True))
        ).astype(bf16)
        dn2_part = (
            dense_dot(grad_gate_pre, gate_w)
            + dense_dot(grad_up_pre, up_w)
            + dot_nt(grad_logits, full_router)
        ).astype(bf16)
        sums = (
            dot_tn(act_scaled, cot_rows),
            dot_tn(grad_gate_pre, rows),
            dot_tn(grad_up_pre, rows),
            dot_tn(rows, grad_logits),
        )
        return out_part, dn2_part, sums

    blocks = max(1, tokens * hidden * 4 // 2**23)
    while tokens % blocks:
        blocks += 1
    if blocks == 1:
        out_part, dn2_part, sums = mixture(rows, cot_all, signed)
    else:

        def step(totals, block):
            out_block, dn2_block, sums = mixture(*block)
            return jax.tree.map(jnp.add, totals, sums), (out_block, dn2_block)

        zeros = (jnp.zeros((hidden, model_width), f32),) * 3 + (
            jnp.zeros((model_width, experts), f32),
        )
        sums, (out_part, dn2_part) = lax.scan(
            step,
            zeros,
            jax.tree.map(lambda v: v.reshape((blocks, -1) + v.shape[1:]), (rows, cot_all, signed)),
        )
    grad_down, grad_gate, grad_up, router_part = sums

    (routed_sum, grad_normed_two), _ = reduce_scatter(
        [
            out_part.reshape(devices, tok_count, model_width),
            dn2_part.reshape(devices, tok_count, model_width),
        ],
        [],
        2,
        "reduce_tokens",
    )
    layer_output = (residual + routed_sum).astype(bf16)

    gain_two_part = jnp.sum(grad_normed_two * unit_two, axis=0)
    grad_resid = cotangent.astype(f32) + norm_back(grad_normed_two, unit_two, inverse_two, gain_two)
    grad_resid_low = grad_resid.astype(bf16)
    wout_part = dot_tn(attended, grad_resid_low)
    grad_att = dot_nt(grad_resid_low, full_out).astype(bf16).reshape(tok_count, HEADS, head_dim)
    softmax_again = jnp.exp(masked_scores() - row_peak) / row_total
    grad_soft = jnp.einsum("qhd,khd->hqk", grad_att, value_rows, preferred_element_type=f32)
    grad_scores = (
        softmax_again * (grad_soft - jnp.sum(softmax_again * grad_soft, axis=-1, keepdims=True))
    ).astype(bf16)
    grad_queries = (
        jnp.einsum("hqk,khd->qhd", grad_scores, key_rows, preferred_element_type=f32) * attn_scale
    )
    grad_key_rows = (
        jnp.einsum("hqk,qhd->khd", grad_scores, queries, preferred_element_type=f32) * attn_scale
    )
    grad_value_rows = jnp.einsum(
        "hqk,qhd->khd", softmax_again.astype(bf16), grad_att, preferred_element_type=f32
    )
    grad_q_pre = rotate(grad_queries, cosine, -sine_table).reshape(tok_count, width).astype(bf16)
    grad_k_pre = rotate(grad_key_rows, cosine_all, -sine_all).reshape(group_len, width).astype(bf16)
    grad_v_pre = grad_value_rows.reshape(group_len, width).astype(bf16)
    wq_part = dot_tn(normed, grad_q_pre)
    wk_part = dot_tn(group_normed, grad_k_pre)
    wv_part = dot_tn(group_normed, grad_v_pre)
    own_normed_grad = dot_nt(grad_q_pre, full_query)
    group_normed_grad = dot_nt(grad_k_pre, full_key) + dot_nt(grad_v_pre, full_value)
    gain_one_part = jnp.sum(own_normed_grad * unit_one, axis=0) + jnp.sum(
        group_normed_grad * group_unit, axis=0
    )

    weight_part = jnp.concatenate([wq_part, wk_part, wv_part, wout_part], axis=1).astype(bf16)
    small_part = jnp.concatenate(
        [
            router_part.reshape(devices, n_router),
            gain_one_part.reshape(devices, d_rows),
            gain_two_part.reshape(devices, d_rows),
        ],
        axis=1,
    )
    small_part = jnp.pad(small_part, ((0, 0), (0, small_len - small_part.shape[1])))
    small_part = small_part.reshape(devices, -1, model_width)
    small_part = jnp.pad(small_part, ((0, 0), (0, -small_part.shape[1] % 16), (0, 0))).astype(bf16)
    (weight_sum, small_sum), (normed_grad_sum,) = reduce_scatter(
        [weight_part.reshape(devices, d_rows, 4 * width), small_part],
        [group_normed_grad.astype(bf16).reshape(tps, tok_count, model_width)],
        3,
        "reduce_weights",
    )
    grad_normed = own_normed_grad + normed_grad_sum
    input_grad = grad_resid + norm_back(grad_normed, unit_one, inverse_one, gain_one)
    small_sum = small_sum.reshape(-1)

    shared_back = jnp.stack([grad_gate[n_routed:], grad_up[n_routed:]])
    shared_back = shared_back.reshape(2, sh_rows, devices, d_rows).transpose(2, 0, 1, 3)
    shared_back = lax.all_to_all(shared_back, AXES, split_axis=0, concat_axis=0, tiled=True)
    shared_back = shared_back.transpose(1, 3, 0, 2).reshape(2, d_rows, devices * sh_rows)

    return (
        layer_output,
        input_grad,
        small_sum[n_router : n_router + d_rows],
        weight_sum[:, :width],
        weight_sum[:, width : 2 * width],
        weight_sum[:, 2 * width : 3 * width],
        weight_sum[:, 3 * width :],
        small_sum[n_router + d_rows : n_router + 2 * d_rows],
        shared_back[0],
        shared_back[1],
        grad_down[n_routed:],
        small_sum[:n_router].reshape(d_rows, experts),
        grad_gate[:n_routed].reshape(expert_gate.shape),
        grad_up[:n_routed].reshape(expert_up.shape),
        grad_down[:n_routed].reshape(expert_down.shape),
    )


def solution(mesh):
    rows = P(AXES, None)
    vector = P(AXES)
    experts = P("ep", "tp", None)
    return jax.shard_map(
        on_device,
        mesh=mesh,
        in_specs=(
            rows, P("ep", None), rows, vector, rows, rows, rows, rows, vector,
            rows, rows, rows, rows, experts, experts, experts, rows,
        ),
        out_specs=(
            rows, rows, vector, rows, rows, rows, rows, vector,
            rows, rows, rows, rows, experts, experts, experts,
        ),
        check_vma=False,
    )
```

time: 2750 us -> 713 us (0.26)
  waiting for transfers between devices: 2000 us -> 0.01 us
  Pallas kernels: 0 us -> 390 us
  blocking collectives: 310 us -> 0 us
  local copies, waits for them, and re-layouts: 133 us -> 72.6 us
  matrix products: 231 us -> 176 us
    reduce_scatter x11 -> x0, waiting for transfers between devices: 1410 us -> none  [the longest x1 208 us: on_device(): lax.psum_scatter(jnp.einsum('ref,efk->rek', expert_act, expert_down, pref...]
    all_gather x11 -> x0, waiting for transfers between devices: 510 us -> none  [the longest x1 111 us: on_device(): lax.all_gather(shared_up, ('ep', 'tp'), axis=0, tiled=True)]
    pallas_call x0 -> x4, Pallas kernels: none -> 390 us  [the longest x2 196 us: reduce_scatter(): pl.pallas_call(functools.partial(reduce_kernel, lines, n_all, n_group), o...]
    all_to_all x2 -> x0, blocking collectives: 183 us -> none  [the longest x1 92.1 us: on_device(): lax.all_to_all(send_rows, 'ep', split_axis=1, concat_axis=0, tiled=True)]
    unnamed x2 -> x0, blocking collectives: 86.8 us -> none
    unnamed x24 -> x0, waiting for transfers between devices: 79.5 us -> none
    dot_general x41 -> x28, matrix products: 224 us -> 172 us  [the longest x24 166 us: dot(): lax.dot_general(left, right, ((contract[0], contract[1]), ((), ())), pref...]
    all_gather x1 -> x0, blocking collectives: 39.8 us -> none  [on_device(): lax.all_gather(router, ('ep', 'tp'), axis=0, tiled=True)]
  transfers between devices with their start and end apart: 25 -> 2, of which waited for: 22 -> 0; matrix products, arithmetic and copies ran while one was open for 10% -> 15% of each run, Pallas kernels for 0% -> 40%
where the time goes in v1:
time: 713 us; the launch traced here: 704 us
  Pallas kernels  390 us (55%)
  matrix products  176 us (25%)
  local copies, waits for them, and re-layouts  72.6 us (10%)
  other arithmetic  51.3 us (7%)
  starting transfers between devices  11.5 us (2%)
    pallas_call x2, Pallas kernels, reduce_scatter(): pl.pallas_call(functools.partial(reduce_kernel, lines, n_all, n_group), o...  196 us
    pallas_call x2, Pallas kernels, gather(): pl.pallas_call(functools.partial(gather_kernel, lines, n_all, n_group), o...  194 us
    dot_general x24, matrix products, dot(): lax.dot_general(left, right, ((contract[0], contract[1]), ((), ())), pref...  166 us
    unnamed x198, local copies, waits for them, and re-layouts  20.4 us
  transfers between devices with their start and end apart: 2, of which 0 were waited for; matrix products, arithmetic and copies ran while one was open for 15% of the time, Pallas kernels for 40%

profile of v1, /device:TPU:0, one launch (start us, length us, event | category | flops | bytes accessed | tf_op | source)
XLA Modules:
  0.0 704.1 jit_solution(11195411413595374232)
XLA Ops:
  0.7 1.6 stack.18
  2.3 1.6 stack.19
  4.4 1.8 reshape.544
  6.2 7.4 %all-to-all-start = ((bf16[32,2,2240]{2,1,0:T(2,128)(2,1)}), bf16[32,2,2240]{2,1,0:T(2,128)(2,1)}, u32[]{:S(2)}, u32[]{:S(2)}) async-start(bf16[32,2,2240]{2,1,0:T(2,128)(2,1)} %reshape.544), calls=%async_computation | async-start | bytes 589824 | tf_op jit(solution)/shard_map/all_to_all | solution.py:502
  15.7 1.9 fusion.67
  17.6 1.9 subtract_convert_fusion.2
  21.3 116.8 %gather_weights.1 = (bf16[32,40,5120]{2,1,0:T(8,128)(2,1)}, bf16[32,16,1280]{2,1,0:T(8,128)(2,1)}, bf16[32,128,1280]{2,1,0:T(8,128)(2,1)}, bf16[4,128,1280]{2,1,0:T(8,128)(2,1)}) custom-call(bf16[40,5120]{1,0:T(8,128)(2,1)} %pad_maximum_fusion.13.refs_0_, bf16[16,1280]{1,0:T(8,128)(2,1)} %pad.20.refs_1_, bf16[128,1280]{1,0:T(8,128)(2,1)} %refs_2_.1, ...), custom_call_target="tpu_custom_call" | custom-call | tf_op jit(solution)/shard_map/gather_weights/pallas_call | solution.py:187
  138.1 1.8 copy.208
  145.5 2.2 slice_bitcast_fusion
  147.7 3.3 fusion.10
  151.9 2.1 copy.204
  154.0 2.1 copy.205
  156.1 2.8 multiply_convert_fusion.4
  159.3 4.9 convolution_convert_fusion.5
  164.2 2.4 copy.162
  166.6 3.9 copy.166
  170.5 4.3 fusion.93
  175.7 1.5 subtract_convert_fusion
  177.4 2.8 fusion.91
  180.2 2.9 convolution_convert_fusion.8
  183.2 2.8 multiply_reduce_fusion.5
  187.9 77.4 %gather_tokens.1 = (bf16[32,128,1280]{2,1,0:T(8,128)(2,1)}, f32[32,16,128]{2,1,0:T(8,128)}) custom-call(bf16[128,1280]{1,0:T(8,128)(2,1)} %copy-done.16, f32[16,128]{1,0:T(8,128)} %negate_select_fusion.refs_1_), custom_call_target="tpu_custom_call" | custom-call | tf_op jit(solution)/shard_map/gather_tokens/pallas_call | solution.py:187
  266.3 1.5 copy.179
  267.8 1.8 reshape.545
  270.1 10.7 %fusion.33 = f32[4096,504]{0,1:T(8,128)} fusion(bf16[4096,1280]{1,0:T(8,128)(2,1)} %bitcast.151, bf16[56,1280]{1,0:T(8,128)(2,1)S(1)} %copy.200, bf16[448,1280]{1,0:T(8,128)(2,1)} %bitcast.208), kind=kOutput, calls=%fused_computation.72 | convolution fusion | flops 5287403520 | bytes 20033536 | tf_op jit(solution)/shard_map/dot_general | solution.py:433
  280.8 7.7 %fusion.35 = f32[4096,504]{0,1:T(8,128)} fusion(bf16[4096,1280]{1,0:T(8,128)(2,1)S(1)} %bitcast.155, bf16[56,1280]{1,0:T(8,128)(2,1)S(1)} %copy.199, bf16[448,1280]{1,0:T(8,128)(2,1)S(1)} %bitcast.206), kind=kOutput, calls=%fused_computation.74 | convolution fusion | flops 5287403520 | bytes 20033536 | tf_op jit(solution)/shard_map/dot_general | solution.py:433
  288.6 3.9 broadcast_in_dim.32
  292.5 27.0 %multiply_convert_fusion = (bf16[4096,504]{0,1:T(8,128)(2,1)}, bf16[4096,504]{0,1:T(8,128)(2,1)}, bf16[4096,504]{0,1:T(8,128)(2,1)}, f32[4096,504]{0,1:T(8,128)}, f32[4096,504]{0,1:T(8,128)}) fusion(f32[4096,448]{0,1:T(8,128)} %bitcast.162, f32[4096,504]{0,1:T(8,128)} %fusion.35, f32[4096,504]{0,1:T(8,128)} %fusion.33, bf16[4096,1280]{1,0:T(8,128)(2,1)} %bitcast.202, ...), kind=kOutput, calls=%fused_computation.4 | convolution fusion | flops 5322498048 | bytes 64532480 | tf_op jit(solution)/shard_map/dot_general | solution.py:433
  319.5 11.6 %fusion.96 = f32[504,1280]{1,0:T(8,128)} fusion(bf16[4096,504]{0,1:T(8,128)(2,1)} %get-tuple-element.118, bf16[4096,1280]{1,0:T(8,128)(2,1)} %bitcast.203), kind=kOutput, calls=%fused_computation.183 | convolution fusion | flops 5284823040 | bytes 17195008 | tf_op jit(solution)/shard_map/dot_general | solution.py:433
  331.1 8.5 %convolution_convert_fusion = bf16[4096,1280]{1,0:T(8,128)(2,1)} fusion(bf16[4096,504]{0,1:T(8,128)(2,1)S(1)} %copy-done.85, bf16[56,1280]{1,0:T(8,128)(2,1)S(1)} %copy-done.79, bf16[448,1280]{1,0:T(8,128)(2,1)S(1)} %bitcast.205), kind=kOutput, calls=%fused_computation.2 | convolution fusion | flops 5292646400 | bytes 15904768 | tf_op jit(solution)/shard_map/dot_general | solution.py:433
  339.6 7.0 fusion.94
  346.6 10.0 %fusion.34 = f32[4096,1280]{1,0:T(8,128)} fusion(bf16[4096,504]{0,1:T(8,128)(2,1)S(1)} %copy-done.84, bf16[56,1280]{1,0:T(8,128)(2,1)S(1)} %copy.199, bf16[448,1280]{1,0:T(8,128)(2,1)S(1)} %bitcast.207), kind=kOutput, calls=%fused_computation.73 | convolution fusion | flops 5287403520 | bytes 26390528 | tf_op jit(solution)/shard_map/dot_general | solution.py:433
  356.6 8.5 %fusion.95 = f32[504,1280]{1,0:T(8,128)} fusion(bf16[4096,504]{0,1:T(8,128)(2,1)} %get-tuple-element.116, bf16[4096,1280]{1,0:T(8,128)(2,1)S(1)} %bitcast.159), kind=kOutput, calls=%fused_computation.182 | convolution fusion | flops 5284823040 | bytes 17195008 | tf_op jit(solution)/shard_map/dot_general | solution.py:433
  365.1 13.7 %fusion.32 = f32[4096,1280]{1,0:T(8,128)} fusion(bf16[4096,504]{0,1:T(8,128)(2,1)} %get-tuple-element.116, bf16[56,1280]{1,0:T(8,128)(2,1)S(1)} %copy.200, bf16[448,1280]{1,0:T(8,128)(2,1)S(1)} %bitcast.209), kind=kOutput, calls=%fused_computation.71 | convolution fusion | flops 5287403520 | bytes 26390528 | tf_op jit(solution)/shard_map/dot_general | solution.py:433
  378.9 7.8 %slice_multiply_fusion = f32[4096,448]{0,1:T(8,128)} fusion(f32[4096,504]{0,1:T(8,128)} %get-tuple-element.164, f32[4096,504]{0,1:T(8,128)S(1)} %bitcast.164), kind=kLoop, calls=%fused_computation.10 | loop fusion | flops 1835008 | bytes 22020096 | tf_op jit(solution)/shard_map/mul | solution.py:586
  386.7 3.5 reduce_sum.122
  390.4 5.4 convolution_convert_fusion.6
  395.8 18.6 %add_convert_fusion = bf16[4096,1280]{1,0:T(8,128)(2,1)} fusion(f32[4096,1280]{1,0:T(8,128)} %fusion.34, f32[4096,1280]{1,0:T(8,128)} %fusion.32, bf16[4096,16]{0,1:T(8,128)(2,1)S(1)} %multiply_convert_fusion.7, bf16[1280,16]{1,0:T(8,128)(2,1)S(1)} %copy-done.17), kind=kOutput, calls=%fused_computation.1 | convolution fusion | flops 183500800 | bytes 52600832 | tf_op jit(solution)/shard_map/dot_general | solution.py:433
  414.5 107.9 %reduce_tokens.1 = (f32[128,1280]{1,0:T(8,128)}, f32[128,1280]{1,0:T(8,128)}) custom-call(bf16[4,2,2,2,128,1280]{5,4,3,2,1,0:T(8,128)(2,1)} %bitcast.161, bf16[4,2,2,2,128,1280]{5,4,3,2,1,0:T(8,128)(2,1)} %bitcast.150), custom_call_target="tpu_custom_call" | custom-call | tf_op jit(solution)/shard_map/reduce_tokens/pallas_call | solution.py:381
  522.4 1.4 multiply_reduce_fusion.3
  523.8 2.3 multiply_add_fusion.2
  526.8 3.3 fusion.17
  530.4 1.7 convolution_convert_fusion.7
  534.0 1.3 fusion.25
  536.9 1.9 reshape.528
  538.8 1.6 stack.22
  540.4 1.7 stack.21
  542.1 2.9 maximum_bitcast_fusion
  545.0 4.0 copy.185
  549.0 3.5 reshape.546
  552.5 4.0 all-to-all-start.1
  557.3 1.6 multiply_subtract_fusion.1
  561.1 3.3 fusion.8
  567.9 4.3 fusion.6
  572.4 5.3 fusion.84
  581.0 1.9 convolution_convert_fusion.3
  582.9 1.9 convolution_convert_fusion.2
  585.9 6.1 pad_maximum_fusion.refs_0_
  592.1 87.9 %reduce_weights.1 = (f32[40,5120]{1,0:T(8,128)}, f32[16,1280]{1,0:T(8,128)}, f32[128,1280]{1,0:T(8,128)}) custom-call(bf16[4,2,2,2,40,5120]{5,4,3,2,1,0:T(8,128)(2,1)} %pad_maximum_fusion.refs_0_, bf16[4,2,2,2,16,1280]{5,4,3,2,1,0:T(8,128)(2,1)} %bitcast.168, bf16[2,2,128,1280]{3,2,1,0:T(8,128)(2,1)} %bitcast.198), custom_call_target="tpu_custom_call" | custom-call | tf_op jit(solution)/shard_map/reduce_weights/pallas_call | solution.py:381
  682.8 1.9 slice.181
  684.7 3.2 slice.185
  687.9 1.5 slice.183
  690.4 1.5 slice.184
  697.0 3.1 reduce.1
  (277 shorter events, 43.4 us)
Async XLA Ops:
  0.6 13.0 %copy-start.80 = (s32[1,3]{1,0:T(1,128)S(1)}, s32[1,3]{1,0:T(1,128)}, u32[]{:S(2)}) copy-start(s32[1,3]{1,0:T(1,128)} %param.18) | copy-start | bytes 40
  0.7 18.8 %copy-start.3 = (bf16[128,1280]{1,0:T(8,128)(2,1)S(1)}, bf16[128,1280]{1,0:T(8,128)(2,1)}, u32[]{:S(2)}) copy-start(bf16[128,1280]{1,0:T(8,128)(2,1)} %refs_3_.1) | copy-start | bytes 983044
  0.7 18.9 %copy-start.69 = (bf16[40,16]{0,1:T(8,128)(2,1)S(1)}, bf16[40,16]{0,1:T(8,128)(2,1)}, u32[]{:S(2)}) copy-start(bf16[40,16]{0,1:T(8,128)(2,1)} %param.29) | copy-start | bytes 3844
  2.3 17.5 %copy-start.73 = (bf16[40]{0:T(256)(128)(2,1)S(1)}, bf16[40]{0:T(256)(128)(2,1)}, u32[]{:S(2)}) copy-start(bf16[40]{0:T(256)(128)(2,1)} %param.25) | copy-start | bytes 244
  2.3 17.5 %copy-start.74 = (bf16[40]{0:T(256)(128)(2,1)S(1)}, bf16[40]{0:T(256)(128)(2,1)}, u32[]{:S(2)}) copy-start(bf16[40]{0:T(256)(128)(2,1)} %param.20) | copy-start | bytes 244
  2.3 18.2 %copy-start.53 = (bf16[40,1280]{1,0:T(8,128)(2,1)S(1)}, bf16[40,1280]{1,0:T(8,128)(2,1)}, u32[]{:S(2)}) copy-start(bf16[40,1280]{1,0:T(8,128)(2,1)} %param.24) | copy-start | bytes 307204
  2.3 18.2 %copy-start.54 = (bf16[40,1280]{1,0:T(8,128)(2,1)S(1)}, bf16[40,1280]{1,0:T(8,128)(2,1)}, u32[]{:S(2)}) copy-start(bf16[40,1280]{1,0:T(8,128)(2,1)} %param.23) | copy-start | bytes 307204
  2.3 18.2 %copy-start.55 = (bf16[40,1280]{1,0:T(8,128)(2,1)S(1)}, bf16[40,1280]{1,0:T(8,128)(2,1)}, u32[]{:S(2)}) copy-start(bf16[40,1280]{1,0:T(8,128)(2,1)} %param.22) | copy-start | bytes 307204
  2.3 18.2 %copy-start.56 = (bf16[40,1280]{1,0:T(8,128)(2,1)S(1)}, bf16[40,1280]{1,0:T(8,128)(2,1)}, u32[]{:S(2)}) copy-start(bf16[40,1280]{1,0:T(8,128)(2,1)} %param.21) | copy-start | bytes 307204
  6.2 261.6 %all-to-all-start = ((bf16[32,2,2240]{2,1,0:T(2,128)(2,1)}), bf16[32,2,2240]{2,1,0:T(2,128)(2,1)}, u32[]{:S(2)}, u32[]{:S(2)}) async-start(bf16[32,2,2240]{2,1,0:T(2,128)(2,1)} %reshape.544), calls=%async_computation | async-start | bytes 589824 | tf_op jit(solution)/shard_map/all_to_all | solution.py:502
  13.6 126.9 %copy-start.70 = (s32[128,7]{0,1:T(8,128)S(1)}, s32[128,7]{0,1:T(8,128)}, u32[]{:S(2)}) copy-start(s32[128,7]{0,1:T(8,128)} %param.19) | copy-start | bytes 10756
  138.1 5.2 copy-start
  142.1 35.1 %copy-start.42 = (f32[128,64]{1,0:T(8,128)}, f32[128,64]{1,0:T(8,128)S(1)}, u32[]{:S(2)}) copy-start(f32[128,64]{1,0:T(8,128)S(1)} %get-tuple-element.155) | copy-start | bytes 98308
  143.3 32.3 %copy-start.37 = (f32[512,64]{0,1:T(8,128)}, f32[512,64]{0,1:T(8,128)S(1)}, u32[]{:S(2)}) copy-start(f32[512,64]{0,1:T(8,128)S(1)} %get-tuple-element.150) | copy-start | bytes 393220
  144.3 41.7 %copy-start.51 = (f32[1280]{0:T(1024)}, f32[1280]{0:T(1024)S(1)}, u32[]{:S(2)}) copy-start(f32[1280]{0:T(1024)S(1)} %reshape.538) | copy-start | bytes 15364
  144.4 14.5 %copy-start.47 = (f32[1280]{0:T(1024)}, f32[1280]{0:T(1024)S(1)}, u32[]{:S(2)}) copy-start(f32[1280]{0:T(1024)S(1)} %reshape.537) | copy-start | bytes 15364
  170.5 4.4 copy-start.61
  170.5 4.4 copy-start.71
  170.5 4.4 copy-start.72
  170.5 5.1 copy-start.45
  183.2 4.1 copy-start.60
  183.2 83.1 %copy-start.13 = (bf16[4,128,1280]{2,1,0:T(8,128)(2,1)S(1)}, bf16[4,128,1280]{2,1,0:T(8,128)(2,1)}, u32[]{:S(2)}) copy-start(bf16[4,128,1280]{2,1,0:T(8,128)(2,1)} %multiply_convert_fusion.4) | copy-start | bytes 3932164
  269.7 11.1 %slice-start = ((s8[10485760]{0:T(1024)(128)(4,1)}), s8[2097152]{0:T(1024)(128)(4,1)S(1)}, s32[]{:S(2)}) async-start(s8[10485760]{0:T(1024)(128)(4,1)} %bitcast.153), calls=%async_computation.2 | async-start | bytes 4194304
  270.0 10.8 %slice-start.1 = ((s8[10485760]{0:T(1024)(128)(4,1)}), s8[4194304]{0:T(1024)(128)(4,1)S(1)}, s32[]{:S(2)}) async-start(s8[10485760]{0:T(1024)(128)(4,1)} %bitcast.153), calls=%async_computation.3 | async-start | bytes 8388608
  270.1 10.8 %slice-start.2 = ((s8[10485760]{0:T(1024)(128)(4,1)}), s8[4194304]{0:T(1024)(128)(4,1)S(1)}, s32[]{:S(2)}) async-start(s8[10485760]{0:T(1024)(128)(4,1)} %bitcast.153), calls=%async_computation.4 | async-start | bytes 8388608
  270.1 10.7 %copy-start.76 = (bf16[2,224,1280]{2,1,0:T(8,128)(2,1)S(1)}, bf16[2,224,1280]{2,1,0:T(8,128)(2,1)}, u32[]{:S(2)}) copy-start(bf16[2,224,1280]{2,1,0:T(8,128)(2,1)} %param.30) | copy-start | bytes 3440644
  288.6 3.9 copy-start.79
  319.4 11.6 %copy-start.85 = (bf16[4096,504]{0,1:T(8,128)(2,1)S(1)}, bf16[4096,504]{0,1:T(8,128)(2,1)}, u32[]{:S(2)}) copy-start(bf16[4096,504]{0,1:T(8,128)(2,1)} %get-tuple-element.118) | copy-start | bytes 12386308
  319.5 20.1 %slice-start.3 = ((s8[10485760]{0:T(1024)(128)(4,1)}), s8[4194304]{0:T(1024)(128)(4,1)S(1)}, s32[]{:S(2)}) async-start(s8[10485760]{0:T(1024)(128)(4,1)} %bitcast.156), calls=%async_computation.5 | async-start | bytes 8388608
  319.5 20.1 %slice-start.4 = ((s8[10485760]{0:T(1024)(128)(4,1)}), s8[4194304]{0:T(1024)(128)(4,1)S(1)}, s32[]{:S(2)}) async-start(s8[10485760]{0:T(1024)(128)(4,1)} %bitcast.156), calls=%async_computation.6 | async-start | bytes 8388608
  331.1 8.5 %slice-start.5 = ((s8[10485760]{0:T(1024)(128)(4,1)}), s8[2097152]{0:T(1024)(128)(4,1)S(1)}, s32[]{:S(2)}) async-start(s8[10485760]{0:T(1024)(128)(4,1)} %bitcast.156), calls=%async_computation.7 | async-start | bytes 4194304
  331.1 8.5 %copy-start.83 = (bf16[4096,504]{0,1:T(8,128)(2,1)S(1)}, bf16[4096,504]{0,1:T(8,128)(2,1)}, u32[]{:S(2)}) copy-start(bf16[4096,504]{0,1:T(8,128)(2,1)} %get-tuple-element.117) | copy-start | bytes 12386308
  339.6 7.0 copy-start.77
  339.6 7.0 copy-start.84
  346.6 32.3 %slice-start.6 = ((s8[8257536]{0:T(1024)(128)(4,1)}), s8[4194304]{0:T(1024)(128)(4,1)S(1)}, s32[]{:S(2)}) async-start(s8[8257536]{0:T(1024)(128)(4,1)} %bitcast.163), calls=%async_computation.8 | async-start | bytes 8388608
  356.6 8.6 %copy-start.78 = (bf16[2,224,1280]{2,1,0:T(8,128)(2,1)S(1)}, bf16[2,224,1280]{2,1,0:T(8,128)(2,1)}, u32[]{:S(2)}) copy-start(bf16[2,224,1280]{2,1,0:T(8,128)(2,1)} %param.31) | copy-start | bytes 3440644
  356.6 22.3 %slice-start.7 = ((s8[8257536]{0:T(1024)(128)(4,1)}), s8[4063232]{0:T(1024)(128)(4,1)S(1)}, s32[]{:S(2)}) async-start(s8[8257536]{0:T(1024)(128)(4,1)} %bitcast.163), calls=%async_computation.9 | async-start | bytes 8126464
  414.4 107.9 %copy-start.8 = (f32[128,1280]{1,0:T(8,128)S(1)}, f32[128,1280]{1,0:T(8,128)}, u32[]{:S(2)}) copy-start(f32[128,1280]{1,0:T(8,128)} %copy-done.7) | copy-start | bytes 1966084
  414.4 107.9 %copy-start.52 = (f32[1280]{0:T(1024)S(1)}, f32[1280]{0:T(1024)}, u32[]{:S(2)}) copy-start(f32[1280]{0:T(1024)} %copy-done.51) | copy-start | bytes 15364
  414.4 107.9 %copy-start.65 = (f32[128]{0:T(128)S(1)}, f32[128]{0:T(128)}, u32[]{:S(2)}) copy-start(f32[128]{0:T(128)} %copy-done.64) | copy-start | bytes 1540
  414.5 109.3 %copy-start.36 = (bf16[128,1280]{1,0:T(8,128)(2,1)S(1)}, bf16[128,1280]{1,0:T(8,128)(2,1)}, u32[]{:S(2)}) copy-start(bf16[128,1280]{1,0:T(8,128)(2,1)} %refs_2_.1) | copy-start | bytes 983044
  536.0 4.4 slice-start.8
  545.0 12.3 %copy-start.43 = (f32[128,64]{1,0:T(8,128)S(1)}, f32[128,64]{1,0:T(8,128)}, u32[]{:S(2)}) copy-start(f32[128,64]{1,0:T(8,128)} %copy-done.42) | copy-start | bytes 98308
  545.0 12.3 %copy-start.49 = (f32[128,64]{1,0:T(8,128)S(1)}, f32[128,64]{1,0:T(8,128)}, u32[]{:S(2)}) copy-start(f32[128,64]{1,0:T(8,128)} %get-tuple-element.153) | copy-start | bytes 98308
  552.5 143.9 %all-to-all-start.1 = ((f32[32,1,4480]{2,1,0:T(1,128)}), f32[32,1,4480]{2,1,0:T(1,128)}, u32[]{:S(2)}, u32[]{:S(2)}) async-start(f32[32,1,4480]{2,1,0:T(1,128)} %reshape.546), calls=%async_computation.1 | async-start | bytes 1146880 | tf_op jit(solution)/shard_map/all_to_all | solution.py:701
  559.8 5.4 copy-start.6
  559.8 5.4 copy-start.48
  561.0 5.1 copy-start.26
  561.0 4.2 copy-start.67
  561.0 6.3 copy-start.38
  561.0 6.3 copy-start.44
  567.9 4.4 copy-start.34
  567.9 4.4 copy-start.2
  567.9 4.4 copy-start.63
  567.9 4.4 copy-start.81
  572.3 5.5 copy-start.50
  572.3 5.5 copy-start.57
  572.3 6.9 copy-start.10
  572.4 6.9 copy-start.15
  592.1 87.9 %copy-start.12 = (f32[128,1280]{1,0:T(8,128)S(1)}, f32[128,1280]{1,0:T(8,128)}, u32[]{:S(2)}) copy-start(f32[128,1280]{1,0:T(8,128)} %copy-done.11) | copy-start | bytes 1966084
  592.1 87.9 %copy-start.68 = (f32[128]{0:T(128)S(1)}, f32[128]{0:T(128)}, u32[]{:S(2)}) copy-start(f32[128]{0:T(128)} %add_rsqrt_fusion.2) | copy-start | bytes 1540
  682.2 5.6 copy-start.23
  690.4 4.0 copy-start.39
  690.4 4.9 copy-start.22
  (34 other events, 76.7 us)

commit v2 on v1

--- a/solution.py
+++ b/solution.py
@@ -48,150 +48,214 @@
     pl.semaphore_wait(barrier, len(partners))
 
 
-def gather_kernel(lines, n_all, n_group, *refs):
+def visit_order(lines):
+    return [sorted(range(lines), key=lambda other: (abs(other - z), other)) for z in range(lines)]
+
+
+def lookup(table, index):
+    out = jnp.int32(table[0])
+    for k in range(1, len(table)):
+        out = jnp.where(index == k, jnp.int32(table[k]), out)
+    return out
+
+
+def pick(values, index):
+    out = values[0]
+    for k in range(1, len(values)):
+        out = jnp.where(index == k, values[k], out)
+    return out
+
+
+def gather_kernel(lines, core_only, n_group, *refs):
+    n_all = len(core_only)
     n = n_all + n_group
     ins, outs = refs[:n], refs[n : 2 * n]
     send_sem, recv_sem, group_send, group_recv, local_sem = refs[2 * n :]
     z, a, b, c = place()
     oa, ob, oc = 1 - a, 1 - b, 1 - c
     to_b, to_a, to_c = device(z, a, ob, c), device(z, oa, b, c), device(z, a, b, oc)
-    to_line = [None] + [device(lax.rem(z + s, lines), a, b, c) for s in range(1, lines)]
-    greet([to_b, to_a, to_c] + to_line[1:])
-
-    back = [lax.rem(z + lines - s, lines) for s in range(lines)]
-    started = []
-
-    def slot(kind, step=0):
-        return {"z": 0, "x": 1, "y": 2, "p": 3, "q": 4, "sz": 5, "sx": 6, "sy": 7, "sp": 8, "sq": 9}[
-            kind
-        ] * lines + step
-
-    def send(i, kind, step, src, dst, to):
-        copy = pltpu.make_async_remote_copy(
-            src, dst, send_sem.at[i, slot(kind, step)], recv_sem.at[i, slot(kind, step)],
-            device_id=to, device_id_type=MESH,
-        )
+    up_next = device(lax.rem(z + 1, lines), a, b, c)
+    down_next = device(lax.rem(z + lines - 1, lines), a, b, c)
+    greet(
+        [to_b, to_a, to_c] + [device(lax.rem(z + s, lines), a, b, c) for s in range(1, lines)]
+    )
+    table = visit_order(lines)
+    zs = [lookup([table[k][u] for k in range(lines)], z) for u in range(lines)]
+    O, X, Y, D = 0, 1, 2, 3
+    sent = []
+
+    def chunk(i, line, kind, part=None, core=None):
+        if core_only[i]:
+            at = line * 4 + kind
+        else:
+            at = number(line, (a, a, oa, oa)[kind], (b, ob, b, ob)[kind], c if core is None else core)
+        if part is None:
+            return outs[i].at[at]
+        return outs[i].at[(at,) + halves(outs[i].shape[1:])[part]]
+
+    def remote(i, slot, step, src, dst, to):
+        k = slot * lines + step
+        return pltpu.make_async_remote_copy(
+            src, dst, send_sem.at[i, k], recv_sem.at[i, k], device_id=to, device_id_type=MESH
+        )
+
+    def hop(i, slot, step, kind, to_kind, line, to, part=None, own=False):
+        src = ins[i] if own else chunk(i, line, kind, part)
+        there = chunk(i, line, to_kind if core_only[i] else kind, part)
+        return remote(i, slot, step, src, there, to)
+
+    def arrival(i, slot, step, kind, line, part=None):
+        here = chunk(i, line, kind, part)
+        remote(i, slot, step, here, here, to_c).wait_recv()
+
+    def send(copy):
         copy.start()
-        started.append(copy)
-
-    def arrived(i, kind, step, dst):
-        pltpu.make_async_remote_copy(
-            dst, dst, send_sem.at[i, slot(kind, step)], recv_sem.at[i, slot(kind, step)],
-            device_id=to_c, device_id_type=MESH,
-        ).wait_recv()
-
-    locals_ = []
+        sent.append(copy)
+
+    def across(i, slot, u, kind, part=None, own=False):
+        if not core_only[i]:
+            here = chunk(i, zs[u], kind, part)
+            send(remote(i, slot, u, ins[i] if own else here, here, to_c))
+
+    def send_own(u):
+        own = u == 0
+        for i in range(n_all):
+            send(hop(i, 0, u, O, X, zs[u], to_b, own=own))
+            send(hop(i, 1, u, O, Y, zs[u], to_a, own=own))
+        for i in range(n_all):
+            across(i, 6, u, O, own=own)
+
+    def xy_event(u):
+        for i in range(n_all):
+            arrival(i, 0, u, X, zs[u])
+            send(hop(i, 2, u, X, D, zs[u], to_a, 0))
+            arrival(i, 1, u, Y, zs[u])
+            send(hop(i, 3, u, Y, D, zs[u], to_b, 1))
+            across(i, 7, u, X)
+            across(i, 8, u, Y)
+
+    def diag_event(u):
+        for i in range(n_all):
+            arrival(i, 2, u, D, zs[u], 0)
+            across(i, 9, u, D, 0)
+            arrival(i, 3, u, D, zs[u], 1)
+            across(i, 10, u, D, 1)
+
+    def chain_up(i, k):
+        return hop(i, 4, k, O, O, z - (k - 1), up_next, own=k == 1)
+
+    def chain_down(i, k):
+        return hop(i, 5, k, O, O, z + (k - 1), down_next, own=k == 1)
+
+    def chain_start(k):
+        if k >= lines:
+            return
+
+        @pl.when((z >= k - 1) & (z + 1 < lines))
+        def _():
+            for i in range(n_all):
+                chain_up(i, k).start()
+
+        @pl.when((z + k - 1 < lines) & (z > 0))
+        def _():
+            for i in range(n_all):
+                chain_down(i, k).start()
+
+    def chain_event(k):
+        @pl.when(z >= k)
+        def _():
+            for i in range(n_all):
+                arrival(i, 4, k, O, z - k)
+
+        @pl.when(z + k < lines)
+        def _():
+            for i in range(n_all):
+                arrival(i, 5, k, O, z + k)
+
+        chain_start(k + 1)
+
+    def chain_drain(k):
+        @pl.when((z >= k - 1) & (z + 1 < lines))
+        def _():
+            for i in range(n_all):
+                chain_up(i, k).wait_send()
+
+        @pl.when((z + k - 1 < lines) & (z > 0))
+        def _():
+            for i in range(n_all):
+                chain_down(i, k).wait_send()
+
     group_copies = []
+
+    def group_copy(g, k, src, dst, to):
+        return pltpu.make_async_remote_copy(
+            src, dst, group_send.at[g, k], group_recv.at[g, k], device_id=to, device_id_type=MESH
+        )
+
+    keeps = []
+    send_own(0)
+    chain_start(1)
     for g in range(n_group):
-        src, out = ins[n_all + g], outs[n_all + g]
-        dst = out.at[b * 2 + c]
-        keep = pltpu.make_async_copy(src, dst, local_sem.at[n_all + g])
+        src, dst = ins[n_all + g], outs[n_all + g].at[b * 2 + c]
+        for k, to in enumerate((to_c, to_b)):
+            group_copies.append(group_copy(g, k, src, dst, to))
+            group_copies[-1].start()
+        keeps.append(pltpu.make_async_copy(src, dst, local_sem.at[n_all + g]))
+    for i in range(n_all):
+        keeps.append(pltpu.make_async_copy(ins[i], chunk(i, z, O), local_sem.at[i]))
+    for keep in keeps:
         keep.start()
-        locals_.append(keep)
-        for k, to in enumerate((to_c, to_b)):
-            copy = pltpu.make_async_remote_copy(
-                src, dst, group_send.at[g, k], group_recv.at[g, k], device_id=to, device_id_type=MESH
-            )
-            copy.start()
-            group_copies.append(copy)
-    for i in range(n_all):
-        src, own = ins[i], outs[i].at[number(z, a, b, c)]
-        keep = pltpu.make_async_copy(src, own, local_sem.at[i])
-        keep.start()
-        locals_.append(keep)
-        send(i, "x", 0, src, own, to_b)
-        send(i, "y", 0, src, own, to_a)
-        for s in range(1, lines):
-            send(i, "z", s, src, own, to_line[s])
-        send(i, "sz", 0, src, own, to_c)
     for g in range(n_group):
-        out = outs[n_all + g]
-        got = out.at[ob * 2 + c]
-        pltpu.make_async_remote_copy(
-            got, got, group_send.at[g, 1], group_recv.at[g, 1], device_id=to_b, device_id_type=MESH
-        ).wait_recv()
-        copy = pltpu.make_async_remote_copy(
-            got, got, group_send.at[g, 2], group_recv.at[g, 2], device_id=to_c, device_id_type=MESH
-        )
-        copy.start()
-        group_copies.append(copy)
-    for s in range(lines):
+        got = outs[n_all + g].at[ob * 2 + c]
+        group_copy(g, 1, got, got, to_b).wait_recv()
+        group_copies.append(group_copy(g, 2, got, got, to_c))
+        group_copies[-1].start()
+    xy_event(0)
+    chain_event(1)
+    send_own(1)
+    for u in range(2, lines):
+        chain_event(u)
+        xy_event(u - 1)
+        diag_event(u - 2)
+        send_own(u)
+    xy_event(lines - 1)
+    diag_event(lines - 2)
+    diag_event(lines - 1)
+    for u in range(lines):
         for i in range(n_all):
-            out = outs[i]
-            first, second = halves(out.shape[1:])
-            at = back[s]
-            if s > 0:
-                got = out.at[number(at, a, b, c)]
-                arrived(i, "z", s, got)
-                send(i, "x", s, got, got, to_b)
-                send(i, "y", s, got, got, to_a)
-                send(i, "sz", s, got, got, to_c)
-        for i in range(n_all):
-            out = outs[i]
-            first, second = halves(out.shape[1:])
-            at = back[s]
-            got = out.at[number(at, a, ob, c)]
-            arrived(i, "x", s, got)
-            half = out.at[(number(at, a, ob, c),) + first]
-            send(i, "p", s, half, half, to_a)
-            send(i, "sx", s, got, got, to_c)
-            got = out.at[number(at, oa, b, c)]
-            arrived(i, "y", s, got)
-            half = out.at[(number(at, oa, b, c),) + second]
-            send(i, "q", s, half, half, to_b)
-            send(i, "sy", s, got, got, to_c)
-    for s in range(lines):
-        for i in range(n_all):
-            out = outs[i]
-            first, second = halves(out.shape[1:])
-            at = back[s]
-            for kind, part in (("p", first), ("q", second)):
-                half = out.at[(number(at, oa, ob, c),) + part]
-                arrived(i, kind, s, half)
-                send(i, "s" + kind, s, half, half, to_c)
-    for s in range(lines):
-        for i in range(n_all):
-            out = outs[i]
-            first, second = halves(out.shape[1:])
-            at = back[s]
-            arrived(i, "sz", s, out.at[number(at, a, b, oc)])
-            arrived(i, "sx", s, out.at[number(at, a, ob, oc)])
-            arrived(i, "sy", s, out.at[number(at, oa, b, oc)])
-            arrived(i, "sp", s, out.at[(number(at, oa, ob, oc),) + first])
-            arrived(i, "sq", s, out.at[(number(at, oa, ob, oc),) + second])
+            if not core_only[i]:
+                for slot, kind, part in ((6, O, None), (7, X, None), (8, Y, None), (9, D, 0), (10, D, 1)):
+                    there = chunk(i, zs[u], kind, part, oc)
+                    remote(i, slot, u, there, there, to_c).wait_recv()
     for g in range(n_group):
-        out = outs[n_all + g]
         for k, t in ((0, b * 2 + oc), (2, ob * 2 + oc)):
-            pltpu.make_async_remote_copy(
-                out.at[t], out.at[t], group_send.at[g, k], group_recv.at[g, k],
-                device_id=to_c, device_id_type=MESH,
-            ).wait_recv()
-    for copy in started + group_copies:
+            got = outs[n_all + g].at[t]
+            group_copy(g, k, got, got, to_c).wait_recv()
+    for copy in sent + group_copies:
         copy.wait_send()
-    for keep in locals_:
+    for k in range(1, lines):
+        chain_drain(k)
+    for keep in keeps:
         keep.wait()
 
 
-def gather(everyone, group, collective_id, name):
+def gather(everyone, core_only, group, collective_id, name):
     eps, tps = lax.axis_size("ep"), lax.axis_size("tp")
-    if eps % 2 or tps != 4 or eps * tps > 64:
-        return [lax.all_gather(v, AXES, axis=0) for v in everyone], [
-            lax.all_gather(v, "tp", axis=0) for v in group
-        ]
     lines = eps // 2
     n_all, n_group = len(everyone), len(group)
-    shapes = [jax.ShapeDtypeStruct((eps * tps,) + v.shape, v.dtype) for v in everyone] + [
-        jax.ShapeDtypeStruct((tps,) + v.shape, v.dtype) for v in group
-    ]
+    shapes = [
+        jax.ShapeDtypeStruct((eps * tps // (2 if core else 1),) + v.shape, v.dtype)
+        for v, core in zip(everyone, core_only)
+    ] + [jax.ShapeDtypeStruct((tps,) + v.shape, v.dtype) for v in group]
     anywhere = pl.BlockSpec(memory_space=pl.ANY)
     outs = pl.pallas_call(
-        functools.partial(gather_kernel, lines, n_all, n_group),
+        functools.partial(gather_kernel, lines, tuple(core_only), n_group),
         out_shape=shapes,
         in_specs=[anywhere] * (n_all + n_group),
         out_specs=[anywhere] * (n_all + n_group),
         scratch_shapes=[
-            pltpu.SemaphoreType.DMA((n_all, 10 * lines)),
-            pltpu.SemaphoreType.DMA((n_all, 10 * lines)),
+            pltpu.SemaphoreType.DMA((n_all, 11 * lines)),
+            pltpu.SemaphoreType.DMA((n_all, 11 * lines)),
             pltpu.SemaphoreType.DMA((max(n_group, 1), 3)),
             pltpu.SemaphoreType.DMA((max(n_group, 1), 3)),
             pltpu.SemaphoreType.DMA((n_all + n_group,)),
@@ -341,13 +405,6 @@
 
 def reduce_scatter(everyone, group, collective_id, name):
     eps, tps = lax.axis_size("ep"), lax.axis_size("tp")
-    need = sum(v.size * 2 * 3 // 2 + v.size // v.shape[0] * 8 for v in everyone) + sum(
-        v.size * 4 for v in group
-    )
-    if eps % 2 or tps != 4 or need > VMEM_BUDGET:
-        return [
-            lax.psum_scatter(v, AXES, scatter_dimension=0).astype(f32) for v in everyone
-        ], [lax.psum_scatter(v, "tp", scatter_dimension=0).astype(f32) for v in group]
     lines = eps // 2
     n_all, n_group = len(everyone), len(group)
     anywhere = pl.BlockSpec(memory_space=pl.ANY)
@@ -395,6 +452,445 @@
     return outs[:n_all], outs[n_all:]
 
 
+def mixture_kernel(lines, tok, aux, cot, wg, wu, wd, sel, sel_t, router_t, ones, *refs):
+    (
+        sums, dw_own, dw_sib, dr,
+        nc, aux_all, vg, vu, vd, dw, acts, dg, du, daff, dlg, pr, qr, xr, yr, zr,
+        ag_send, ag_recv, rs_send, rs_recv, w_send, w_recv, local_sem,
+    ) = refs
+    z, a, b, c = place()
+    oa, ob, oc = 1 - a, 1 - b, 1 - c
+    to_b, to_a, to_c = device(z, a, ob, c), device(z, oa, b, c), device(z, a, b, oc)
+    count, width = tok.shape
+    half = count // 2
+    hc = wg.shape[0]
+    hidden = 2 * hc
+    n_sel = sel.shape[1]
+    block = 256
+    unit_rows = 4 * count
+    table = visit_order(lines)
+    zs = [lookup([table[k][u] for k in range(lines)], z) for u in range(lines)]
+    O, X, Y, D = 0, 1, 2, 3
+
+    barrier = pltpu.get_barrier_semaphore()
+    partners = [to_b, to_a, to_c] + [
+        device(lax.rem(z + s, lines), a, b, c) for s in range(1, lines)
+    ]
+    for partner in partners:
+        pl.semaphore_signal(barrier, inc=1, device_id=partner, device_id_type=MESH)
+    pl.semaphore_wait(barrier, len(partners))
+
+    def remote(src, dst, send_sem, recv_sem, to):
+        return pltpu.make_async_remote_copy(
+            src, dst, send_sem, recv_sem, device_id=to, device_id_type=MESH
+        )
+
+    local = []
+    mine = pl.ds(c * hc, hc)
+    theirs = pl.ds(oc * hc, hc)
+    w_copies = []
+    for k, (src, dst) in enumerate(((wg, vg), (wu, vu), (wd, vd))):
+        copy = pltpu.make_async_copy(src, dst.at[mine], local_sem.at[k])
+        copy.start()
+        local.append(copy)
+        copy = remote(src, dst.at[mine], w_send.at[k], w_recv.at[k], to_c)
+        copy.start()
+        w_copies.append(copy)
+
+    def spot(line, kind):
+        return line * 4 + kind
+
+    def tok_at(line, kind, part=None):
+        first = spot(line, kind) * count
+        if part is None:
+            return nc.at[pl.ds(first, count), pl.ds(0, width)]
+        return nc.at[pl.ds(first + part * half, half), pl.ds(0, width)]
+
+    def ag(slot, step, arr):
+        k = slot * lines + step
+        return ag_send.at[arr, k], ag_recv.at[arr, k]
+
+    def ag_copies(slot, step, src_kind, dst_kind, line, to, part=None, own=False):
+        src = tok if own else tok_at(line, src_kind, part)
+        copies = [remote(src, tok_at(line, dst_kind, part), *ag(slot, step, 0), to)]
+        if part != 1:
+            src = aux if own else aux_all.at[spot(line, src_kind)]
+            copies.append(remote(src, aux_all.at[spot(line, dst_kind)], *ag(slot, step, 1), to))
+        return copies
+
+    def send_own(u):
+        own = u == 0
+        return ag_copies(0, u, O, X, zs[u], to_b, own=own) + ag_copies(1, u, O, Y, zs[u], to_a, own=own)
+
+    def send_halves(u):
+        return ag_copies(2, u, X, D, zs[u], to_a, 0) + ag_copies(3, u, Y, D, zs[u], to_b, 1)
+
+    def start(copies):
+        for copy in copies:
+            copy.start()
+
+    def wait_recv(copies):
+        for copy in copies:
+            copy.wait_recv()
+
+    def wait_send(copies):
+        for copy in copies:
+            copy.wait_send()
+
+    up_next = device(lax.rem(z + 1, lines), a, b, c)
+    down_next = device(lax.rem(z + lines - 1, lines), a, b, c)
+
+    def chain_up(k, own=False):
+        return ag_copies(4, k, O, O, z - (k - 1), up_next, own=own)
+
+    def chain_down(k, own=False):
+        return ag_copies(5, k, O, O, z + (k - 1), down_next, own=own)
+
+    def chain_event(k):
+        @pl.when(z >= k)
+        def _():
+            wait_recv(ag_copies(4, k, O, O, z - k, up_next))
+
+            if k + 1 < lines:
+
+                @pl.when(z + 1 < lines)
+                def _():
+                    start(chain_up(k + 1))
+
+        @pl.when(z + k < lines)
+        def _():
+            wait_recv(ag_copies(5, k, O, O, z + k, down_next))
+
+            if k + 1 < lines:
+
+                @pl.when(z > 0)
+                def _():
+                    start(chain_down(k + 1))
+
+    def chain_drain(k):
+        @pl.when((z >= k - 1) & (z + 1 < lines))
+        def _():
+            wait_send(chain_up(k, own=k == 1))
+
+        @pl.when((z + k - 1 < lines) & (z > 0))
+        def _():
+            wait_send(chain_down(k, own=k == 1))
+
+    def xy_event(u):
+        wait_recv(ag_copies(0, u, O, X, zs[u], to_b))
+        wait_recv(ag_copies(1, u, O, Y, zs[u], to_a))
+        start(send_halves(u))
+
+    def diag_event(u):
+        wait_recv(ag_copies(2, u, X, D, zs[u], to_a, 0))
+        wait_recv(ag_copies(3, u, Y, D, zs[u], to_b, 1))
+
+    def sent_event(u):
+        wait_send(send_own(u))
+        wait_send(send_halves(u))
+
+    start(send_own(0))
+
+    @pl.when(z + 1 < lines)
+    def _():
+        start(chain_up(1, own=True))
+
+    @pl.when(z > 0)
+    def _():
+        start(chain_down(1, own=True))
+
+    copy = pltpu.make_async_copy(tok, tok_at(z, O), local_sem.at[3])
+    copy.start()
+    local.append(copy)
+    copy = pltpu.make_async_copy(aux, aux_all.at[spot(z, O)], local_sem.at[4])
+    copy.start()
+    local.append(copy)
+    copy = pltpu.make_async_copy(cot, nc.at[:, pl.ds(width, width)], local_sem.at[5])
+    copy.start()
+    local.append(copy)
+
+    def zero(i, carry):
+        dw[:, pl.ds(i * 64, 64), :] = jnp.zeros((3, 64, width), f32)
+        return carry
+
+    lax.fori_loop(0, hidden // 64, zero, 0)
+    dr[...] = jnp.zeros_like(dr)
+
+    def res(line, kind, part=None):
+        first = spot(line, kind) * count
+        if part is None:
+            return nc.at[pl.ds(first, count)]
+        return nc.at[pl.ds(first + part * half, half)]
+
+    def part_of(ref, u, part):
+        return ref.at[u, pl.ds(part * half, half)]
+
+    def rs(slot, u):
+        k = slot * lines + u
+        return rs_send.at[k], rs_recv.at[k]
+
+    def p_copy(u):
+        return remote(res(zs[u], D, 0), pr.at[u], *rs(0, u), to_a)
+
+    def q_copy(u):
+        return remote(res(zs[u], D, 1), qr.at[u], *rs(1, u), to_b)
+
+    def x_copy(u, part):
+        return remote(res(zs[u], X, part), part_of(xr, u, part), *rs(2 + part, u), to_b)
+
+    def y_copy(u, part):
+        return remote(res(zs[u], Y, part), part_of(yr, u, part), *rs(4 + part, u), to_a)
+
+    def z_copy(u):
+        slot = lax.rem(z - zs[u] + lines, lines) - 1
+        k = 6 * lines
+        return remote(
+            res(zs[u], O), zr.at[slot], rs_send.at[k + u], rs_recv.at[k + slot],
+            device(zs[u], a, b, c),
+        )
+
+    def add(first, rows, others):
+        def body(k, carry):
+            there = pl.ds(pl.multiple_of(k * 256, 256), 256)
+            at = pl.ds(first, rows)
+            total = nc[at, there].astype(f32)
+            for ref, u in others:
+                total = total + ref[u, :, there].astype(f32)
+            nc[at, there] = total.astype(bf16)
+            return carry
+
+        lax.fori_loop(0, 2 * width // 256, body, 0)
+
+    def rs_start(u):
+        p_copy(u).start()
+        q_copy(u).start()
+        x_copy(u, 1).start()
+        y_copy(u, 0).start()
+
+    def rs_mid(u):
+        p_copy(u).wait_recv()
+        add(spot(zs[u], X) * count, half, [(pr, u)])
+        x_copy(u, 0).start()
+        q_copy(u).wait_recv()
+        add(spot(zs[u], Y) * count + half, half, [(qr, u)])
+        y_copy(u, 1).start()
+
+    def rs_end(u):
+        for part in (0, 1):
+            x_copy(u, part).wait_recv()
+            y_copy(u, part).wait_recv()
+        add(spot(zs[u], O) * count, count, [(xr, u), (yr, u)])
+        if u > 0:
+            z_copy(u).start()
+
+    def expand(line, columns):
+        return jnp.concatenate(
+            [dot_tn(aux_all[spot(line, kind)], sel[:, columns]) for kind in range(4)], axis=0
+        )
+
+    def unit(u, carry):
+        line = pick(zs, u)
+        rows = pl.ds(pl.multiple_of(line * unit_rows, unit_rows), unit_rows)
+
+        for v in range(lines):
+
+            @pl.when(u == v)
+            def _(v=v):
+                diag_event(v)
+
+        daff[...] = jnp.zeros_like(daff)
+
+        def hidden_step(i, carry):
+            h = pl.ds(pl.multiple_of(i * block, block), block)
+            x = nc[rows, 0:width]
+            gate_pre = dot_nt(x, vg[h, :])
+            up_pre = dot_nt(x, vu[h, :])
+            grad = dot_nt(nc[rows, width : 2 * width], vd[h, :])
+            scale = jnp.maximum(expand(line, h) + ones[:, h], 0.0)
+            sigma = 1.0 / (1.0 + jnp.exp(-gate_pre))
+            silu = gate_pre * sigma
+            act = silu * up_pre
+            acts[:, h] = (act * scale).astype(bf16)
+            daff[...] += dense_dot((act * grad).astype(bf16), sel_t[h, :])
+            grad = grad * scale
+            dg[:, h] = (grad * up_pre * sigma * (1.0 + gate_pre * (1.0 - sigma))).astype(bf16)
+            du[:, h] = (grad * silu).astype(bf16)
+            return carry
+
+        lax.fori_loop(0, hidden // block, hidden_step, 0)
+        signed = expand(line, pl.ds(hidden, n_sel - hidden))
+        affinity = jnp.abs(signed)
+        grad_aff = jnp.where(signed > 0, daff[...], 0.0)
+        total = jnp.sum(affinity * grad_aff, axis=1, keepdims=True)
+        dlg[...] = (affinity * (grad_aff - total)).astype(bf16)
+
+        @pl.when(u == 0)
+        def _():
+            if lines > 2:
+                chain_event(2)
+
+        for v in range(1, lines - 1):
+
+            @pl.when(u == v)
+            def _(v=v):
+                xy_event(v + 1)
+                if v + 2 < lines:
+                    start(send_own(v + 2))
+
+        def weight_step(i, carry):
+            h = pl.ds(pl.multiple_of(i * block, block), block)
+            x = nc[rows, 0:width]
+            dw[0, h, :] += dot_tn(dg[:, h], x)
+            dw[1, h, :] += dot_tn(du[:, h], x)
+            dw[2, h, :] += dot_tn(acts[:, h], nc[rows, width : 2 * width])
+            return carry
+
+        lax.fori_loop(0, hidden // block, weight_step, 0)
+        dr[...] += dot_tn(dlg[...], nc[rows, 0:width])
+
+        for v in range(lines):
+
+            @pl.when(u == v)
+            def _(v=v):
+                if v == 0:
+                    xy_event(1)
+                    if lines > 2:
+                        start(send_own(2))
+                    chain_drain(1)
+                elif v == 1:
+                    for k in range(2, lines):
+                        chain_drain(k)
+                elif v == 2:
+                    rs_mid(1)
+                sent_event(v)
+
+        def back_step(i, carry):
+            n = pl.ds(pl.multiple_of(i * block, block), block)
+            n2 = pl.ds(pl.multiple_of(width + i * block, block), block)
+            out = dense_dot(acts[...], vd[:, n])
+            back = (
+                dense_dot(dg[...], vg[:, n])
+                + dense_dot(du[...], vu[:, n])
+                + dense_dot(dlg[...], router_t[:, n])
+            )
+            nc[rows, n] = out.astype(bf16)
+            nc[rows, n2] = back.astype(bf16)
+            return carry
+
+        lax.fori_loop(0, width // block, back_step, 0)
+
+        @pl.when(u == 0)
+        def _():
+            for k in range(3, lines):
+                chain_event(k)
+
+        for v in range(1, lines):
+
+            @pl.when(u == v)
+            def _(v=v):
+                rs_start(v)
+
+        return carry
+
+    xy_event(0)
+    chain_event(1)
+    start(send_own(1))
+    for copy in w_copies:
+        copy.wait_recv()
+    for copy in local:
+        copy.wait()
+    lax.fori_loop(0, lines, unit, 0)
+
+    own_out = pltpu.make_async_copy(dw.at[:, mine], dw_own, local_sem.at[6])
+    own_out.start()
+    sib_out = remote(dw.at[:, theirs], dw_sib, w_send.at[3], w_recv.at[3], to_c)
+    sib_out.start()
+    rs_mid(2)
+    rs_end(1)
+    rs_start(0)
+    rs_mid(3)
+    rs_end(2)
+    rs_mid(0)
+    rs_end(3)
+    rs_end(0)
+    for slot in range(lines - 1):
+        k = 6 * lines + slot
+        remote(
+            zr.at[slot], zr.at[slot], rs_send.at[k], rs_recv.at[k], to_c
+        ).wait_recv()
+
+    def finish(k, carry):
+        there = pl.ds(pl.multiple_of(k * 128, 128), 128)
+        total = nc[pl.ds(spot(z, O) * count, count), there].astype(f32)
+        for slot in range(lines - 1):
+            total = total + zr[slot, :, there].astype(f32)
+        sums[:, there] = total
+        return carry
+
+    lax.fori_loop(0, 2 * width // 128, finish, 0)
+    for u in range(lines):
+        p_copy(u).wait_send()
+        q_copy(u).wait_send()
+        for part in (0, 1):
+            x_copy(u, part).wait_send()
+            y_copy(u, part).wait_send()
+        if u > 0:
+            z_copy(u).wait_send()
+    for copy in w_copies:
+        copy.wait_send()
+    sib_out.wait()
+    own_out.wait()
+
+
+def mixture_call(tok, aux, cot, weights, sel, sel_t, router_t, ones, collective_id):
+    lines = lax.axis_size("ep") // 2
+    count, width = tok.shape
+    hc = weights[0].shape[0]
+    anywhere = pl.BlockSpec(memory_space=pl.ANY)
+    vmem = pl.BlockSpec(memory_space=pltpu.VMEM)
+    n_rows = lines * 4 * count
+    return pl.pallas_call(
+        functools.partial(mixture_kernel, lines),
+        out_shape=(
+            jax.ShapeDtypeStruct((count, 2 * width), f32),
+            jax.ShapeDtypeStruct((3, hc, width), f32),
+            jax.ShapeDtypeStruct((3, hc, width), f32),
+            jax.ShapeDtypeStruct((128, width), f32),
+        ),
+        in_specs=[anywhere] * 6 + [vmem] * 4,
+        out_specs=(vmem, anywhere, anywhere, vmem),
+        scratch_shapes=[
+            pltpu.VMEM((n_rows, 2 * width), bf16),
+            pltpu.VMEM((lines * 4,) + aux.shape, bf16),
+            pltpu.VMEM((2 * hc, width), bf16),
+            pltpu.VMEM((2 * hc, width), bf16),
+            pltpu.VMEM((2 * hc, width), bf16),
+            pltpu.VMEM((3, 2 * hc, width), f32),
+            pltpu.VMEM((4 * count, 2 * hc), bf16),
+            pltpu.VMEM((4 * count, 2 * hc), bf16),
+            pltpu.VMEM((4 * count, 2 * hc), bf16),
+            pltpu.VMEM((4 * count, 128), f32),
+            pltpu.VMEM((4 * count, 128), bf16),
+            pltpu.VMEM((lines, count // 2, 2 * width), bf16),
+            pltpu.VMEM((lines, count // 2, 2 * width), bf16),
+            pltpu.VMEM((lines, count, 2 * width), bf16),
+            pltpu.VMEM((lines, count, 2 * width), bf16),
+            pltpu.VMEM((lines - 1, count, 2 * width), bf16),
+            pltpu.SemaphoreType.DMA((2, 6 * lines)),
+            pltpu.SemaphoreType.DMA((2, 6 * lines)),
+            pltpu.SemaphoreType.DMA((7 * lines,)),
+            pltpu.SemaphoreType.DMA((7 * lines,)),
+            pltpu.SemaphoreType.DMA((4,)),
+            pltpu.SemaphoreType.DMA((4,)),
+            pltpu.SemaphoreType.DMA((7,)),
+        ],
+        compiler_params=pltpu.CompilerParams(
+            collective_id=collective_id, has_side_effects=True, vmem_limit_bytes=62 * 2**20
+        ),
+        name="mixture",
+    )(tok, aux, cot, *weights, sel, sel_t, router_t, ones)
+
+
 def documents(positions, lengths):
     seq_ends = jnp.cumsum(lengths)
     doc_index = (positions >= seq_ends[0]).astype(jnp.int32) + (positions >= seq_ends[1]).astype(
@@ -483,9 +979,16 @@
     small = jnp.pad(small, ((0, -small.shape[0] % 16), (0, 0)))
     weights = jnp.concatenate([w_query, w_key, w_value, w_out], axis=1)
 
-    (all_weights, all_small, all_cot), (group_hidden,) = gather(
-        [weights, small, cotangent], [hidden_in], 0, "gather_weights"
-    )
+    small_slice = eps == 8 and tps == 4
+    if small_slice:
+        (all_weights, all_small, all_cot), (group_hidden,) = gather(
+            [weights, small, cotangent], [False, False, True], [hidden_in], 0, "gather_weights"
+        )
+    else:
+        all_weights, all_small, all_cot = [
+            lax.all_gather(v, AXES, axis=0) for v in (weights, small, cotangent)
+        ]
+        group_hidden = lax.all_gather(hidden_in, "tp", axis=0)
     all_weights = all_weights.reshape(devices * d_rows, 4 * width)
     full_query = all_weights[:, :width]
     full_key = all_weights[:, width : 2 * width]
@@ -496,7 +999,7 @@
     full_router = all_small[:, :n_router].reshape(devices * d_rows, experts)
     gain_one = all_small[:, n_router : n_router + d_rows].reshape(-1).astype(f32)
     gain_two = all_small[:, n_router + d_rows : n_router + 2 * d_rows].reshape(-1).astype(f32)
-    cot_all = all_cot.reshape(tokens, model_width)
+    cot_all = all_cot.reshape(-1, model_width)
 
     shared_cols = jnp.stack([shared_gate, shared_up], axis=1).reshape(d_rows, 2, devices, sh_rows)
     shared_cols = lax.all_to_all(
@@ -555,10 +1058,6 @@
     named = jnp.any(expert_ids[:, :, None] == expert_range[None, None, :], axis=1)
     signed = jnp.where(named, affinity, -affinity)
 
-    (all_normed, all_signed), _ = gather([normed_two, signed.T], [], 1, "gather_tokens")
-    rows = all_normed.reshape(tokens, model_width)
-    signed = all_signed.transpose(0, 2, 1).reshape(tokens, experts)
-
     first_expert = lax.axis_index("ep") * exp_local
     n_routed = exp_local * exp_hidden
     hidden = n_routed + sh_rows
@@ -611,12 +1110,41 @@
         )
         return out_part, dn2_part, sums
 
-    blocks = max(1, tokens * hidden * 4 // 2**23)
-    while tokens % blocks:
-        blocks += 1
-    if blocks == 1:
-        out_part, dn2_part, sums = mixture(rows, cot_all, signed)
+    if small_slice:
+        lanes = 128
+        h_core = -(-hidden // lanes) * lanes
+        pad = ((0, h_core - hidden), (0, 0))
+        signed_high = lax.reduce_precision(signed, 8, 7)
+        aux = jnp.concatenate([signed_high.T, (signed - signed_high).T]).astype(bf16)
+        owner = jnp.arange(h_core, dtype=jnp.int32)
+        owner = jnp.where(owner < n_routed, first_expert + owner // exp_hidden, experts)
+        owner = jnp.concatenate([owner, owner])
+        sel_t = (owner[:, None] == jnp.arange(lanes, dtype=jnp.int32)[None, :]).astype(bf16)
+        sel = jnp.concatenate([sel_t[:, :experts].T, jnp.eye(experts, lanes, dtype=bf16)], axis=1)
+        sel = jnp.concatenate([sel, sel])
+        ones = (jnp.arange(2 * h_core, dtype=jnp.int32) % h_core)[None, :]
+        ones = ((ones >= n_routed) & (ones < hidden)).astype(f32)
+        router_t = jnp.pad(full_router.T, ((0, lanes - experts), (0, 0)))
+        token_sums, grads_here, grads_there, router_sum = mixture_call(
+            normed_two,
+            aux,
+            cot_all,
+            [jnp.pad(w, pad) for w in (gate_w, up_w, down_w)],
+            sel,
+            sel_t,
+            router_t,
+            ones,
+            2,
+        )
+        routed_sum, grad_normed_two = token_sums[:, :model_width], token_sums[:, model_width:]
+        grads = grads_here + grads_there
+        grad_gate, grad_up, grad_down = [grads[k, :hidden] for k in range(3)]
+        router_part = router_sum[:experts].T
     else:
+        rows, signed_all = [lax.all_gather(v, AXES, axis=0, tiled=True) for v in (normed_two, signed)]
+        blocks = max(1, tokens * hidden * 4 // 2**23)
+        while tokens % blocks:
+            blocks += 1
 
         def step(totals, block):
             out_block, dn2_block, sums = mixture(*block)
@@ -628,19 +1156,15 @@
         sums, (out_part, dn2_part) = lax.scan(
             step,
             zeros,
-            jax.tree.map(lambda v: v.reshape((blocks, -1) + v.shape[1:]), (rows, cot_all, signed)),
-        )
-    grad_down, grad_gate, grad_up, router_part = sums
-
-    (routed_sum, grad_normed_two), _ = reduce_scatter(
-        [
-            out_part.reshape(devices, tok_count, model_width),
-            dn2_part.reshape(devices, tok_count, model_width),
-        ],
-        [],
-        2,
-        "reduce_tokens",
-    )
+            jax.tree.map(
+                lambda v: v.reshape((blocks, -1) + v.shape[1:]), (rows, cot_all, signed_all)
+            ),
+        )
+        grad_down, grad_gate, grad_up, router_part = sums
+        routed_sum, grad_normed_two = [
+            lax.psum_scatter(v.reshape(tokens, model_width), AXES, tiled=True).astype(f32)
+            for v in (out_part, dn2_part)
+        ]
     layer_output = (residual + routed_sum).astype(bf16)
 
     gain_two_part = jnp.sum(grad_normed_two * unit_two, axis=0)
@@ -686,12 +1210,17 @@
     small_part = jnp.pad(small_part, ((0, 0), (0, small_len - small_part.shape[1])))
     small_part = small_part.reshape(devices, -1, model_width)
     small_part = jnp.pad(small_part, ((0, 0), (0, -small_part.shape[1] % 16), (0, 0))).astype(bf16)
-    (weight_sum, small_sum), (normed_grad_sum,) = reduce_scatter(
-        [weight_part.reshape(devices, d_rows, 4 * width), small_part],
-        [group_normed_grad.astype(bf16).reshape(tps, tok_count, model_width)],
-        3,
-        "reduce_weights",
-    )
+    weight_part = weight_part.reshape(devices, d_rows, 4 * width)
+    group_part = group_normed_grad.astype(bf16).reshape(tps, tok_count, model_width)
+    if small_slice:
+        (weight_sum, small_sum), (normed_grad_sum,) = reduce_scatter(
+            [weight_part, small_part], [group_part], 3, "reduce_weights"
+        )
+    else:
+        weight_sum, small_sum = [
+            lax.psum_scatter(v, AXES).astype(f32) for v in (weight_part, small_part)
+        ]
+        normed_grad_sum = lax.psum_scatter(group_part, "tp").astype(f32)
     grad_normed = own_normed_grad + normed_grad_sum
     input_grad = grad_resid + norm_back(grad_normed, unit_one, inverse_one, gain_one)
     small_sum = small_sum.reshape(-1)

time: 713 us -> 561 us (0.79)
  matrix products: 176 us -> 51.6 us
  Pallas kernels: 390 us -> 366 us
  local copies, waits for them, and re-layouts: 72.6 us -> 60.5 us
    dot_general x24 -> x13, matrix products: 166 us -> 39.3 us  [dot(): lax.dot_general(left, right, ((contract[0], contract[1]), ((), ())), pref...]
    pallas_call x2 -> x1, Pallas kernels: 196 us -> 87.9 us  [reduce_scatter(): pl.pallas_call(functools.partial(reduce_kernel, lines, n_all, n_group), o...]
    pallas_call x2, Pallas kernels: 194 us -> 278 us  [the longest x1 160 us: mixture_call(): pl.pallas_call(functools.partial(mixture_kernel, lines), out_shape=(jax.S...]
    mul x1 -> x0, other arithmetic: 7.8 us -> none  [mixture(): act * grad_hidden]
    unnamed x198 -> x128, local copies, waits for them, and re-layouts: 20.4 us -> 18.3 us
  transfers between devices with their start and end apart: 2 -> 2, of which waited for: 0 -> 0; matrix products, arithmetic and copies ran while one was open for 15% -> 20% of each run, Pallas kernels for 40% -> 37%
where the time goes in v2:
time: 561 us; the launch traced here: 552 us
  Pallas kernels  366 us (65%)
  local copies, waits for them, and re-layouts  60.5 us (11%)
  other arithmetic  53.6 us (10%)
  matrix products  51.6 us (9%)
  starting transfers between devices  17.9 us (3%)
    pallas_call x1, Pallas kernels, mixture_call(): pl.pallas_call(functools.partial(mixture_kernel, lines), out_shape=(jax.S...  160 us
    pallas_call x1, Pallas kernels, gather(): pl.pallas_call(functools.partial(gather_kernel, lines, tuple(core_only),...  118 us
    pallas_call x1, Pallas kernels, reduce_scatter(): pl.pallas_call(functools.partial(reduce_kernel, lines, n_all, n_group), o...  87.9 us
    dot_general x13, matrix products, dot(): lax.dot_general(left, right, ((contract[0], contract[1]), ((), ())), pref...  39.3 us
    unnamed x128, local copies, waits for them, and re-layouts  18.3 us
  transfers between devices with their start and end apart: 2, of which 0 were waited for; matrix products, arithmetic and copies ran while one was open for 20% of the time, Pallas kernels for 37%

profile of v2, /device:TPU:0, one launch (start us, length us, event | category | flops | bytes accessed | tf_op | source)
XLA Modules:
  0.0 552.0 jit_solution(18197330088011422280)
XLA Ops:
  0.7 1.6 stack.18
  2.3 1.6 stack.19
  4.4 1.8 reshape.575
  6.2 7.4 %all-to-all-start = ((bf16[32,2,2240]{2,1,0:T(2,128)(2,1)}), bf16[32,2,2240]{2,1,0:T(2,128)(2,1)}, u32[]{:S(2)}, u32[]{:S(2)}) async-start(bf16[32,2,2240]{2,1,0:T(2,128)(2,1)} %reshape.575), calls=%async_computation | async-start | bytes 589824 | tf_op jit(solution)/shard_map/all_to_all | solution.py:1005
  14.4 1.3 subtract_convert_fusion.2
  15.7 1.3 fusion.79
  17.0 1.8 fusion.77
  20.7 117.8 %gather_weights.1 = (bf16[32,40,5120]{2,1,0:T(8,128)(2,1)}, bf16[32,16,1280]{2,1,0:T(8,128)(2,1)}, bf16[16,128,1280]{2,1,0:T(8,128)(2,1)}, bf16[4,128,1280]{2,1,0:T(8,128)(2,1)}) custom-call(bf16[40,5120]{1,0:T(8,128)(2,1)} %pad_maximum_fusion.4.refs_0_, bf16[16,1280]{1,0:T(8,128)(2,1)} %pad.33.refs_1_, bf16[128,1280]{1,0:T(8,128)(2,1)} %refs_2_.1, ...), custom_call_target="tpu_custom_call" | custom-call | tf_op jit(solution)/shard_map/gather_weights/pallas_call | solution.py:251
  138.5 1.7 copy.213
  142.2 2.2 slice_bitcast_fusion
  144.4 3.3 fusion.9
  148.7 2.0 copy.210
  150.7 2.0 copy.211
  152.8 1.6 multiply_reduce_fusion.2
  154.4 2.7 multiply_convert_fusion.1
  157.2 3.4 copy.171
  160.6 0.9 fusion.63
  161.5 1.2 fusion.61
  162.8 1.7 multiply_convert_fusion.2
  164.5 3.8 convolution_convert_fusion.4
  168.3 1.9 copy.167
  170.3 3.9 fusion.97
  175.7 2.7 fusion.95
  178.5 2.8 convolution_convert_fusion.6
  181.4 2.7 multiply_reduce_fusion.5
  188.1 1.0 copy.176
  189.1 1.5 copy.185
  191.2 2.4 fusion.28.wd
  193.6 1.8 reshape.576
  195.9 3.3 fusion.26
  199.1 160.3 %mixture.1 = (f32[128,2560]{1,0:T(8,128)}, f32[3,512,1280]{2,1,0:T(8,128)}, f32[3,512,1280]{2,1,0:T(8,128)}, f32[128,1280]{1,0:T(8,128)}) custom-call(bf16[128,1280]{1,0:T(8,128)(2,1)} %copy-done.6, bf16[32,128]{1,0:T(8,128)(2,1)} %pad_maximum_fusion.10.aux, bf16[2048,1280]{1,0:T(8,128)(2,1)} %bitcast.130, bf16[512,1280]{1,0:T(8,128)(2,1)} %get-tuple-element.172.wg, ...), custom_call_target="tpu_custom_call" | custom-call | tf_op jit(solution)/shard_map/mixture/pallas_call | solution.py:852
  359.5 1.9 multiply_reduce_fusion.3
  361.5 2.4 multiply_add_fusion.2
  363.8 3.2 fusion.22
  367.3 2.5 multiply_reduce_fusion.1
  369.9 1.6 convolution_convert_fusion.5
  372.6 2.1 multiply_bitcast_fusion
  375.2 6.5 %add.165 = f32[3,512,1280]{2,1,0:T(8,128)S(1)} add(f32[3,512,1280]{2,1,0:T(8,128)} %get-tuple-element.35, f32[3,512,1280]{2,1,0:T(8,128)} %get-tuple-element.36) | non-fusion elementwise | flops 1966080 | bytes 23592960 | tf_op jit(solution)/shard_map/add | solution.py:1140
  381.7 3.0 copy-done
  385.7 1.7 stack.21
  387.3 2.6 stack.22
  389.9 2.6 maximum_bitcast_fusion
  392.6 3.0 copy.191
  395.5 2.4 reshape.577
  397.9 10.5 %all-to-all-start.1 = ((f32[32,1,4480]{2,1,0:T(1,128)}), f32[32,1,4480]{2,1,0:T(1,128)S(1)}, u32[]{:S(2)}, u32[]{:S(2)}) async-start(f32[32,1,4480]{2,1,0:T(1,128)} %reshape.577), calls=%async_computation.1 | async-start | bytes 1146880 | tf_op jit(solution)/shard_map/all_to_all | solution.py:1230
  408.5 2.2 multiply_subtract_fusion
  410.7 5.9 %fusion.5 = f32[512,1280]{1,0:T(8,128)} fusion(bf16[512,1280]{0,1:T(8,128)(2,1)S(1)} %bitcast.161, bf16[1280,5120]{1,0:T(8,128)(2,1)} %bitcast.140), kind=kOutput, calls=%fused_computation.12 | convolution fusion | flops 1677721600 | bytes 7208960 | tf_op jit(solution)/shard_map/dot_general | solution.py:929
  417.4 3.3 fusion.7
  421.6 5.2 fusion.88
  428.6 1.2 pad.39.clone
  429.9 1.2 copy.183
  431.1 3.8 convolution_convert_fusion.2
  434.9 1.9 convolution_convert_fusion.1
  436.8 1.0 convolution_convert_fusion
  437.8 1.1 convolution_convert_fusion.3
  438.9 6.5 %pad_maximum_fusion.refs_0_ = bf16[4,2,2,2,40,5120]{5,4,3,2,1,0:T(8,128)(2,1)} fusion(bf16[4,2,2,2,40,1280]{5,4,3,2,1,0:T(8,128)(2,1)S(1)} %convolution_convert_fusion, bf16[4,2,2,2,40,1280]{5,4,3,2,1,0:T(8,128)(2,1)S(1)} %convolution_convert_fusion.1, bf16[4,2,2,2,40,1280]{5,4,3,2,1,0:T(8,128)(2,1)S(1)} %convolution_convert_fusion.2, ...), kind=kLoop, calls=%fused_computation.1 | loop fusion | flops 52428800 | bytes 26214400 | tf_op jit(solution)/shard_map/concatenate | solution.py:1201
  445.4 87.9 %reduce_weights.1 = (f32[40,5120]{1,0:T(8,128)}, f32[16,1280]{1,0:T(8,128)}, f32[128,1280]{1,0:T(8,128)}) custom-call(bf16[4,2,2,2,40,5120]{5,4,3,2,1,0:T(8,128)(2,1)} %pad_maximum_fusion.refs_0_, bf16[4,2,2,2,16,1280]{5,4,3,2,1,0:T(8,128)(2,1)} %bitcast.134, bf16[2,2,128,1280]{3,2,1,0:T(8,128)(2,1)} %bitcast.164), custom_call_target="tpu_custom_call" | custom-call | tf_op jit(solution)/shard_map/reduce_weights/pallas_call | solution.py:438
  533.3 1.4 fusion.40
  534.7 2.2 fusion.43
  539.4 6.1 %fusion.87 = (f32[1,448,1280]{2,1,0:T(8,128)}, f32[1,448,1280]{2,1,0:T(8,128)}, f32[1,448,1280]{2,1,0:T(8,128)}) fusion(f32[3,512,1280]{2,1,0:T(8,128)} %copy-done), kind=kLoop, calls=%fused_computation.173 | loop fusion | bytes 13762560 | tf_op jit(solution)/shard_map/slice | solution.py:1248
  546.0 2.0 reduce.1
  548.0 1.0 reshape.578
  549.3 1.1 squeeze.32
  550.5 1.1 squeeze.33
  (192 shorter events, 22.0 us)
Async XLA Ops:
  0.6 13.0 %copy-start.55 = (s32[1,3]{1,0:T(1,128)S(1)}, s32[1,3]{1,0:T(1,128)}, u32[]{:S(2)}) copy-start(s32[1,3]{1,0:T(1,128)} %param.18) | copy-start | bytes 40
  0.7 18.1 %copy-start.49 = (bf16[40,16]{0,1:T(8,128)(2,1)S(1)}, bf16[40,16]{0,1:T(8,128)(2,1)}, u32[]{:S(2)}) copy-start(bf16[40,16]{0,1:T(8,128)(2,1)} %param.29) | copy-start | bytes 3844
  0.7 18.3 %copy-start.54 = (bf16[40]{0:T(256)(128)(2,1)S(1)}, bf16[40]{0:T(256)(128)(2,1)}, u32[]{:S(2)}) copy-start(bf16[40]{0:T(256)(128)(2,1)} %param.20) | copy-start | bytes 244
  0.7 18.3 %copy-start.53 = (bf16[40]{0:T(256)(128)(2,1)S(1)}, bf16[40]{0:T(256)(128)(2,1)}, u32[]{:S(2)}) copy-start(bf16[40]{0:T(256)(128)(2,1)} %param.25) | copy-start | bytes 244
  0.7 18.4 %copy-start.2 = (bf16[128,1280]{1,0:T(8,128)(2,1)S(1)}, bf16[128,1280]{1,0:T(8,128)(2,1)}, u32[]{:S(2)}) copy-start(bf16[128,1280]{1,0:T(8,128)(2,1)} %refs_3_.1) | copy-start | bytes 983044
  2.3 17.6 %copy-start.34 = (bf16[40,1280]{1,0:T(8,128)(2,1)S(1)}, bf16[40,1280]{1,0:T(8,128)(2,1)}, u32[]{:S(2)}) copy-start(bf16[40,1280]{1,0:T(8,128)(2,1)} %param.24) | copy-start | bytes 307204
  2.3 17.6 %copy-start.35 = (bf16[40,1280]{1,0:T(8,128)(2,1)S(1)}, bf16[40,1280]{1,0:T(8,128)(2,1)}, u32[]{:S(2)}) copy-start(bf16[40,1280]{1,0:T(8,128)(2,1)} %param.23) | copy-start | bytes 307204
  2.3 17.6 %copy-start.36 = (bf16[40,1280]{1,0:T(8,128)(2,1)S(1)}, bf16[40,1280]{1,0:T(8,128)(2,1)}, u32[]{:S(2)}) copy-start(bf16[40,1280]{1,0:T(8,128)(2,1)} %param.22) | copy-start | bytes 307204
  2.3 17.6 %copy-start.37 = (bf16[40,1280]{1,0:T(8,128)(2,1)S(1)}, bf16[40,1280]{1,0:T(8,128)(2,1)}, u32[]{:S(2)}) copy-start(bf16[40,1280]{1,0:T(8,128)(2,1)} %param.21) | copy-start | bytes 307204
  6.2 187.5 %all-to-all-start = ((bf16[32,2,2240]{2,1,0:T(2,128)(2,1)}), bf16[32,2,2240]{2,1,0:T(2,128)(2,1)}, u32[]{:S(2)}, u32[]{:S(2)}) async-start(bf16[32,2,2240]{2,1,0:T(2,128)(2,1)} %reshape.575), calls=%async_computation | async-start | bytes 589824 | tf_op jit(solution)/shard_map/all_to_all | solution.py:1005
  142.2 20.6 %copy-start.27 = (f32[1280]{0:T(1024)}, f32[1280]{0:T(1024)S(1)}, u32[]{:S(2)}) copy-start(f32[1280]{0:T(1024)S(1)} %reshape.568) | copy-start | bytes 15364
  142.2 2.2 copy-start.47
  142.2 2.2 copy-start.3
  154.4 8.4 %copy-start.43 = (f32[512]{0:T(512)}, f32[512]{0:T(512)S(1)}, u32[]{:S(2)}) copy-start(f32[512]{0:T(512)S(1)} %get-tuple-element.154) | copy-start | bytes 6148
  162.8 11.5 %copy-start.18 = (f32[512,64]{0,1:T(8,128)}, f32[512,64]{0,1:T(8,128)S(1)}, u32[]{:S(2)}) copy-start(f32[512,64]{0,1:T(8,128)S(1)} %get-tuple-element.152) | copy-start | bytes 393220
  168.3 1.9 copy-start.5
  170.3 4.0 copy-start.25
  174.2 0.7 copy-start.51
  174.2 0.7 copy-start.52
  174.2 1.1 copy-start.8
  174.2 1.3 copy-start.9
  174.7 3.7 copy-start.21
  174.7 3.7 copy-start.23
  175.7 2.8 copy-start.11
  175.7 2.8 copy-start.13
  178.5 2.8 copy-start.41
  178.5 2.9 copy-start.4
  181.3 2.7 copy-start.38
  181.3 2.8 copy-start.30
  181.3 3.1 copy-start.50
  184.0 1.9 copy-start.45
  184.1 6.5 %copy-start.32 = (f32[1280]{0:T(1024)}, f32[1280]{0:T(1024)S(1)}, u32[]{:S(2)}) copy-start(f32[1280]{0:T(1024)S(1)} %reshape.569) | copy-start | bytes 15364
  184.7 0.8 copy-start.10
  185.5 5.1 copy-start.40
  185.5 5.7 %copy-start.31 = (bf16[56,1280]{1,0:T(8,128)(2,1)S(1)}, bf16[56,1280]{1,0:T(8,128)(2,1)}, u32[]{:S(2)}) copy-start(bf16[56,1280]{1,0:T(8,128)(2,1)} %param.28) | copy-start | bytes 430084
  185.7 8.0 %copy-start.6 = (bf16[128,1280]{1,0:T(8,128)(2,1)}, bf16[128,1280]{1,0:T(8,128)(2,1)S(1)}, u32[]{:S(2)}) copy-start(bf16[128,1280]{1,0:T(8,128)(2,1)S(1)} %multiply_convert_fusion.3.tok) | copy-start | bytes 983044
  199.1 160.4 %copy-start.33 = (f32[1280]{0:T(1024)S(1)}, f32[1280]{0:T(1024)}, u32[]{:S(2)}) copy-start(f32[1280]{0:T(1024)} %copy-done.32) | copy-start | bytes 15364
  199.1 160.4 %copy-start.46 = (f32[128]{0:T(128)S(1)}, f32[128]{0:T(128)}, u32[]{:S(2)}) copy-start(f32[128]{0:T(128)} %copy-done.45) | copy-start | bytes 1540
  363.8 3.4 copy-start.16
  363.8 3.4 copy-start.42
  367.3 2.6 copy-start.7
  371.5 1.0 copy-start.12
  371.5 1.1 copy-start.14
  372.6 2.1 copy-start.22
  372.6 2.1 copy-start.24
  381.7 3.1 copy-start
  392.6 15.9 %copy-start.19 = (f32[512,64]{0,1:T(8,128)S(1)}, f32[512,64]{0,1:T(8,128)}, u32[]{:S(2)}) copy-start(f32[512,64]{0,1:T(8,128)} %copy-done.18) | copy-start | bytes 393220
  397.9 147.5 %all-to-all-start.1 = ((f32[32,1,4480]{2,1,0:T(1,128)}), f32[32,1,4480]{2,1,0:T(1,128)S(1)}, u32[]{:S(2)}, u32[]{:S(2)}) async-start(f32[32,1,4480]{2,1,0:T(1,128)} %reshape.577), calls=%async_computation.1 | async-start | bytes 1146880 | tf_op jit(solution)/shard_map/all_to_all | solution.py:1230
  410.7 5.9 %copy-start.17 = (bf16[512,10,128]{0,2,1:T(8,128)(2,1)}, bf16[512,10,128]{0,2,1:T(8,128)(2,1)S(1)}, u32[]{:S(2)}) copy-start(bf16[512,10,128]{0,2,1:T(8,128)(2,1)S(1)} %maximum_convert_fusion) | copy-start | bytes 3932164
  410.7 5.9 %copy-start.29 = (f32[128,64]{1,0:T(8,128)S(1)}, f32[128,64]{1,0:T(8,128)}, u32[]{:S(2)}) copy-start(f32[128,64]{1,0:T(8,128)} %get-tuple-element.155) | copy-start | bytes 98308
  417.1 3.6 copy-start.28
  417.1 3.6 copy-start.48
  417.4 4.2 copy-start.1
  417.4 4.2 copy-start.44
  417.4 4.2 copy-start.56
  417.4 4.2 copy-start.58
  421.6 6.7 %copy-start.39 = (bf16[1280]{0:T(1024)(128)(2,1)S(1)}, bf16[1280]{0:T(1024)(128)(2,1)}, u32[]{:S(2)}) copy-start(bf16[1280]{0:T(1024)(128)(2,1)} %get-tuple-element.112) | copy-start | bytes 7684
  431.0 3.8 copy-start.15
  431.0 3.8 copy-start.57
  533.3 3.7 copy-start.20
  534.7 3.1 copy-start.26

commit v3 on v2

--- a/solution.py
+++ b/solution.py
@@ -31,16 +31,6 @@
     return ((line * 2 + a) * 2 + b) * 2 + c
 
 
-def halves(shape):
-    rows, cols = shape
-    if cols % 256 == 0:
-        return (
-            (pl.ds(0, rows), pl.ds(0, cols // 2)),
-            (pl.ds(0, rows), pl.ds(cols // 2, cols // 2)),
-        )
-    return ((pl.ds(0, rows // 2), pl.ds(0, cols)), (pl.ds(rows // 2, rows // 2), pl.ds(0, cols)))
-
-
 def greet(partners):
     barrier = pltpu.get_barrier_semaphore()
     for partner in partners:
@@ -48,6 +38,9 @@
     pl.semaphore_wait(barrier, len(partners))
 
 
+O, X, Y, D = 0, 1, 2, 3
+
+
 def visit_order(lines):
     return [sorted(range(lines), key=lambda other: (abs(other - z), other)) for z in range(lines)]
 
@@ -66,390 +59,428 @@
     return out
 
 
-def gather_kernel(lines, core_only, n_group, *refs):
-    n_all = len(core_only)
-    n = n_all + n_group
-    ins, outs = refs[:n], refs[n : 2 * n]
-    send_sem, recv_sem, group_send, group_recv, local_sem = refs[2 * n :]
-    z, a, b, c = place()
-    oa, ob, oc = 1 - a, 1 - b, 1 - c
-    to_b, to_a, to_c = device(z, a, ob, c), device(z, oa, b, c), device(z, a, b, oc)
-    up_next = device(lax.rem(z + 1, lines), a, b, c)
-    down_next = device(lax.rem(z + lines - 1, lines), a, b, c)
-    greet(
-        [to_b, to_a, to_c] + [device(lax.rem(z + s, lines), a, b, c) for s in range(1, lines)]
-    )
-    table = visit_order(lines)
-    zs = [lookup([table[k][u] for k in range(lines)], z) for u in range(lines)]
-    O, X, Y, D = 0, 1, 2, 3
-    sent = []
-
-    def chunk(i, line, kind, part=None, core=None):
-        if core_only[i]:
-            at = line * 4 + kind
-        else:
-            at = number(line, (a, a, oa, oa)[kind], (b, ob, b, ob)[kind], c if core is None else core)
-        if part is None:
-            return outs[i].at[at]
-        return outs[i].at[(at,) + halves(outs[i].shape[1:])[part]]
-
-    def remote(i, slot, step, src, dst, to):
-        k = slot * lines + step
-        return pltpu.make_async_remote_copy(
-            src, dst, send_sem.at[i, k], recv_sem.at[i, k], device_id=to, device_id_type=MESH
-        )
-
-    def hop(i, slot, step, kind, to_kind, line, to, part=None, own=False):
-        src = ins[i] if own else chunk(i, line, kind, part)
-        there = chunk(i, line, to_kind if core_only[i] else kind, part)
-        return remote(i, slot, step, src, there, to)
-
-    def arrival(i, slot, step, kind, line, part=None):
-        here = chunk(i, line, kind, part)
-        remote(i, slot, step, here, here, to_c).wait_recv()
-
-    def send(copy):
+class Ways:
+    def __init__(self, lines):
+        self.lines = lines
+        z, a, b, c = self.spot = place()
+        oa, ob, oc = 1 - a, 1 - b, 1 - c
+        self.to_b, self.to_a = device(z, a, ob, c), device(z, oa, b, c)
+        self.to_c = device(z, a, b, oc)
+        self.up_next = device(lax.rem(z + 1, lines), a, b, c)
+        self.down_next = device(lax.rem(z + lines - 1, lines), a, b, c)
+        self.peers = [device(lax.rem(z + s, lines), a, b, c) for s in range(1, lines)]
+        table = visit_order(lines)
+        self.zs = [lookup([table[k][u] for k in range(lines)], z) for u in range(lines)]
+        self.column = ((a, b), (a, ob), (oa, b), (oa, ob))
+
+    def greet(self):
+        greet([self.to_b, self.to_a, self.to_c] + self.peers)
+
+    def chip(self, line, kind):
+        a, b = self.column[kind]
+        return (line * 2 + a) * 2 + b
+
+
+def remote(src, dst, send_sem, recv_sem, to):
+    return pltpu.make_async_remote_copy(
+        src, dst, send_sem, recv_sem, device_id=to, device_id_type=MESH
+    )
+
+
+class Gather:
+    def __init__(self, ways, chunk, sems, own=None, relative=False, across=False):
+        self.ways, self.chunk, self.own = ways, chunk, own
+        self.send_sem, self.recv_sem = sems
+        self.relative, self.across_core = relative, across
+        self.sent = []
+
+    def copy(self, slot, step, src, dst, to):
+        k = slot * self.ways.lines + step
+        return remote(src, dst, self.send_sem(k), self.recv_sem(k), to)
+
+    def hop(self, slot, step, kind, to_kind, line, to, part=None, own=False):
+        src = self.own if own and self.own is not None else self.chunk(line, kind, part, False)
+        dst = self.chunk(line, to_kind if self.relative else kind, part, False)
+        return self.copy(slot, step, src, dst, to)
+
+    def send(self, copy):
         copy.start()
-        sent.append(copy)
-
-    def across(i, slot, u, kind, part=None, own=False):
-        if not core_only[i]:
-            here = chunk(i, zs[u], kind, part)
-            send(remote(i, slot, u, ins[i] if own else here, here, to_c))
-
-    def send_own(u):
-        own = u == 0
-        for i in range(n_all):
-            send(hop(i, 0, u, O, X, zs[u], to_b, own=own))
-            send(hop(i, 1, u, O, Y, zs[u], to_a, own=own))
-        for i in range(n_all):
-            across(i, 6, u, O, own=own)
-
-    def xy_event(u):
-        for i in range(n_all):
-            arrival(i, 0, u, X, zs[u])
-            send(hop(i, 2, u, X, D, zs[u], to_a, 0))
-            arrival(i, 1, u, Y, zs[u])
-            send(hop(i, 3, u, Y, D, zs[u], to_b, 1))
-            across(i, 7, u, X)
-            across(i, 8, u, Y)
-
-    def diag_event(u):
-        for i in range(n_all):
-            arrival(i, 2, u, D, zs[u], 0)
-            across(i, 9, u, D, 0)
-            arrival(i, 3, u, D, zs[u], 1)
-            across(i, 10, u, D, 1)
-
-    def chain_up(i, k):
-        return hop(i, 4, k, O, O, z - (k - 1), up_next, own=k == 1)
-
-    def chain_down(i, k):
-        return hop(i, 5, k, O, O, z + (k - 1), down_next, own=k == 1)
-
-    def chain_start(k):
+        self.sent.append(copy)
+
+    def arrival(self, slot, step, kind, line, part=None, other=False):
+        here = self.chunk(line, kind, part, other)
+        self.copy(slot, step, here, here, self.ways.to_c).wait_recv()
+
+    def across(self, slot, u, kind, part=None, own=False):
+        if self.across_core:
+            here = self.chunk(self.ways.zs[u], kind, part, False)
+            src = self.own if own and self.own is not None else here
+            self.send(self.copy(slot, u, src, here, self.ways.to_c))
+
+    def send_own(self, u):
+        w, own = self.ways, u == 0
+        self.send(self.hop(0, u, O, X, w.zs[u], w.to_b, own=own))
+        self.send(self.hop(1, u, O, Y, w.zs[u], w.to_a, own=own))
+        self.across(6, u, O, own=own)
+
+    def xy_event(self, u):
+        w = self.ways
+        self.arrival(0, u, X, w.zs[u])
+        self.send(self.hop(2, u, X, D, w.zs[u], w.to_a, 0))
+        self.arrival(1, u, Y, w.zs[u])
+        self.send(self.hop(3, u, Y, D, w.zs[u], w.to_b, 1))
+        self.across(7, u, X)
+        self.across(8, u, Y)
+
+    def diag_event(self, u):
+        line = self.ways.zs[u]
+        self.arrival(2, u, D, line, 0)
+        self.across(9, u, D, 0)
+        self.arrival(3, u, D, line, 1)
+        self.across(10, u, D, 1)
+
+    def chain_up(self, k):
+        w = self.ways
+        return self.hop(4, k, O, O, w.spot[0] - (k - 1), w.up_next, own=k == 1)
+
+    def chain_down(self, k):
+        w = self.ways
+        return self.hop(5, k, O, O, w.spot[0] + (k - 1), w.down_next, own=k == 1)
+
+    def chain_start(self, k):
+        z, lines = self.ways.spot[0], self.ways.lines
         if k >= lines:
             return
 
         @pl.when((z >= k - 1) & (z + 1 < lines))
         def _():
-            for i in range(n_all):
-                chain_up(i, k).start()
+            self.chain_up(k).start()
 
         @pl.when((z + k - 1 < lines) & (z > 0))
         def _():
-            for i in range(n_all):
-                chain_down(i, k).start()
-
-    def chain_event(k):
+            self.chain_down(k).start()
+
+    def chain_event(self, k):
+        z, lines = self.ways.spot[0], self.ways.lines
+
         @pl.when(z >= k)
         def _():
-            for i in range(n_all):
-                arrival(i, 4, k, O, z - k)
+            self.arrival(4, k, O, z - k)
 
         @pl.when(z + k < lines)
         def _():
-            for i in range(n_all):
-                arrival(i, 5, k, O, z + k)
-
-        chain_start(k + 1)
-
-    def chain_drain(k):
-        @pl.when((z >= k - 1) & (z + 1 < lines))
-        def _():
-            for i in range(n_all):
-                chain_up(i, k).wait_send()
-
-        @pl.when((z + k - 1 < lines) & (z > 0))
-        def _():
-            for i in range(n_all):
-                chain_down(i, k).wait_send()
-
-    group_copies = []
-
-    def group_copy(g, k, src, dst, to):
-        return pltpu.make_async_remote_copy(
-            src, dst, group_send.at[g, k], group_recv.at[g, k], device_id=to, device_id_type=MESH
+            self.arrival(5, k, O, z + k)
+
+        self.chain_start(k + 1)
+
+    def begin(self):
+        self.send_own(0)
+        self.chain_start(1)
+
+    def events(self):
+        lines = self.ways.lines
+        out = [
+            lambda: (self.xy_event(0), self.chain_event(1), self.send_own(1)),
+        ]
+        for u in range(2, lines):
+            out.append(lambda u=u: (self.chain_event(u), self.xy_event(u - 1), self.send_own(u)))
+            out.append(lambda u=u: self.diag_event(u - 2))
+        out.append(lambda: self.xy_event(lines - 1))
+        out.append(lambda: self.diag_event(lines - 2))
+        out.append(lambda: self.diag_event(lines - 1))
+        return out
+
+    def other_core(self):
+        if self.across_core:
+            for u in range(self.ways.lines):
+                for slot, kind, part in (
+                    (6, O, None), (7, X, None), (8, Y, None), (9, D, 0), (10, D, 1),
+                ):
+                    self.arrival(slot, u, kind, self.ways.zs[u], part, True)
+
+    def drain(self):
+        z, lines = self.ways.spot[0], self.ways.lines
+        for copy in self.sent:
+            copy.wait_send()
+        for k in range(1, lines):
+
+            @pl.when((z >= k - 1) & (z + 1 < lines))
+            def _(k=k):
+                self.chain_up(k).wait_send()
+
+            @pl.when((z + k - 1 < lines) & (z > 0))
+            def _(k=k):
+                self.chain_down(k).wait_send()
+
+
+def softmax_rows(scores):
+    weights = jnp.exp(scores - jnp.max(scores, axis=-1, keepdims=True))
+    return weights * (1.0 / jnp.sum(weights, axis=-1, keepdims=True))
+
+
+def turn(values, cosine, signed_sine):
+    return values * cosine + pltpu.roll(values, values.shape[-1] // 2, 1) * signed_sine
+
+
+def document_of(positions, first_end, second_end):
+    return (positions >= first_end).astype(jnp.int32) + (positions >= second_end).astype(jnp.int32)
+
+
+def make_bias(bias, lengths, tp_index):
+    rows, cols = bias.shape
+    first_end = lengths[0, 0]
+    second_end = first_end + lengths[0, 1]
+    q_pos = lax.broadcasted_iota(jnp.int32, (rows, cols), 0) + tp_index * rows
+    k_pos = lax.broadcasted_iota(jnp.int32, (rows, cols), 1)
+    allowed = (
+        document_of(q_pos, first_end, second_end) == document_of(k_pos, first_end, second_end)
+    ) & (q_pos >= k_pos)
+    bias[...] = jnp.where(allowed, 0.0, -1e30)
+
+
+def front_kernel(lines, experts, scale, *refs):
+    (
+        lengths, ids, freq, hidden, small, wq, wk, wv, wo, cot,
+        w_out, cot_out, tok, aux, small_t, residual, attended, q_out, k_out, v_out, n_out,
+        cos_out, sin_out, group,
+        wall, stage, small_stage, small_all, bias,
+        g_send, g_recv, s_send, s_recv, x_send, x_recv, local_sem,
+    ) = refs
+    ways = Ways(lines)
+    z, a, b, c = ways.spot
+    ob, oc = 1 - b, 1 - c
+    count, width = hidden.shape
+    d_rows = wq.shape[0]
+    chip_rows = 2 * d_rows
+    half = width // 2
+    heads = width // 128
+    group_len = 4 * count
+    ways.greet()
+
+    shards = (wq, wk, wv, wo)
+    swaps = [
+        remote(
+            shards[k].at[:, pl.ds(pl.multiple_of(oc * half, 128), half)], stage.at[k],
+            s_send.at[k], s_recv.at[k], ways.to_c,
         )
-
-    keeps = []
-    send_own(0)
-    chain_start(1)
-    for g in range(n_group):
-        src, dst = ins[n_all + g], outs[n_all + g].at[b * 2 + c]
-        for k, to in enumerate((to_c, to_b)):
-            group_copies.append(group_copy(g, k, src, dst, to))
-            group_copies[-1].start()
-        keeps.append(pltpu.make_async_copy(src, dst, local_sem.at[n_all + g]))
-    for i in range(n_all):
-        keeps.append(pltpu.make_async_copy(ins[i], chunk(i, z, O), local_sem.at[i]))
-    for keep in keeps:
-        keep.start()
-    for g in range(n_group):
-        got = outs[n_all + g].at[ob * 2 + c]
-        group_copy(g, 1, got, got, to_b).wait_recv()
-        group_copies.append(group_copy(g, 2, got, got, to_c))
-        group_copies[-1].start()
-    xy_event(0)
-    chain_event(1)
-    send_own(1)
-    for u in range(2, lines):
-        chain_event(u)
-        xy_event(u - 1)
-        diag_event(u - 2)
-        send_own(u)
-    xy_event(lines - 1)
-    diag_event(lines - 2)
-    diag_event(lines - 1)
-    for u in range(lines):
-        for i in range(n_all):
-            if not core_only[i]:
-                for slot, kind, part in ((6, O, None), (7, X, None), (8, Y, None), (9, D, 0), (10, D, 1)):
-                    there = chunk(i, zs[u], kind, part, oc)
-                    remote(i, slot, u, there, there, to_c).wait_recv()
-    for g in range(n_group):
-        for k, t in ((0, b * 2 + oc), (2, ob * 2 + oc)):
-            got = outs[n_all + g].at[t]
-            group_copy(g, k, got, got, to_c).wait_recv()
-    for copy in sent + group_copies:
+        for k in range(4)
+    ] + [remote(small, small_stage, s_send.at[4], s_recv.at[4], ways.to_c)]
+    for copy in swaps:
+        copy.start()
+
+    def group_copy(k, src, dst, to):
+        return remote(src, dst, x_send.at[k], x_recv.at[k], to)
+
+    own_group = group.at[b * 2 + c]
+    group_copies = [group_copy(0, hidden, own_group, ways.to_c), group_copy(1, hidden, own_group, ways.to_b)]
+    for copy in group_copies:
+        copy.start()
+    own_group[...] = hidden[...]
+
+    def chip_block(own, other):
+        own, other = own.astype(f32), other.astype(f32)
+        first = jnp.where(c == 0, own, other)
+        second = jnp.where(c == 0, other, own)
+        return jnp.concatenate([first, second], axis=0).astype(bf16)
+
+    base = pl.multiple_of(ways.chip(z, O) * chip_rows, 16)
+    for copy in swaps:
+        copy.wait_recv()
+    small_all[pl.ds(base, chip_rows), :] = chip_block(small[...], small_stage[...])
+    for k in range(4):
+        mine = shards[k][:, pl.ds(pl.multiple_of(c * half, 128), half)]
+        wall[pl.ds(base, chip_rows), pl.ds(pl.multiple_of((c * 4 + k) * half, 128), half)] = chip_block(
+            mine, stage[k]
+        )
+
+    def small_chunk(line, kind, part, other):
+        rows = pl.multiple_of(ways.chip(line, kind) * chip_rows, 16)
+        if part is None:
+            return small_all.at[pl.ds(rows, chip_rows)]
+        low = chip_rows // 32 * 16
+        return small_all.at[pl.ds(rows, low) if part == 0 else pl.ds(rows + low, chip_rows - low)]
+
+    def weight_chunk(first, cols, cut):
+        def chunk(line, kind, part, other):
+            rows = pl.multiple_of(ways.chip(line, kind) * chip_rows, 16)
+            col = (oc if other else c) * 4 * half + first
+            if part is None:
+                start, size = col, cols
+            elif part == 0:
+                start, size = col, cut
+            else:
+                start, size = col + cut, cols - cut
+            return wall.at[pl.ds(rows, chip_rows), pl.ds(pl.multiple_of(start, 128), size)]
+
+        return chunk
+
+    def cot_chunk(line, kind, part, other):
+        first = (line * 4 + kind) * count
+        if part is None:
+            return cot_out.at[pl.ds(first, count)]
+        return cot_out.at[pl.ds(first + part * (count // 2), count // 2)]
+
+    def sems(i):
+        return (lambda k: g_send.at[i, k], lambda k: g_recv.at[i, k])
+
+    tiles = half // 128
+    g_small = Gather(ways, small_chunk, sems(0))
+    g_qkv = Gather(ways, weight_chunk(0, 3 * half, (3 * tiles + 1) // 2 * 128), sems(1), across=True)
+    g_out = Gather(ways, weight_chunk(3 * half, half, tiles // 2 * 128), sems(2), across=True)
+    g_cot = Gather(ways, cot_chunk, sems(3), own=cot, relative=True)
+    keep = pltpu.make_async_copy(cot, cot_chunk(z, O, None, False), local_sem.at[0])
+    keep.start()
+    g_small.begin()
+    g_qkv.begin()
+
+    first_end = lengths[0, 0]
+    second_end = first_end + lengths[0, 1]
+    position = lax.broadcasted_iota(jnp.int32, (group_len, 128), 0)
+    doc = document_of(position, first_end, second_end)
+    start = jnp.where(doc == 0, 0, jnp.where(doc == 1, first_end, second_end))
+    angles = (position - start).astype(f32) * freq[...]
+    lane = lax.broadcasted_iota(jnp.int32, (group_len, 128), 1)
+    cos_out[...] = jnp.cos(angles)
+    sin_out[...] = jnp.where(lane < 64, -1.0, 1.0) * jnp.sin(angles)
+    make_bias(bias, lengths, b * 2 + c)
+    got = group.at[ob * 2 + c]
+    group_copy(1, got, got, ways.to_b).wait_recv()
+    group_copies.append(group_copy(2, got, got, ways.to_c))
+    group_copies[-1].start()
+    for k, t in ((0, b * 2 + oc), (2, ob * 2 + oc)):
+        got = group.at[t]
+        group_copy(k, got, got, ways.to_c).wait_recv()
+
+    for k, events in enumerate(zip(g_small.events(), g_qkv.events())):
+        for event in events:
+            event()
+        if k == 2 * lines - 3:
+            g_out.begin()
+    flat = jnp.transpose(small_all[...].astype(f32))
+    small_t[...] = flat.astype(bf16)
+    gain_one = flat[experts : experts + 1, :]
+    gain_two = flat[experts + 1 : experts + 2, :]
+    for t in range(4):
+        x = group[t].astype(f32)
+        r = lax.rsqrt(jnp.mean(x * x, axis=-1, keepdims=True) + epsilon)
+        n_out[t * count : (t + 1) * count, :] = (x * r * gain_one).astype(bf16)
+    g_qkv.other_core()
+
+    out_events = g_out.events()
+    later = out_events[:-2] + [g_cot.begin] + out_events[-2:] + [g_out.other_core] + g_cot.events()
+
+    def service(n=1):
+        for _ in range(n):
+            if later:
+                later.pop(0)()
+
+    own_rows = pl.ds(pl.multiple_of((b * 2 + c) * count, count), count)
+    for h in range(2):
+        cols = pl.ds((h * 4 + 1) * half, half)
+        keys = dense_dot(n_out[...], wall[:, cols])
+        for j in range(half // 128):
+            k_out[:, h * half + j * 128 : h * half + (j + 1) * 128] = turn(
+                keys[:, j * 128 : (j + 1) * 128], cos_out[...], sin_out[...]
+            ).astype(bf16)
+        service()
+        cols = pl.ds((h * 4 + 2) * half, half)
+        v_out[:, h * half : (h + 1) * half] = dense_dot(n_out[...], wall[:, cols]).astype(bf16)
+        service()
+        queries = dense_dot(n_out[own_rows, :], wall[:, pl.ds(h * 4 * half, half)])
+        for j in range(half // 128):
+            q_out[:, h * half + j * 128 : h * half + (j + 1) * 128] = turn(
+                queries[:, j * 128 : (j + 1) * 128], cos_out[own_rows, :], sin_out[own_rows, :]
+            ).astype(bf16)
+        service()
+    for h in range(heads):
+        cols = pl.ds(h * 128, 128)
+        probs = softmax_rows(dot_nt(q_out[:, cols], k_out[:, cols]) * scale + bias[...])
+        attended[:, cols] = dense_dot(probs.astype(bf16), v_out[:, cols]).astype(bf16)
+        if h % 2:
+            service()
+    while len(later) > len(g_cot.events()):
+        service()
+    for h in range(2):
+        projected = dense_dot(attended[...], wall[:, pl.ds((h * 4 + 3) * half, half)])
+        residual[:, h * half : (h + 1) * half] = (
+            hidden[:, h * half : (h + 1) * half].astype(f32) + projected
+        )
+    service()
+    res = residual[...]
+    r2 = lax.rsqrt(jnp.mean(res * res, axis=-1, keepdims=True) + epsilon)
+    normed = (res * r2 * gain_two).astype(bf16)
+    tok[...] = normed
+    logits = dense_dot(normed, small_all[...])
+    lane = lax.broadcasted_iota(jnp.int32, (count, 128), 1)
+    affinity = softmax_rows(jnp.where(lane < experts, logits, -1e30))
+    named = lane < 0
+    for j in range(ids.shape[1]):
+        named = named | (ids[:, j : j + 1] == lane)
+    signed = jnp.transpose(jnp.where(named, affinity, -affinity))[:experts, :]
+    high = signed.astype(bf16)
+    aux[0:experts, :] = high
+    aux[experts : 2 * experts, :] = (signed - high.astype(f32)).astype(bf16)
+    save = pltpu.make_async_copy(wall, w_out, local_sem.at[1])
+    save.start()
+    service(len(later))
+    for g in (g_small, g_qkv, g_out, g_cot):
+        g.drain()
+    for copy in swaps + group_copies:
         copy.wait_send()
-    for k in range(1, lines):
-        chain_drain(k)
-    for keep in keeps:
-        keep.wait()
-
-
-def gather(everyone, core_only, group, collective_id, name):
-    eps, tps = lax.axis_size("ep"), lax.axis_size("tp")
-    lines = eps // 2
-    n_all, n_group = len(everyone), len(group)
-    shapes = [
-        jax.ShapeDtypeStruct((eps * tps // (2 if core else 1),) + v.shape, v.dtype)
-        for v, core in zip(everyone, core_only)
-    ] + [jax.ShapeDtypeStruct((tps,) + v.shape, v.dtype) for v in group]
-    anywhere = pl.BlockSpec(memory_space=pl.ANY)
-    outs = pl.pallas_call(
-        functools.partial(gather_kernel, lines, tuple(core_only), n_group),
-        out_shape=shapes,
-        in_specs=[anywhere] * (n_all + n_group),
-        out_specs=[anywhere] * (n_all + n_group),
-        scratch_shapes=[
-            pltpu.SemaphoreType.DMA((n_all, 11 * lines)),
-            pltpu.SemaphoreType.DMA((n_all, 11 * lines)),
-            pltpu.SemaphoreType.DMA((max(n_group, 1), 3)),
-            pltpu.SemaphoreType.DMA((max(n_group, 1), 3)),
-            pltpu.SemaphoreType.DMA((n_all + n_group,)),
-        ],
-        compiler_params=pltpu.CompilerParams(collective_id=collective_id, has_side_effects=True),
-        name=name,
-    )(*everyone, *group)
-    return outs[:n_all], outs[n_all:]
-
-
-def add_into(dst, src, rows, first, cols, dst_at=(), src_at=()):
-    step = 256 if cols % 256 == 0 else 128
-
-    def body(k, carry):
-        there = pl.ds(pl.multiple_of(first + k * step, 128), step)
-        here = pl.ds(pl.multiple_of(k * step, 128), step)
-        total = dst[dst_at + (slice(None), there)].astype(f32) + src[
-            src_at + (slice(None), here)
-        ].astype(f32)
-        dst[dst_at + (slice(None), there)] = total.astype(bf16)
-        return carry
-
-    lax.fori_loop(0, cols // step, body, 0)
-
-
-def reduce_kernel(lines, n_all, n_group, *refs):
-    n = n_all + n_group
-    ins, outs = refs[:n], refs[n : 2 * n]
-    rest = list(refs[2 * n :])
-    per_all = [[rest.pop(0) for _ in range(7)] for _ in range(n_all)]
-    per_group = [[rest.pop(0) for _ in range(3)] for _ in range(n_group)]
-    send_sem, recv_sem, group_send, group_recv, local_sem = rest
-    z, a, b, c = place()
-    oa, ob, oc = 1 - a, 1 - b, 1 - c
-    to_b, to_a, to_c = device(z, a, ob, c), device(z, oa, b, c), device(z, a, b, oc)
-    to_line = [None] + [device(lax.rem(z + s, lines), a, b, c) for s in range(1, lines)]
-    greet([to_b, to_a, to_c] + to_line[1:])
-    order = list(range(1, lines)) + [0]
-    goal = [lax.rem(z + s, lines) for s in range(lines)]
-    started = []
-    kinds = {"s": 0, "p": 1, "q": 2, "x": 3, "y": 4, "z": 5}
-
-    def sems(i, kind, step):
-        k = kinds[kind] * lines + step
-        return send_sem.at[i, k], recv_sem.at[i, k]
-
-    def send(i, kind, step, src, dst, to):
-        copy = pltpu.make_async_remote_copy(
-            src, dst, *sems(i, kind, step), device_id=to, device_id_type=MESH
-        )
-        copy.start()
-        started.append(copy)
-
-    def arrived(i, kind, step, dst):
-        pltpu.make_async_remote_copy(
-            dst, dst, *sems(i, kind, step), device_id=to_c, device_id_type=MESH
-        ).wait_recv()
-
-    loads = {}
-    for s in order:
-        for i in range(n_all):
-            acc, sib = per_all[i][:2]
-            send(i, "s", s, ins[i].at[goal[s], :, :, oc], sib.at[s], to_c)
-            load = pltpu.make_async_copy(
-                ins[i].at[goal[s], :, :, c], acc.at[s], local_sem.at[i, s]
-            )
-            load.start()
-            loads[i, s] = load
-    group_copies, group_loads = [], []
-    for g in range(n_group):
-        acc, sib, far = per_group[g]
-        src = ins[n_all + g]
-        copy = pltpu.make_async_remote_copy(
-            src.at[:, oc], sib, group_send.at[g, 0], group_recv.at[g, 0],
-            device_id=to_c, device_id_type=MESH,
-        )
-        copy.start()
-        group_copies.append(copy)
-        load = pltpu.make_async_copy(src.at[:, c], acc, local_sem.at[n_all + g, 0])
-        load.start()
-        group_loads.append(load)
-    for s in order:
-        for i in range(n_all):
-            acc, sib, p, q, x, y, line = per_all[i]
-            rows, cols = acc.shape[-2:]
-            first, second = halves((rows, cols))
-            loads[i, s].wait()
-            arrived(i, "s", s, sib.at[s])
-            for u, v in ((oa, ob), (a, ob), (oa, b), (a, b)):
-                add_into(acc, sib, rows, 0, cols, (s, u, v), (s, u, v))
-                if (u is oa) and (v is ob):
-                    send(i, "p", s, acc.at[(s, oa, ob) + first], p.at[s], to_a)
-                    send(i, "q", s, acc.at[(s, oa, ob) + second], q.at[s], to_b)
-    for g in range(n_group):
-        acc, sib, far = per_group[g]
-        rows, cols = acc.shape[-2:]
-        group_loads[g].wait()
-        pltpu.make_async_remote_copy(
-            sib, sib, group_send.at[g, 0], group_recv.at[g, 0], device_id=to_c, device_id_type=MESH
-        ).wait_recv()
-        for u in (ob, b):
-            add_into(acc, sib, rows, 0, cols, (u,), (u,))
-            if u is ob:
-                copy = pltpu.make_async_remote_copy(
-                    acc.at[ob], far, group_send.at[g, 1], group_recv.at[g, 1],
-                    device_id=to_b, device_id_type=MESH,
-                )
-                copy.start()
-                group_copies.append(copy)
-    for s in order:
-        for i in range(n_all):
-            acc, sib, p, q, x, y, line = per_all[i]
-            rows, cols = acc.shape[-2:]
-            arrived(i, "p", s, p.at[s])
-            add_into(acc, p, rows, 0, cols // 2, (s, a, ob), (s,))
-            send(i, "x", s, acc.at[s, a, ob], x.at[s], to_b)
-            arrived(i, "q", s, q.at[s])
-            add_into(acc, q, rows, cols // 2, cols // 2, (s, oa, b), (s,))
-            send(i, "y", s, acc.at[s, oa, b], y.at[s], to_a)
-    for s in order:
-        for i in range(n_all):
-            acc, sib, p, q, x, y, line = per_all[i]
-            rows, cols = acc.shape[-2:]
-            arrived(i, "x", s, x.at[s])
-            add_into(acc, x, rows, 0, cols, (s, a, b), (s,))
-            arrived(i, "y", s, y.at[s])
-            add_into(acc, y, rows, 0, cols, (s, a, b), (s,))
-            if s > 0:
-                send(i, "z", s, acc.at[s, a, b], line.at[s - 1], to_line[s])
-    for g in range(n_group):
-        acc, sib, far = per_group[g]
-        pltpu.make_async_remote_copy(
-            far, far, group_send.at[g, 1], group_recv.at[g, 1], device_id=to_b, device_id_type=MESH
-        ).wait_recv()
-        outs[n_all + g][...] = acc[b].astype(f32) + far[...].astype(f32)
-    for i in range(n_all):
-        acc, sib, p, q, x, y, line = per_all[i]
-        for s in range(1, lines):
-            arrived(i, "z", s, line.at[s - 1])
-        total = acc[0, a, b].astype(f32)
-        for s in range(1, lines):
-            total = total + line[s - 1].astype(f32)
-        outs[i][...] = total
-    for copy in started + group_copies:
-        copy.wait_send()
-
-
-def reduce_scatter(everyone, group, collective_id, name):
-    eps, tps = lax.axis_size("ep"), lax.axis_size("tp")
-    lines = eps // 2
-    n_all, n_group = len(everyone), len(group)
+    keep.wait()
+    save.wait()
+
+
+def front_call(lengths, ids, hidden, small, wq, wk, wv, wo, cot, experts, scale, collective_id):
+    lines = lax.axis_size("ep") // 2
+    count, width = hidden.shape
+    d_rows = wq.shape[0]
+    group_len = 4 * count
     anywhere = pl.BlockSpec(memory_space=pl.ANY)
     vmem = pl.BlockSpec(memory_space=pltpu.VMEM)
-    scratch = []
-    for v in everyone:
-        rows, cols = v.shape[1:]
-        scratch += [
-            pltpu.VMEM((lines, 2, 2, rows, cols), bf16),
-            pltpu.VMEM((lines, 2, 2, rows, cols), bf16),
-            pltpu.VMEM((lines, rows, cols // 2), bf16),
-            pltpu.VMEM((lines, rows, cols // 2), bf16),
-            pltpu.VMEM((lines, rows, cols), bf16),
-            pltpu.VMEM((lines, rows, cols), bf16),
-            pltpu.VMEM((lines - 1, rows, cols), bf16),
-        ]
-    for v in group:
-        rows, cols = v.shape[1:]
-        scratch += [
-            pltpu.VMEM((2, rows, cols), bf16),
-            pltpu.VMEM((2, rows, cols), bf16),
-            pltpu.VMEM((rows, cols), bf16),
-        ]
-    scratch += [
-        pltpu.SemaphoreType.DMA((n_all, 6 * lines)),
-        pltpu.SemaphoreType.DMA((n_all, 6 * lines)),
-        pltpu.SemaphoreType.DMA((max(n_group, 1), 2)),
-        pltpu.SemaphoreType.DMA((max(n_group, 1), 2)),
-        pltpu.SemaphoreType.DMA((n_all + n_group, lines)),
-    ]
-    outs = pl.pallas_call(
-        functools.partial(reduce_kernel, lines, n_all, n_group),
-        out_shape=[jax.ShapeDtypeStruct(v.shape[1:], f32) for v in list(everyone) + list(group)],
-        in_specs=[anywhere] * (n_all + n_group),
-        out_specs=[vmem] * (n_all + n_group),
-        scratch_shapes=scratch,
+    smem = pl.BlockSpec(memory_space=pltpu.SMEM)
+    lane = jnp.arange(128) % 64
+    freq = (10000.0 ** (-2.0 * lane.astype(f32) / 128))[None, :]
+    shape = jax.ShapeDtypeStruct
+    return pl.pallas_call(
+        functools.partial(front_kernel, lines, experts, scale),
+        out_shape=(
+            shape((width, 4 * width), bf16),
+            shape((lines * 4 * count, width), bf16),
+            shape((count, width), bf16),
+            shape((2 * experts, count), bf16),
+            shape((128, width), bf16),
+            shape((count, width), f32),
+            shape((count, width), bf16),
+            shape((count, width), bf16),
+            shape((group_len, width), bf16),
+            shape((group_len, width), bf16),
+            shape((group_len, width), bf16),
+            shape((group_len, 128), f32),
+            shape((group_len, 128), f32),
+            shape((4, count, width), bf16),
+        ),
+        in_specs=[smem] + [vmem] * 8 + [anywhere],
+        out_specs=(anywhere, anywhere) + (vmem,) * 12,
+        scratch_shapes=[
+            pltpu.VMEM((width, 4 * width), bf16),
+            pltpu.VMEM((4, d_rows, width // 2), bf16),
+            pltpu.VMEM((d_rows, 128), bf16),
+            pltpu.VMEM((width, 128), bf16),
+            pltpu.VMEM((count, group_len), f32),
+            pltpu.SemaphoreType.DMA((4, 11 * lines)),
+            pltpu.SemaphoreType.DMA((4, 11 * lines)),
+            pltpu.SemaphoreType.DMA((5,)),
+            pltpu.SemaphoreType.DMA((5,)),
+            pltpu.SemaphoreType.DMA((3,)),
+            pltpu.SemaphoreType.DMA((3,)),
+            pltpu.SemaphoreType.DMA((2,)),
+        ],
         compiler_params=pltpu.CompilerParams(
-            collective_id=collective_id, has_side_effects=True, vmem_limit_bytes=VMEM_BUDGET
+            collective_id=collective_id, has_side_effects=True, vmem_limit_bytes=60 * 2**20
         ),
-        name=name,
-    )(
-        *[v.reshape((lines, 2, 2, 2) + v.shape[1:]) for v in everyone],
-        *[v.reshape((2, 2) + v.shape[1:]) for v in group],
-    )
-    return outs[:n_all], outs[n_all:]
+        name="front",
+    )(lengths, ids, freq, hidden, small, wq, wk, wv, wo, cot)
 
 
 def mixture_kernel(lines, tok, aux, cot, wg, wu, wd, sel, sel_t, router_t, ones, *refs):
@@ -891,6 +922,398 @@
     )(tok, aux, cot, *weights, sel, sel_t, router_t, ones)
 
 
+class Reduce:
+    def __init__(self, ways, chunk, cut, pq, xr, yr, zr, sems):
+        self.ways, self.chunk, self.cut = ways, chunk, cut
+        self.pq, self.xr, self.yr, self.zr = pq, xr, yr, zr
+        self.send_sem, self.recv_sem = sems
+
+    def copy(self, slot, u, src, dst, to):
+        k = slot * self.ways.lines + u
+        return remote(src, dst, self.send_sem(k), self.recv_sem(k), to)
+
+    def diag(self, part, u):
+        w = self.ways
+        return self.copy(
+            part, u, self.chunk(w.zs[u], D, part), self.cut(self.pq, u, part),
+            w.to_b if part else w.to_a,
+        )
+
+    def side_b(self, part, u):
+        w = self.ways
+        return self.copy(2 + part, u, self.chunk(w.zs[u], X, part), self.cut(self.xr, u, part), w.to_b)
+
+    def side_a(self, part, u):
+        w = self.ways
+        return self.copy(4 + part, u, self.chunk(w.zs[u], Y, part), self.cut(self.yr, u, part), w.to_a)
+
+    def along(self, u):
+        w = self.ways
+        z, a, b, c = w.spot
+        slot = lax.rem(z - w.zs[u] + w.lines, w.lines) - 1
+        k = 6 * w.lines
+        return remote(
+            self.chunk(w.zs[u], O, None), self.zr(slot), self.send_sem(k + u),
+            self.recv_sem(k + slot), device(w.zs[u], a, b, c),
+        )
+
+    def start(self, u):
+        self.diag(0, u).start()
+        self.diag(1, u).start()
+        self.side_b(1, u).start()
+        self.side_a(0, u).start()
+
+    def mid(self, u):
+        w = self.ways
+        self.diag(0, u).wait_recv()
+        accumulate(self.chunk(w.zs[u], X, 0), [self.cut(self.pq, u, 0)])
+        self.side_b(0, u).start()
+        self.diag(1, u).wait_recv()
+        accumulate(self.chunk(w.zs[u], Y, 1), [self.cut(self.pq, u, 1)])
+        self.side_a(1, u).start()
+
+    def end(self, u):
+        w = self.ways
+        for part in (0, 1):
+            self.side_b(part, u).wait_recv()
+            self.side_a(part, u).wait_recv()
+            accumulate(
+                self.chunk(w.zs[u], O, part), [self.cut(self.xr, u, part), self.cut(self.yr, u, part)]
+            )
+        if u > 0:
+            self.along(u).start()
+
+    def events(self):
+        lines = self.ways.lines
+        order = list(range(1, lines)) + [0]
+        out = []
+        for k in range(lines + 2):
+            if k < lines:
+                out.append(lambda k=k: self.start(order[k]))
+            if 1 <= k <= lines:
+                out.append(lambda k=k: self.mid(order[k - 1]))
+            if k >= 2:
+                out.append(lambda k=k: self.end(order[k - 2]))
+        return out
+
+    def total(self):
+        w = self.ways
+        sums = self.chunk(w.spot[0], O, None)[...].astype(f32)
+        for slot in range(w.lines - 1):
+            k = 6 * w.lines + slot
+            here = self.zr(slot)
+            remote(here, here, self.send_sem(k), self.recv_sem(k), w.to_c).wait_recv()
+            sums = sums + here[...].astype(f32)
+        return sums
+
+    def drain(self):
+        for u in range(self.ways.lines):
+            for part in (0, 1):
+                self.diag(part, u).wait_send()
+                self.side_b(part, u).wait_send()
+                self.side_a(part, u).wait_send()
+            if u > 0:
+                self.along(u).wait_send()
+
+
+def accumulate(dst, others):
+    total = dst[...].astype(f32)
+    for ref in others:
+        total = total + ref[...].astype(f32)
+    dst[...] = total.astype(bf16)
+
+
+def back_kernel(lines, experts, scale, *refs):
+    (
+        lengths, sums, residual, cot, group, small_t, router_part, attended, q, keys, vals, normed,
+        cosine, sine, wall_in,
+        layer_out, input_grad, gq, gk, gv, go, small_out,
+        wall, part, landed, pq, xr, yr, zr, fin, fin_other,
+        s_part, s_landed, s_pq, s_xr, s_yr, s_zr,
+        grads, low, datt, dq, dk, dv, dn_part, dn_other, dn_far, bias, rows_t,
+        c_send, c_recv, r_send, r_recv, d_send, d_recv, local_sem,
+    ) = refs
+    ways = Ways(lines)
+    z, a, b, c = ways.spot
+    ob, oc = 1 - b, 1 - c
+    count, width = cot.shape
+    half = width // 2
+    heads = width // 128
+    chip_rows = pq.shape[2]
+    d_rows = chip_rows // 2
+    load = pltpu.make_async_copy(wall_in, wall, local_sem.at[0])
+    load.start()
+    ways.greet()
+
+    res = residual[...]
+    r2 = lax.rsqrt(jnp.mean(res * res, axis=-1, keepdims=True) + epsilon)
+    unit_two = res * r2
+    dn2 = sums[:, width : 2 * width]
+    gain_two = small_t[experts + 1 : experts + 2, :].astype(f32)
+    gain_one = small_t[experts : experts + 1, :].astype(f32)
+    rows_t[...] = router_part[...]
+    rows_t[experts + 1 : experts + 2, :] = jnp.sum(dn2 * unit_two, axis=0, keepdims=True)
+    scaled = dn2 * gain_two
+    back = r2 * (scaled - unit_two * jnp.mean(scaled * unit_two, axis=-1, keepdims=True))
+    grads[...] = cot[...].astype(f32) + back
+    low[...] = grads[...].astype(bf16)
+    layer_out[...] = (res + sums[:, 0:width]).astype(bf16)
+    make_bias(bias, lengths, b * 2 + c)
+
+    cuts = [half // 256 * 128, (half // 128 - half // 256) * 128] * 2
+
+    def weight_reduce(k):
+        def span(p):
+            return (0, half) if p is None else ((0, cuts[k]) if p == 0 else (cuts[k], half - cuts[k]))
+
+        def chunk(line, kind, p):
+            start, size = span(p)
+            rows = pl.multiple_of(ways.chip(line, kind) * chip_rows, 16)
+            first = pl.multiple_of((c * 4 + k) * half + start, 128)
+            return part.at[pl.ds(rows, chip_rows), pl.ds(first, size)]
+
+        def cut(ref, u, p):
+            start, size = span(p)
+            return ref.at[k, u, :, pl.ds(start, size)]
+
+        return Reduce(
+            ways, chunk, cut, pq, xr, yr, lambda slot: zr.at[k, slot],
+            (lambda i: r_send.at[k, i], lambda i: r_recv.at[k, i]),
+        )
+
+    def small_span(p):
+        first = chip_rows // 32 * 16
+        return (0, chip_rows) if p is None else ((0, first) if p == 0 else (first, chip_rows - first))
+
+    def small_chunk(line, kind, p):
+        start, size = small_span(p)
+        return s_part.at[pl.ds(pl.multiple_of(ways.chip(line, kind) * chip_rows + start, 16), size)]
+
+    def small_cut(ref, u, p):
+        start, size = small_span(p)
+        return ref.at[u, pl.ds(start, size)]
+
+    small_reduce = Reduce(
+        ways, small_chunk, small_cut, s_pq, s_xr, s_yr, lambda slot: s_zr.at[slot],
+        (lambda i: r_send.at[4, i], lambda i: r_recv.at[4, i]),
+    )
+    reduces = [weight_reduce(k) for k in range(4)]
+
+    def across(k):
+        cols = pl.ds(pl.multiple_of((oc * 4 + k) * half, 128), half)
+        return remote(part.at[:, cols], landed.at[k], c_send.at[k], c_recv.at[k], ways.to_c)
+
+    def own_cols(k):
+        return pl.ds(pl.multiple_of((c * 4 + k) * half, 128), half)
+
+    def swapped(k):
+        across(k).wait_recv()
+
+        def body(i, carry):
+            rows = pl.ds(pl.multiple_of(i * chip_rows, 16), chip_rows)
+            accumulate(part.at[rows, own_cols(k)], [landed.at[k, rows]])
+            return carry
+
+        lax.fori_loop(0, width // chip_rows, body, 0)
+
+    later = []
+
+    def service(n=1):
+        for _ in range(n):
+            if later:
+                later.pop(0)()
+
+    def weight_grad(k, left, right):
+        for h in range(2):
+            cols = pl.ds((h * 4 + k) * half, half)
+            part[:, cols] = dot_tn(left, right[:, h * half : (h + 1) * half]).astype(bf16)
+        across(k).start()
+        later.append(lambda: swapped(k))
+        later.extend(reduces[k].events())
+
+    weight_grad(3, attended[...], low)
+    load.wait()
+    datt[...] = (
+        dot_nt(low[:, 0:half], wall[:, pl.ds(3 * half, half)])
+        + dot_nt(low[:, half:width], wall[:, pl.ds(7 * half, half)])
+    ).astype(bf16)
+    service()
+
+    own_rows = pl.ds(pl.multiple_of((b * 2 + c) * count, count), count)
+    for h in range(heads):
+        cols = pl.ds(h * 128, 128)
+        probs = softmax_rows(dot_nt(q[:, cols], keys[:, cols]) * scale + bias[...])
+        dprobs = dot_nt(datt[:, cols], vals[:, cols])
+        dscores = (
+            probs * (dprobs - jnp.sum(probs * dprobs, axis=-1, keepdims=True))
+        ).astype(bf16)
+        dq[:, cols] = turn(
+            dense_dot(dscores, keys[:, cols]) * scale, cosine[own_rows, :], -sine[own_rows, :]
+        ).astype(bf16)
+        dk[:, cols] = turn(dot_tn(dscores, q[:, cols]) * scale, cosine[...], -sine[...]).astype(bf16)
+        dv[:, cols] = dot_tn(probs.astype(bf16), datt[:, cols]).astype(bf16)
+        service()
+    weight_grad(2, normed[...], dv)
+    service(2)
+    weight_grad(1, normed[...], dk)
+    service(2)
+    weight_grad(0, normed[own_rows, :], dq)
+    service(2)
+
+    for t in range(4):
+        rows = slice(t * count, (t + 1) * count)
+        total = jnp.zeros((count, width), f32)
+        for h in range(2):
+            mine = slice(h * half, (h + 1) * half)
+            total = total + dot_nt(dk[rows, mine], wall[:, pl.ds((h * 4 + 1) * half, half)])
+            total = total + dot_nt(dv[rows, mine], wall[:, pl.ds((h * 4 + 2) * half, half)])
+        dn_part[t] = total.astype(bf16)
+        x = group[t].astype(f32)
+        unit = x * lax.rsqrt(jnp.mean(x * x, axis=-1, keepdims=True) + epsilon)
+        gain_row = jnp.sum(total * unit, axis=0, keepdims=True)
+        if t == 0:
+            rows_t[experts : experts + 1, :] = gain_row
+        else:
+            rows_t[experts : experts + 1, :] += gain_row
+        service()
+
+    def dn_copy(k, src, dst, to):
+        return remote(src, dst, d_send.at[k], d_recv.at[k], to)
+
+    dn_copies = [
+        dn_copy(0, dn_part.at[b * 2 + oc], dn_other.at[0], ways.to_c),
+        dn_copy(1, dn_part.at[ob * 2 + oc], dn_other.at[1], ways.to_c),
+    ]
+    for copy in dn_copies:
+        copy.start()
+    own = jnp.zeros((count, width), f32)
+    for h in range(2):
+        own = own + dot_nt(dq[:, h * half : (h + 1) * half], wall[:, pl.ds(h * 4 * half, half)])
+    x = group[b * 2 + c].astype(f32)
+    r1 = lax.rsqrt(jnp.mean(x * x, axis=-1, keepdims=True) + epsilon)
+    unit_one = x * r1
+    rows_t[experts : experts + 1, :] += jnp.sum(own * unit_one, axis=0, keepdims=True)
+    s_part[...] = jnp.transpose(rows_t[...]).astype(bf16)
+    small_swap = remote(s_part, s_landed, c_send.at[4], c_recv.at[4], ways.to_c)
+    small_swap.start()
+    service()
+    dn_copies[1].wait_recv()
+    accumulate(dn_part.at[ob * 2 + c], [dn_other.at[1]])
+    dn_copies.append(dn_copy(2, dn_part.at[ob * 2 + c], dn_far, ways.to_b))
+    dn_copies[2].start()
+    dn_copies[0].wait_recv()
+    small_swap.wait()
+    accumulate(s_part, [s_landed])
+    later.extend(small_reduce.events())
+    service(2)
+    dn_copies[2].wait_recv()
+    total = (
+        own
+        + dn_part[b * 2 + c].astype(f32)
+        + dn_other[0].astype(f32)
+        + dn_far[...].astype(f32)
+    )
+    scaled = total * gain_one
+    input_grad[...] = grads[...] + r1 * (
+        scaled - unit_one * jnp.mean(scaled * unit_one, axis=-1, keepdims=True)
+    )
+    service(len(later))
+
+    theirs = pl.ds(pl.multiple_of(oc * d_rows, 8), d_rows)
+    mine = pl.ds(pl.multiple_of(c * d_rows, 8), d_rows)
+    fin_copies = []
+    for k in (3, 2, 1, 0):
+        fin[k] = reduces[k].total()
+        copy = remote(fin.at[k, theirs], fin_other.at[k], c_send.at[5 + k], c_recv.at[5 + k], ways.to_c)
+        copy.start()
+        fin_copies.append(copy)
+    s_total = small_reduce.total()
+    small_out[...] = jnp.where(c == 0, s_total[:d_rows], s_total[d_rows:])
+    for k, copy in zip((3, 2, 1, 0), fin_copies):
+        copy.wait_recv()
+        out = (gq, gk, gv, go)[k]
+        out[:, pl.ds(pl.multiple_of(c * half, 128), half)] = fin[k, mine, :]
+        out[:, pl.ds(pl.multiple_of(oc * half, 128), half)] = fin_other[k]
+    for r in reduces + [small_reduce]:
+        r.drain()
+    for copy in dn_copies + fin_copies:
+        copy.wait_send()
+    for k in range(4):
+        across(k).wait_send()
+
+
+def back_call(
+    lengths, sums, residual, cot, group, small_t, router_part, attended, q, keys, vals, normed,
+    cosine, sine, wall, d_rows, experts, scale, collective_id,
+):
+    lines = lax.axis_size("ep") // 2
+    count, width = cot.shape
+    half = width // 2
+    chip_rows = 2 * d_rows
+    group_len = 4 * count
+    anywhere = pl.BlockSpec(memory_space=pl.ANY)
+    vmem = pl.BlockSpec(memory_space=pltpu.VMEM)
+    smem = pl.BlockSpec(memory_space=pltpu.SMEM)
+    shape = jax.ShapeDtypeStruct
+    dma = pltpu.SemaphoreType.DMA
+    return pl.pallas_call(
+        functools.partial(back_kernel, lines, experts, scale),
+        out_shape=(
+            shape((count, width), bf16),
+            shape((count, width), f32),
+            shape((d_rows, width), f32),
+            shape((d_rows, width), f32),
+            shape((d_rows, width), f32),
+            shape((d_rows, width), f32),
+            shape((d_rows, 128), f32),
+        ),
+        in_specs=[smem] + [vmem] * 13 + [anywhere],
+        out_specs=(vmem,) * 7,
+        scratch_shapes=[
+            pltpu.VMEM(wall.shape, bf16),
+            pltpu.VMEM(wall.shape, bf16),
+            pltpu.VMEM((4, width, half), bf16),
+            pltpu.VMEM((4, lines, chip_rows, half), bf16),
+            pltpu.VMEM((4, lines, chip_rows, half), bf16),
+            pltpu.VMEM((4, lines, chip_rows, half), bf16),
+            pltpu.VMEM((4, lines - 1, chip_rows, half), bf16),
+            pltpu.VMEM((4, chip_rows, half), f32),
+            pltpu.VMEM((4, d_rows, half), f32),
+            pltpu.VMEM((width, 128), bf16),
+            pltpu.VMEM((width, 128), bf16),
+            pltpu.VMEM((lines, chip_rows, 128), bf16),
+            pltpu.VMEM((lines, chip_rows, 128), bf16),
+            pltpu.VMEM((lines, chip_rows, 128), bf16),
+            pltpu.VMEM((lines - 1, chip_rows, 128), bf16),
+            pltpu.VMEM((count, width), f32),
+            pltpu.VMEM((count, width), bf16),
+            pltpu.VMEM((count, width), bf16),
+            pltpu.VMEM((count, width), bf16),
+            pltpu.VMEM((group_len, width), bf16),
+            pltpu.VMEM((group_len, width), bf16),
+            pltpu.VMEM((4, count, width), bf16),
+            pltpu.VMEM((2, count, width), bf16),
+            pltpu.VMEM((count, width), bf16),
+            pltpu.VMEM((count, group_len), f32),
+            pltpu.VMEM((128, width), f32),
+            dma((9,)),
+            dma((9,)),
+            dma((5, 7 * lines)),
+            dma((5, 7 * lines)),
+            dma((3,)),
+            dma((3,)),
+            dma((1,)),
+        ],
+        compiler_params=pltpu.CompilerParams(
+            collective_id=collective_id, has_side_effects=True, vmem_limit_bytes=62 * 2**20
+        ),
+        name="back",
+    )(
+        lengths, sums, residual, cot, group, small_t, router_part, attended, q, keys, vals, normed,
+        cosine, sine, wall,
+    )
+
+
 def documents(positions, lengths):
     seq_ends = jnp.cumsum(lengths)
     doc_index = (positions >= seq_ends[0]).astype(jnp.int32) + (positions >= seq_ends[1]).astype(
@@ -941,7 +1364,7 @@
     return dot(left, right, ((0,), (0,)))
 
 
-def on_device(
+def any_slice(
     hidden_in,
     seq_lengths,
     expert_ids,
@@ -979,16 +1402,10 @@
     small = jnp.pad(small, ((0, -small.shape[0] % 16), (0, 0)))
     weights = jnp.concatenate([w_query, w_key, w_value, w_out], axis=1)
 
-    small_slice = eps == 8 and tps == 4
-    if small_slice:
-        (all_weights, all_small, all_cot), (group_hidden,) = gather(
-            [weights, small, cotangent], [False, False, True], [hidden_in], 0, "gather_weights"
-        )
-    else:
-        all_weights, all_small, all_cot = [
-            lax.all_gather(v, AXES, axis=0) for v in (weights, small, cotangent)
-        ]
-        group_hidden = lax.all_gather(hidden_in, "tp", axis=0)
+    all_weights, all_small, all_cot = [
+        lax.all_gather(v, AXES, axis=0) for v in (weights, small, cotangent)
+    ]
+    group_hidden = lax.all_gather(hidden_in, "tp", axis=0)
     all_weights = all_weights.reshape(devices * d_rows, 4 * width)
     full_query = all_weights[:, :width]
     full_key = all_weights[:, width : 2 * width]
@@ -1110,61 +1527,30 @@
         )
         return out_part, dn2_part, sums
 
-    if small_slice:
-        lanes = 128
-        h_core = -(-hidden // lanes) * lanes
-        pad = ((0, h_core - hidden), (0, 0))
-        signed_high = lax.reduce_precision(signed, 8, 7)
-        aux = jnp.concatenate([signed_high.T, (signed - signed_high).T]).astype(bf16)
-        owner = jnp.arange(h_core, dtype=jnp.int32)
-        owner = jnp.where(owner < n_routed, first_expert + owner // exp_hidden, experts)
-        owner = jnp.concatenate([owner, owner])
-        sel_t = (owner[:, None] == jnp.arange(lanes, dtype=jnp.int32)[None, :]).astype(bf16)
-        sel = jnp.concatenate([sel_t[:, :experts].T, jnp.eye(experts, lanes, dtype=bf16)], axis=1)
-        sel = jnp.concatenate([sel, sel])
-        ones = (jnp.arange(2 * h_core, dtype=jnp.int32) % h_core)[None, :]
-        ones = ((ones >= n_routed) & (ones < hidden)).astype(f32)
-        router_t = jnp.pad(full_router.T, ((0, lanes - experts), (0, 0)))
-        token_sums, grads_here, grads_there, router_sum = mixture_call(
-            normed_two,
-            aux,
-            cot_all,
-            [jnp.pad(w, pad) for w in (gate_w, up_w, down_w)],
-            sel,
-            sel_t,
-            router_t,
-            ones,
-            2,
-        )
-        routed_sum, grad_normed_two = token_sums[:, :model_width], token_sums[:, model_width:]
-        grads = grads_here + grads_there
-        grad_gate, grad_up, grad_down = [grads[k, :hidden] for k in range(3)]
-        router_part = router_sum[:experts].T
-    else:
-        rows, signed_all = [lax.all_gather(v, AXES, axis=0, tiled=True) for v in (normed_two, signed)]
-        blocks = max(1, tokens * hidden * 4 // 2**23)
-        while tokens % blocks:
-            blocks += 1
-
-        def step(totals, block):
-            out_block, dn2_block, sums = mixture(*block)
-            return jax.tree.map(jnp.add, totals, sums), (out_block, dn2_block)
-
-        zeros = (jnp.zeros((hidden, model_width), f32),) * 3 + (
-            jnp.zeros((model_width, experts), f32),
-        )
-        sums, (out_part, dn2_part) = lax.scan(
-            step,
-            zeros,
-            jax.tree.map(
-                lambda v: v.reshape((blocks, -1) + v.shape[1:]), (rows, cot_all, signed_all)
-            ),
-        )
-        grad_down, grad_gate, grad_up, router_part = sums
-        routed_sum, grad_normed_two = [
-            lax.psum_scatter(v.reshape(tokens, model_width), AXES, tiled=True).astype(f32)
-            for v in (out_part, dn2_part)
-        ]
+    rows, signed_all = [lax.all_gather(v, AXES, axis=0, tiled=True) for v in (normed_two, signed)]
+    blocks = max(1, tokens * hidden * 4 // 2**23)
+    while tokens % blocks:
+        blocks += 1
+
+    def step(totals, block):
+        out_block, dn2_block, sums = mixture(*block)
+        return jax.tree.map(jnp.add, totals, sums), (out_block, dn2_block)
+
+    zeros = (jnp.zeros((hidden, model_width), f32),) * 3 + (
+        jnp.zeros((model_width, experts), f32),
+    )
+    sums, (out_part, dn2_part) = lax.scan(
+        step,
+        zeros,
+        jax.tree.map(
+            lambda v: v.reshape((blocks, -1) + v.shape[1:]), (rows, cot_all, signed_all)
+        ),
+    )
+    grad_down, grad_gate, grad_up, router_part = sums
+    routed_sum, grad_normed_two = [
+        lax.psum_scatter(v.reshape(tokens, model_width), AXES, tiled=True).astype(f32)
+        for v in (out_part, dn2_part)
+    ]
     layer_output = (residual + routed_sum).astype(bf16)
 
     gain_two_part = jnp.sum(grad_normed_two * unit_two, axis=0)
@@ -1212,15 +1598,10 @@
     small_part = jnp.pad(small_part, ((0, 0), (0, -small_part.shape[1] % 16), (0, 0))).astype(bf16)
     weight_part = weight_part.reshape(devices, d_rows, 4 * width)
     group_part = group_normed_grad.astype(bf16).reshape(tps, tok_count, model_width)
-    if small_slice:
-        (weight_sum, small_sum), (normed_grad_sum,) = reduce_scatter(
-            [weight_part, small_part], [group_part], 3, "reduce_weights"
-        )
-    else:
-        weight_sum, small_sum = [
-            lax.psum_scatter(v, AXES).astype(f32) for v in (weight_part, small_part)
-        ]
-        normed_grad_sum = lax.psum_scatter(group_part, "tp").astype(f32)
+    weight_sum, small_sum = [
+        lax.psum_scatter(v, AXES).astype(f32) for v in (weight_part, small_part)
+    ]
+    normed_grad_sum = lax.psum_scatter(group_part, "tp").astype(f32)
     grad_normed = own_normed_grad + normed_grad_sum
     input_grad = grad_resid + norm_back(grad_normed, unit_one, inverse_one, gain_one)
     small_sum = small_sum.reshape(-1)
@@ -1249,12 +1630,121 @@
     )
 
 
+def small_slice(
+    hidden_in,
+    seq_lengths,
+    expert_ids,
+    attn_gain,
+    w_query,
+    w_key,
+    w_value,
+    w_out,
+    ffn_gain,
+    shared_gate,
+    shared_up,
+    shared_down,
+    router,
+    expert_gate,
+    expert_up,
+    expert_down,
+    cotangent,
+):
+    tok_count, model_width = hidden_in.shape
+    eps, tps = lax.axis_size("ep"), lax.axis_size("tp")
+    devices = eps * tps
+    exp_local, exp_hidden = expert_gate.shape[:2]
+    experts = exp_local * eps
+    group_len = tps * tok_count
+    tokens = devices * tok_count
+    d_rows = w_query.shape[0]
+    width = w_query.shape[1]
+    sh_rows = shared_down.shape[0]
+    head_dim = width // HEADS
+    attn_scale = head_dim ** (-0.5)
+
+    lanes = 128
+    vectors = jnp.stack([attn_gain, ffn_gain], axis=1)
+    small = jnp.concatenate([router, vectors], axis=1)
+    small = jnp.pad(small, ((0, 0), (0, lanes - small.shape[1])))
+    (
+        w_all, cot_all, normed_two, aux, small_t, residual, attended, queries, key_rows, value_rows,
+        group_normed, cos_all, sin_all, group_hidden,
+    ) = front_call(
+        seq_lengths, expert_ids, hidden_in, small, w_query, w_key, w_value, w_out, cotangent,
+        experts, attn_scale, 0,
+    )
+    shared_cols = jnp.stack([shared_gate, shared_up], axis=1).reshape(d_rows, 2, devices, sh_rows)
+    shared_cols = lax.all_to_all(
+        shared_cols.transpose(2, 1, 3, 0), AXES, split_axis=0, concat_axis=0, tiled=True
+    )
+    shared_t = shared_cols.transpose(1, 2, 0, 3).reshape(2, sh_rows, model_width)
+
+    first_expert = lax.axis_index("ep") * exp_local
+    n_routed = exp_local * exp_hidden
+    hidden = n_routed + sh_rows
+    gate_w = jnp.concatenate([expert_gate.reshape(n_routed, model_width), shared_t[0]])
+    up_w = jnp.concatenate([expert_up.reshape(n_routed, model_width), shared_t[1]])
+    down_w = jnp.concatenate([expert_down.reshape(n_routed, model_width), shared_down])
+
+    h_core = -(-hidden // lanes) * lanes
+    pad = ((0, h_core - hidden), (0, 0))
+    owner = jnp.arange(h_core, dtype=jnp.int32)
+    owner = jnp.where(owner < n_routed, first_expert + owner // exp_hidden, experts)
+    owner = jnp.concatenate([owner, owner])
+    sel_t = (owner[:, None] == jnp.arange(lanes, dtype=jnp.int32)[None, :]).astype(bf16)
+    sel = jnp.concatenate([sel_t[:, :experts].T, jnp.eye(experts, lanes, dtype=bf16)], axis=1)
+    sel = jnp.concatenate([sel, sel])
+    ones = (jnp.arange(2 * h_core, dtype=jnp.int32) % h_core)[None, :]
+    ones = ((ones >= n_routed) & (ones < hidden)).astype(f32)
+    token_sums, grads_here, grads_there, router_sum = mixture_call(
+        normed_two,
+        aux,
+        cot_all,
+        [jnp.pad(w, pad) for w in (gate_w, up_w, down_w)],
+        sel,
+        sel_t,
+        small_t,
+        ones,
+        2,
+    )
+    layer_output, input_grad, grad_q, grad_k, grad_v, grad_o, small_sum = back_call(
+        seq_lengths, token_sums, residual, cotangent, group_hidden, small_t, router_sum, attended,
+        queries, key_rows, value_rows, group_normed, cos_all, sin_all, w_all, d_rows, experts,
+        attn_scale, 3,
+    )
+    grad_gate, grad_up, grad_down = [(grads_here[k] + grads_there[k])[:hidden] for k in range(3)]
+
+    shared_back = jnp.stack([grad_gate[n_routed:], grad_up[n_routed:]])
+    shared_back = shared_back.reshape(2, sh_rows, devices, d_rows).transpose(2, 0, 1, 3)
+    shared_back = lax.all_to_all(shared_back, AXES, split_axis=0, concat_axis=0, tiled=True)
+    shared_back = shared_back.transpose(1, 3, 0, 2).reshape(2, d_rows, devices * sh_rows)
+
+    return (
+        layer_output,
+        input_grad,
+        small_sum[:, experts],
+        grad_q,
+        grad_k,
+        grad_v,
+        grad_o,
+        small_sum[:, experts + 1],
+        shared_back[0],
+        shared_back[1],
+        grad_down[n_routed:],
+        small_sum[:, :experts],
+        grad_gate[:n_routed].reshape(expert_gate.shape),
+        grad_up[:n_routed].reshape(expert_up.shape),
+        grad_down[:n_routed].reshape(expert_down.shape),
+    )
+
+
 def solution(mesh):
     rows = P(AXES, None)
     vector = P(AXES)
     experts = P("ep", "tp", None)
+    small = mesh.shape["ep"] == 8 and mesh.shape["tp"] == 4
     return jax.shard_map(
-        on_device,
+        small_slice if small else any_slice,
         mesh=mesh,
         in_specs=(
             rows, P("ep", None), rows, vector, rows, rows, rows, rows, vector,

time: 561 us -> 492 us (0.88); the launches traced: 552 us -> 489 us
  matrix products: 51.6 us -> 0 us
  Pallas kernels: 366 us -> 406 us
  other arithmetic: 53.6 us -> 18.4 us
  local copies, waits for them, and re-layouts: 60.5 us -> 43.6 us
    dot_general x18 -> x0, matrix products: 48.9 us -> none  [the longest x13 39.3 us: dot(): lax.dot_general(left, right, ((contract[0], contract[1]), ((), ())), pref...]
    pallas_call x2, Pallas kernels: 206 us -> 246 us  [the longest x1 133 us: front_call(): pl.pallas_call(functools.partial(front_kernel, lines, experts, scale), ou...]
    concatenate x8 -> x5, other arithmetic: 14.3 us -> 4.13 us  [the longest x1 1.66 us: small_slice(): jnp.concatenate([expert_gate.reshape(n_routed, model_width), shared_t[0]])]
    convert_element_type x12 -> x3, other arithmetic: 9.94 us -> 0.81 us  [the longest x1 0.6 us: small_slice(): ones = ((ones >= n_routed) & (ones < hidden)).astype(f32)]
    dot_general x4 -> x0, local copies, waits for them, and re-layouts: 8.26 us -> none  [dot(): lax.dot_general(left, right, ((contract[0], contract[1]), ((), ())), pref...]
    reduce_sum x6 -> x0, other arithmetic: 6.08 us -> none  [the longest x1 1.94 us: on_device(): gain_two_part = jnp.sum(grad_normed_two * unit_two, axis=0)]
    add x4 -> x1, other arithmetic: 12.8 us -> 8.16 us  [small_slice(): grads_here[k] + grads_there[k]]
    unnamed x128 -> x47, local copies, waits for them, and re-layouts: 18.3 us -> 16.5 us
  transfers between devices with their start and end apart: 2 -> 2, of which waited for: 0 -> 0; matrix products, arithmetic and copies ran while one was open for 20% -> 3% of each run, Pallas kernels for 37% -> 50%
where the time goes in v3:
time: 492 us; the launch traced here: 489 us
  Pallas kernels  406 us (83%)
  local copies, waits for them, and re-layouts  43.6 us (9%)
  starting transfers between devices  20 us (4%)
  other arithmetic  18.4 us (4%)
    pallas_call x1, Pallas kernels, mixture_call(): pl.pallas_call(functools.partial(mixture_kernel, lines), out_shape=(jax.S...  159 us
    pallas_call x1, Pallas kernels, front_call(): pl.pallas_call(functools.partial(front_kernel, lines, experts, scale), ou...  133 us
    pallas_call x1, Pallas kernels, back_call(): pl.pallas_call(functools.partial(back_kernel, lines, experts, scale), out...  113 us
    unnamed x47, local copies, waits for them, and re-layouts  16.5 us
    all_to_all x1, starting transfers between devices, small_slice(): lax.all_to_all(shared_back, AXES, split_axis=0, concat_axis=0, tiled=True)  12.2 us
  transfers between devices with their start and end apart: 2, of which 0 were waited for; matrix products, arithmetic and copies ran while one was open for 3% of the time, Pallas kernels for 50%

profile of v3, /device:TPU:0, one launch (start us, length us, event | category | flops | bytes accessed | tf_op | source)
XLA Modules:
  0.0 488.9 jit_solution(11615617978377477258)
XLA Ops:
  0.6 1.5 stack.26
  2.2 1.5 stack.27
  3.7 0.0 copy-start.13
  3.7 0.0 copy-start.15
  3.8 0.0 copy-start.16
  3.8 0.1 maximum_bitcast_fusion.1
  3.9 0.3 copy.86
  4.2 0.0 copy-start.4
  4.2 1.8 reshape.160
  6.0 7.8 %all-to-all-start = ((bf16[32,2,2240]{2,1,0:T(2,128)(2,1)}), bf16[32,2,2240]{2,1,0:T(2,128)(2,1)S(1)}, u32[]{:S(2)}, u32[]{:S(2)}) async-start(bf16[32,2,2240]{2,1,0:T(2,128)(2,1)} %reshape.160), calls=%async_computation | async-start | bytes 589824 | tf_op jit(solution)/shard_map/all_to_all | solution.py:1677
  13.9 0.6 and_convert_fusion.ones
  14.5 0.1 copy.71
  14.6 0.1 copy.72
  14.7 0.1 copy.73
  14.8 0.2 fusion.9.sel_t
  15.0 0.7 fusion.14.refs_4_
  15.7 0.5 fusion.23.refs_2_
  16.3 0.7 copy.74.refs_1_
  17.0 0.1 copy.78
  17.1 132.8 %front.1 = (bf16[1280,5120]{1,0:T(8,128)(2,1)}, bf16[2048,1280]{1,0:T(8,128)(2,1)}, bf16[128,1280]{1,0:T(8,128)(2,1)}, bf16[32,128]{1,0:T(8,128)(2,1)}, bf16[128...) custom-call(s32[1,3]{1,0:T(1,128)} %refs_0_.3, ...), custom_call_target="tpu_custom_call" | custom-call | tf_op jit(solution)/shard_map/front/pallas_call | solution.py:445
  149.9 0.6 maximum_maximum_fusion.sel
  150.5 1.1 fusion.8.wd
  151.7 1.0 reshape.161
  152.7 0.0 copy-start.3
  152.7 0.1 bitcast_bitcast_fusion.1
  152.8 0.1 fusion.25
  152.8 0.2 copy.83
  153.0 0.2 copy.84
  153.2 0.8 copy-done.2
  153.9 0.3 copy-done.3
  154.3 1.7 fusion.6
  155.9 159.5 %mixture.1 = (f32[128,2560]{1,0:T(8,128)}, f32[3,512,1280]{2,1,0:T(8,128)}, f32[3,512,1280]{2,1,0:T(8,128)}, f32[128,1280]{1,0:T(8,128)}) custom-call(bf16[128,1280]{1,0:T(8,128)(2,1)} %get-tuple-element.40.tok, bf16[32,128]{1,0:T(8,128)(2,1)} %get-tuple-element.41.aux, bf16[2048,1280]{1,0:T(8,128)(2,1)} %get-tuple-element.42.cot, ...), custom_call_target="tpu_custom_call" | custom-call | tf_op jit(solution)/shard_map/mixture/pallas_call | solution.py:883
  315.4 8.2 %slice_add_fusion = (f32[1,512,1280]{2,1,0:T(8,128)}, f32[1,512,1280]{2,1,0:T(8,128)S(1)}, f32[1,512,1280]{2,1,0:T(8,128)S(1)}) fusion(f32[3,512,1280]{2,1,0:T(8,128)} %get-tuple-element.64, f32[3,512,1280]{2,1,0:T(8,128)} %get-tuple-element.63), kind=kLoop, calls=%fused_computation.7 | loop fusion | flops 1966080 | bytes 23592960 | tf_op jit(solution)/shard_map/add | solution.py:1715
  323.6 1.5 copy-done
  325.1 0.7 slice.105
  325.8 1.7 stack.29
  327.5 0.7 slice.106
  328.2 2.6 stack.30
  330.8 2.6 maximum_bitcast_fusion
  333.4 4.0 copy.79
  337.4 3.5 reshape.162
  340.9 12.2 %all-to-all-start.1 = ((f32[32,1,4480]{2,1,0:T(1,128)}), f32[32,1,4480]{2,1,0:T(1,128)S(1)}, u32[]{:S(2)}, u32[]{:S(2)}) async-start(f32[32,1,4480]{2,1,0:T(1,128)} %reshape.162), calls=%async_computation.1 | async-start | bytes 1146880 | tf_op jit(solution)/shard_map/all_to_all | solution.py:1719
  353.1 3.2 slice.110
  356.3 1.5 slice.111
  357.8 113.4 %back.1 = (bf16[128,1280]{1,0:T(8,128)(2,1)}, f32[128,1280]{1,0:T(8,128)}, f32[40,1280]{1,0:T(8,128)}, f32[40,1280]{1,0:T(8,128)}, f32[40,1280]{1,0:T(8,128)}, /*index=5*/f32[40,1280]{1,0:T(8,128)}, f32[40,128]{1,0:T(8,128)}) custom-call(s32[1,3]{1,0:T(1,128)} %refs_0_.3, f32[128,2560]{1,0:T(8,128)} %get-tuple-element.44.refs_1_, ...), custom_call_target="tpu_custom_call" | custom-call | tf_op jit(solution)/shard_map/back/pallas_call | solution.py:1259
  471.2 1.4 copy.82
  472.6 3.2 slice.112
  475.8 0.7 slice_reduce_fusion
  476.5 1.7 slice_bitcast_fusion
  478.2 0.5 broadcast.137
  478.7 2.0 reduce.4
  480.7 1.0 reshape.163
  481.7 0.1 bitcast_bitcast_fusion
  481.8 0.1 fusion.24
  481.9 0.1 copy.80
  482.1 1.1 squeeze.28
  483.1 0.1 copy.81
  483.3 1.1 squeeze.29
  484.4 0.7 copy.93
  485.1 0.8 copy.94
  485.9 0.7 copy.95
  486.6 0.7 copy.96
  487.3 0.7 copy.97
  488.0 0.7 copy.98
  (32 shorter events, 0.1 us)
Async XLA Ops:
  3.7 10.7 %copy-start.13 = (bf16[40,16]{0,1:T(8,128)(2,1)S(1)}, bf16[40,16]{0,1:T(8,128)(2,1)}, u32[]{:S(2)}) copy-start(bf16[40,16]{0,1:T(8,128)(2,1)} %param.29) | copy-start | bytes 3844
  3.7 10.8 %copy-start.15 = (bf16[40]{0:T(256)(128)(2,1)S(1)}, bf16[40]{0:T(256)(128)(2,1)}, u32[]{:S(2)}) copy-start(bf16[40]{0:T(256)(128)(2,1)} %param.20) | copy-start | bytes 244
  3.8 10.9 %copy-start.16 = (bf16[40]{0:T(256)(128)(2,1)S(1)}, bf16[40]{0:T(256)(128)(2,1)}, u32[]{:S(2)}) copy-start(bf16[40]{0:T(256)(128)(2,1)} %param.25) | copy-start | bytes 244
  3.9 12.3 %copy-start.14 = (s32[128,7]{0,1:T(8,128)S(1)}, s32[128,7]{0,1:T(8,128)}, u32[]{:S(2)}) copy-start(s32[128,7]{0,1:T(8,128)} %param.19) | copy-start | bytes 10756
  4.2 146.3 %copy-start.4 = (bf16[2,224,1280]{2,1,0:T(8,128)(2,1)S(1)}, bf16[2,224,1280]{2,1,0:T(8,128)(2,1)}, u32[]{:S(2)}) copy-start(bf16[2,224,1280]{2,1,0:T(8,128)(2,1)} %param.32) | copy-start | bytes 3440644
  4.2 146.3 %copy-start.12 = (bf16[56,1280]{1,0:T(8,128)(2,1)S(1)}, bf16[56,1280]{1,0:T(8,128)(2,1)}, u32[]{:S(2)}) copy-start(bf16[56,1280]{1,0:T(8,128)(2,1)} %param.28) | copy-start | bytes 430084
  6.0 145.7 %all-to-all-start = ((bf16[32,2,2240]{2,1,0:T(2,128)(2,1)}), bf16[32,2,2240]{2,1,0:T(2,128)(2,1)S(1)}, u32[]{:S(2)}, u32[]{:S(2)}) async-start(bf16[32,2,2240]{2,1,0:T(2,128)(2,1)} %reshape.160), calls=%async_computation | async-start | bytes 589824 | tf_op jit(solution)/shard_map/all_to_all | solution.py:1677
  15.0 136.7 %copy-start.1 = (bf16[1024,128]{1,0:T(8,128)(2,1)}, bf16[1024,128]{1,0:T(8,128)(2,1)S(1)}, u32[]{:S(2)}) copy-start(bf16[1024,128]{1,0:T(8,128)(2,1)S(1)} %fusion.9.sel_t) | copy-start | bytes 786436
  152.7 1.3 copy-start.2
  152.7 1.6 copy-start.3
  323.6 1.5 copy-start
  340.9 137.3 %all-to-all-start.1 = ((f32[32,1,4480]{2,1,0:T(1,128)}), f32[32,1,4480]{2,1,0:T(1,128)S(1)}, u32[]{:S(2)}, u32[]{:S(2)}) async-start(f32[32,1,4480]{2,1,0:T(1,128)} %reshape.162), calls=%async_computation.1 | async-start | bytes 1146880 | tf_op jit(solution)/shard_map/all_to_all | solution.py:1719
  472.6 3.2 copy-start.11
  482.1 2.3 copy-start.6
  482.1 3.0 copy-start.5
  483.1 2.8 copy-start.10
  483.3 3.3 copy-start.9
  483.3 4.0 copy-start.8
  484.4 3.6 copy-start.7

commit v4 on v3

--- a/solution.py
+++ b/solution.py
@@ -42,7 +42,9 @@
 
 
 def visit_order(lines):
-    return [sorted(range(lines), key=lambda other: (abs(other - z), other)) for z in range(lines)]
+    return [
+        sorted(range(lines), key=lambda other: (abs(other - z), other != z ^ 1)) for z in range(lines)
+    ]
 
 
 def lookup(table, index):
@@ -72,6 +74,9 @@
         table = visit_order(lines)
         self.zs = [lookup([table[k][u] for k in range(lines)], z) for u in range(lines)]
         self.column = ((a, b), (a, ob), (oa, b), (oa, ob))
+        self.pair = device(z + 1 - 2 * lax.rem(z, 2), a, b, c)
+        outer = (z == 0) | (z == lines - 1)
+        self.carried = [True, False, outer, jnp.logical_not(outer)]
 
     def greet(self):
         greet([self.to_b, self.to_a, self.to_c] + self.peers)
@@ -79,6 +84,20 @@
     def chip(self, line, kind):
         a, b = self.column[kind]
         return (line * 2 + a) * 2 + b
+
+
+def when(condition, act):
+    if condition is True:
+        act()
+    elif condition is not False:
+
+        @pl.when(condition)
+        def _():
+            act()
+
+
+def other(condition):
+    return not condition if isinstance(condition, bool) else jnp.logical_not(condition)
 
 
 def remote(src, dst, send_sem, recv_sem, to):
@@ -92,7 +111,6 @@
         self.ways, self.chunk, self.own = ways, chunk, own
         self.send_sem, self.recv_sem = sems
         self.relative, self.across_core = relative, across
-        self.sent = []
 
     def copy(self, slot, step, src, dst, to):
         k = slot * self.ways.lines + step
@@ -103,41 +121,63 @@
         dst = self.chunk(line, to_kind if self.relative else kind, part, False)
         return self.copy(slot, step, src, dst, to)
 
-    def send(self, copy):
-        copy.start()
-        self.sent.append(copy)
+    def sends(self, u):
+        w, own = self.ways, u == 0
+        line, carried = w.zs[u], w.carried[u]
+        copies = {
+            "X": (True, lambda: self.hop(0, u, O, X, line, w.to_b, own=own)),
+            "Y": (True, lambda: self.hop(1, u, O, Y, line, w.to_a, own=own)),
+            "p": (carried, lambda: self.hop(2, u, X, D, line, w.to_a, 0)),
+            "q": (carried, lambda: self.hop(3, u, Y, D, line, w.to_b, 1)),
+            "pair": (carried, lambda: self.hop(11, 1 if own else u, D, D, line, w.pair)),
+        }
+        if self.across_core:
+
+            def across(slot, kind):
+                here = self.chunk(line, kind, None, False)
+                src = self.own if kind == O and own and self.own is not None else here
+                return self.copy(slot, u, src, here, w.to_c)
+
+            for kind, slot in ((O, 6), (X, 7), (Y, 8), (D, 9)):
+                copies[kind] = (True, lambda slot=slot, kind=kind: across(slot, kind))
+        return copies
+
+    def send(self, u, *names, condition=True):
+        copies = self.sends(u)
+        for name in names:
+            if name in copies:
+                always, make = copies[name]
+                when(always if condition is True else condition, lambda: make().start())
 
     def arrival(self, slot, step, kind, line, part=None, other=False):
         here = self.chunk(line, kind, part, other)
         self.copy(slot, step, here, here, self.ways.to_c).wait_recv()
 
-    def across(self, slot, u, kind, part=None, own=False):
-        if self.across_core:
-            here = self.chunk(self.ways.zs[u], kind, part, False)
-            src = self.own if own and self.own is not None else here
-            self.send(self.copy(slot, u, src, here, self.ways.to_c))
-
     def send_own(self, u):
-        w, own = self.ways, u == 0
-        self.send(self.hop(0, u, O, X, w.zs[u], w.to_b, own=own))
-        self.send(self.hop(1, u, O, Y, w.zs[u], w.to_a, own=own))
-        self.across(6, u, O, own=own)
+        self.send(u, "X", "Y", O)
 
     def xy_event(self, u):
-        w = self.ways
-        self.arrival(0, u, X, w.zs[u])
-        self.send(self.hop(2, u, X, D, w.zs[u], w.to_a, 0))
-        self.arrival(1, u, Y, w.zs[u])
-        self.send(self.hop(3, u, Y, D, w.zs[u], w.to_b, 1))
-        self.across(7, u, X)
-        self.across(8, u, Y)
-
-    def diag_event(self, u):
         line = self.ways.zs[u]
-        self.arrival(2, u, D, line, 0)
-        self.across(9, u, D, 0)
-        self.arrival(3, u, D, line, 1)
-        self.across(10, u, D, 1)
+        self.arrival(0, u, X, line)
+        self.send(u, "p")
+        self.arrival(1, u, Y, line)
+        self.send(u, "q", X, Y)
+
+    def diag_carried(self, u):
+        line, carried = self.ways.zs[u], self.ways.carried[u]
+
+        def halves():
+            self.arrival(2, u, D, line, 0)
+            self.arrival(3, u, D, line, 1)
+
+        when(carried, halves)
+        self.send(u, "pair")
+        self.send(u, D, condition=carried)
+
+    def diag_handed(self, u):
+        handed = other(self.ways.carried[u])
+        when(handed, lambda: self.arrival(11, u, D, self.ways.zs[u]))
+        self.send(u, D, condition=handed)
 
     def chain_up(self, k):
         w = self.ways
@@ -178,39 +218,43 @@
         self.chain_start(1)
 
     def events(self):
-        lines = self.ways.lines
         out = [
             lambda: (self.xy_event(0), self.chain_event(1), self.send_own(1)),
+            lambda: (self.diag_carried(0), self.chain_event(2), self.send_own(2)),
+            lambda: (self.xy_event(1), self.chain_event(3), self.send_own(3)),
+            lambda: (self.xy_event(2), self.diag_handed(1)),
+            lambda: (self.diag_carried(2), self.xy_event(3)),
+            lambda: (self.diag_carried(3), self.diag_handed(2)),
+            lambda: self.diag_handed(3),
         ]
-        for u in range(2, lines):
-            out.append(lambda u=u: (self.chain_event(u), self.xy_event(u - 1), self.send_own(u)))
-            out.append(lambda u=u: self.diag_event(u - 2))
-        out.append(lambda: self.xy_event(lines - 1))
-        out.append(lambda: self.diag_event(lines - 2))
-        out.append(lambda: self.diag_event(lines - 1))
         return out
 
     def other_core(self):
         if self.across_core:
             for u in range(self.ways.lines):
-                for slot, kind, part in (
-                    (6, O, None), (7, X, None), (8, Y, None), (9, D, 0), (10, D, 1),
-                ):
-                    self.arrival(slot, u, kind, self.ways.zs[u], part, True)
+                for slot, kind in ((6, O), (7, X), (8, Y), (9, D)):
+                    self.arrival(slot, u, kind, self.ways.zs[u], None, True)
+
+    def drain_unit(self, u):
+        for condition, make in self.sends(u).values():
+            when(condition, lambda make=make: make().wait_send())
+
+    def drain_chain(self, k):
+        z, lines = self.ways.spot[0], self.ways.lines
+
+        @pl.when((z >= k - 1) & (z + 1 < lines))
+        def _():
+            self.chain_up(k).wait_send()
+
+        @pl.when((z + k - 1 < lines) & (z > 0))
+        def _():
+            self.chain_down(k).wait_send()
 
     def drain(self):
-        z, lines = self.ways.spot[0], self.ways.lines
-        for copy in self.sent:
-            copy.wait_send()
-        for k in range(1, lines):
-
-            @pl.when((z >= k - 1) & (z + 1 < lines))
-            def _(k=k):
-                self.chain_up(k).wait_send()
-
-            @pl.when((z + k - 1 < lines) & (z > 0))
-            def _(k=k):
-                self.chain_down(k).wait_send()
+        for u in range(self.ways.lines):
+            self.drain_unit(u)
+        for k in range(1, self.ways.lines):
+            self.drain_chain(k)
 
 
 def softmax_rows(scores):
@@ -257,6 +301,18 @@
     group_len = 4 * count
     ways.greet()
 
+    def cot_chunk(line, kind, part, other):
+        first = (line * 4 + kind) * count
+        if part is None:
+            return cot_out.at[pl.ds(first, count)]
+        return cot_out.at[pl.ds(first + part * (count // 2), count // 2)]
+
+    def sems(i):
+        return (lambda k: g_send.at[i, k], lambda k: g_recv.at[i, k])
+
+    g_cot = Gather(ways, cot_chunk, sems(3), own=cot, relative=True)
+    g_cot.begin()
+
     shards = (wq, wk, wv, wo)
     swaps = [
         remote(
@@ -314,20 +370,10 @@
 
         return chunk
 
-    def cot_chunk(line, kind, part, other):
-        first = (line * 4 + kind) * count
-        if part is None:
-            return cot_out.at[pl.ds(first, count)]
-        return cot_out.at[pl.ds(first + part * (count // 2), count // 2)]
-
-    def sems(i):
-        return (lambda k: g_send.at[i, k], lambda k: g_recv.at[i, k])
-
     tiles = half // 128
     g_small = Gather(ways, small_chunk, sems(0))
     g_qkv = Gather(ways, weight_chunk(0, 3 * half, (3 * tiles + 1) // 2 * 128), sems(1), across=True)
     g_out = Gather(ways, weight_chunk(3 * half, half, tiles // 2 * 128), sems(2), across=True)
-    g_cot = Gather(ways, cot_chunk, sems(3), own=cot, relative=True)
     keep = pltpu.make_async_copy(cot, cot_chunk(z, O, None, False), local_sem.at[0])
     keep.start()
     g_small.begin()
@@ -351,11 +397,16 @@
         got = group.at[t]
         group_copy(k, got, got, ways.to_c).wait_recv()
 
-    for k, events in enumerate(zip(g_small.events(), g_qkv.events())):
-        for event in events:
-            event()
-        if k == 2 * lines - 3:
+    small_events, qkv_events = g_small.events(), g_qkv.events()
+    out_events, cot_events = g_out.events(), g_cot.events()
+    for k in range(len(qkv_events)):
+        if k == 3:
             g_out.begin()
+        qkv_events[k]()
+        small_events[k]()
+        if k >= 4:
+            out_events[k - 4]()
+    cot_events[0]()
     flat = jnp.transpose(small_all[...].astype(f32))
     small_t[...] = flat.astype(bf16)
     gain_one = flat[experts : experts + 1, :]
@@ -366,8 +417,8 @@
         n_out[t * count : (t + 1) * count, :] = (x * r * gain_one).astype(bf16)
     g_qkv.other_core()
 
-    out_events = g_out.events()
-    later = out_events[:-2] + [g_cot.begin] + out_events[-2:] + [g_out.other_core] + g_cot.events()
+    later = [out_events[3], cot_events[1], out_events[4], cot_events[2], out_events[5]]
+    later += [out_events[6], g_out.other_core] + cot_events[3:]
 
     def service(n=1):
         for _ in range(n):
@@ -398,7 +449,7 @@
         attended[:, cols] = dense_dot(probs.astype(bf16), v_out[:, cols]).astype(bf16)
         if h % 2:
             service()
-    while len(later) > len(g_cot.events()):
+    while len(later) > len(cot_events) - 3:
         service()
     for h in range(2):
         projected = dense_dot(attended[...], wall[:, pl.ds((h * 4 + 3) * half, half)])
@@ -468,8 +519,8 @@
             pltpu.VMEM((d_rows, 128), bf16),
             pltpu.VMEM((width, 128), bf16),
             pltpu.VMEM((count, group_len), f32),
-            pltpu.SemaphoreType.DMA((4, 11 * lines)),
-            pltpu.SemaphoreType.DMA((4, 11 * lines)),
+            pltpu.SemaphoreType.DMA((4, 12 * lines)),
+            pltpu.SemaphoreType.DMA((4, 12 * lines)),
             pltpu.SemaphoreType.DMA((5,)),
             pltpu.SemaphoreType.DMA((5,)),
             pltpu.SemaphoreType.DMA((3,)),
@@ -483,15 +534,142 @@
     )(lengths, ids, freq, hidden, small, wq, wk, wv, wo, cot)
 
 
+class Reduce:
+    def __init__(self, ways, chunk, cut, pq, xr, yr, dz, zr, sems):
+        self.ways, self.chunk, self.cut = ways, chunk, cut
+        self.pq, self.xr, self.yr, self.dz, self.zr = pq, xr, yr, dz, zr
+        self.send_sem, self.recv_sem = sems
+
+    def copy(self, slot, u, src, dst, to):
+        k = slot * self.ways.lines + u
+        return remote(src, dst, self.send_sem(k), self.recv_sem(k), to)
+
+    def diag(self, part, u):
+        w = self.ways
+        return self.copy(
+            part, u, self.chunk(w.zs[u], D, part), self.cut(self.pq, u, part),
+            w.to_b if part else w.to_a,
+        )
+
+    def side_b(self, part, u):
+        w = self.ways
+        return self.copy(2 + part, u, self.chunk(w.zs[u], X, part), self.cut(self.xr, u, part), w.to_b)
+
+    def side_a(self, part, u):
+        w = self.ways
+        return self.copy(4 + part, u, self.chunk(w.zs[u], Y, part), self.cut(self.yr, u, part), w.to_a)
+
+    def hand(self, u, at):
+        w = self.ways
+        return self.copy(
+            7, at, self.chunk(w.zs[u], D, None), self.cut(self.dz, min(at, 1), None), w.pair
+        )
+
+    def along(self, u):
+        w = self.ways
+        z, a, b, c = w.spot
+        slot = lax.rem(z - w.zs[u] + w.lines, w.lines) - 1
+        k = 6 * w.lines
+        return remote(
+            self.chunk(w.zs[u], O, None), self.zr(slot), self.send_sem(k + u),
+            self.recv_sem(k + slot), device(w.zs[u], a, b, c),
+        )
+
+    def start(self, u):
+        def whole():
+            self.hand(u, u if u > 1 else 0).start()
+            self.side_b(0, u).start()
+            self.side_a(1, u).start()
+
+        self.side_b(1, u).start()
+        self.side_a(0, u).start()
+        when(other(self.ways.carried[u]), whole)
+
+    def carry(self, u):
+        def act():
+            self.hand(u, u).wait_recv()
+            for part in (0, 1):
+                accumulate(
+                    self.chunk(self.ways.zs[u], D, part), [self.cut(self.dz, min(u, 1), part)]
+                )
+                self.diag(part, u).start()
+
+        when(self.ways.carried[u], act)
+
+    def mid(self, u):
+        w = self.ways
+
+        def act():
+            self.diag(0, u).wait_recv()
+            accumulate(self.chunk(w.zs[u], X, 0), [self.cut(self.pq, u, 0)])
+            self.side_b(0, u).start()
+            self.diag(1, u).wait_recv()
+            accumulate(self.chunk(w.zs[u], Y, 1), [self.cut(self.pq, u, 1)])
+            self.side_a(1, u).start()
+
+        when(w.carried[u], act)
+
+    def end(self, u):
+        w = self.ways
+        for part in (0, 1):
+            self.side_b(part, u).wait_recv()
+            self.side_a(part, u).wait_recv()
+            accumulate(
+                self.chunk(w.zs[u], O, part), [self.cut(self.xr, u, part), self.cut(self.yr, u, part)]
+            )
+        if u > 0:
+            self.along(u).start()
+
+    def events(self):
+        return [
+            lambda: (self.start(2), self.start(3)),
+            lambda: (self.carry(2), self.carry(3), self.start(1)),
+            lambda: (self.mid(2), self.mid(3), self.start(0)),
+            lambda: (self.end(2), self.end(3)),
+            lambda: (self.carry(0), self.end(1)),
+            lambda: self.mid(0),
+            lambda: self.end(0),
+        ]
+
+    def total(self):
+        w = self.ways
+        sums = self.chunk(w.spot[0], O, None)[...].astype(f32)
+        for slot in range(w.lines - 1):
+            k = 6 * w.lines + slot
+            here = self.zr(slot)
+            remote(here, here, self.send_sem(k), self.recv_sem(k), w.to_c).wait_recv()
+            sums = sums + here[...].astype(f32)
+        return sums
+
+    def drain(self):
+        w = self.ways
+        for u in range(w.lines):
+            for part in (0, 1):
+                when(w.carried[u], lambda part=part, u=u: self.diag(part, u).wait_send())
+                self.side_b(part, u).wait_send()
+                self.side_a(part, u).wait_send()
+            when(other(w.carried[u]), lambda u=u: self.hand(u, u if u > 1 else 0).wait_send())
+            if u > 0:
+                self.along(u).wait_send()
+
+
+def accumulate(dst, others):
+    total = dst[...].astype(f32)
+    for ref in others:
+        total = total + ref[...].astype(f32)
+    dst[...] = total.astype(bf16)
+
+
 def mixture_kernel(lines, tok, aux, cot, wg, wu, wd, sel, sel_t, router_t, ones, *refs):
     (
-        sums, dw_own, dw_sib, dr,
-        nc, aux_all, vg, vu, vd, dw, acts, dg, du, daff, dlg, pr, qr, xr, yr, zr,
+        sums, out_part, dw_own, dw_sib, dr,
+        nc, aux_all, vg, vu, vd, dw, acts, dg, du, daff, dlg, pq, xr, yr, dz, zr,
         ag_send, ag_recv, rs_send, rs_recv, w_send, w_recv, local_sem,
     ) = refs
-    z, a, b, c = place()
-    oa, ob, oc = 1 - a, 1 - b, 1 - c
-    to_b, to_a, to_c = device(z, a, ob, c), device(z, oa, b, c), device(z, a, b, oc)
+    ways = Ways(lines)
+    z, a, b, c = ways.spot
+    oc = 1 - c
+    zs = ways.zs
     count, width = tok.shape
     half = count // 2
     hc = wg.shape[0]
@@ -499,23 +677,35 @@
     n_sel = sel.shape[1]
     block = 256
     unit_rows = 4 * count
-    table = visit_order(lines)
-    zs = [lookup([table[k][u] for k in range(lines)], z) for u in range(lines)]
-    O, X, Y, D = 0, 1, 2, 3
-
-    barrier = pltpu.get_barrier_semaphore()
-    partners = [to_b, to_a, to_c] + [
-        device(lax.rem(z + s, lines), a, b, c) for s in range(1, lines)
+    ways.greet()
+
+    def rows_of(line, kind, part):
+        first = (line * 4 + kind) * count
+        return pl.ds(first, count) if part is None else pl.ds(first + part * half, half)
+
+    def aux_chunk(line, kind, part, _):
+        rows = aux.shape[0]
+        at = line * 4 + kind
+        if part is None:
+            return aux_all.at[at]
+        return aux_all.at[at, pl.ds(part * (rows // 2), rows // 2)]
+
+    def sems(i):
+        return (lambda k: ag_send.at[i, k], lambda k: ag_recv.at[i, k])
+
+    gathers = [
+        Gather(
+            ways, lambda line, kind, part, _: nc.at[rows_of(line, kind, part), pl.ds(0, width)],
+            sems(0), own=tok, relative=True,
+        ),
+        Gather(ways, aux_chunk, sems(1), own=aux, relative=True),
     ]
-    for partner in partners:
-        pl.semaphore_signal(barrier, inc=1, device_id=partner, device_id_type=MESH)
-    pl.semaphore_wait(barrier, len(partners))
-
-    def remote(src, dst, send_sem, recv_sem, to):
-        return pltpu.make_async_remote_copy(
-            src, dst, send_sem, recv_sem, device_id=to, device_id_type=MESH
-        )
-
+
+    def each(name, *args):
+        for g in gathers:
+            getattr(g, name)(*args)
+
+    each("begin")
     local = []
     mine = pl.ds(c * hc, hc)
     theirs = pl.ds(oc * hc, hc)
@@ -524,116 +714,14 @@
         copy = pltpu.make_async_copy(src, dst.at[mine], local_sem.at[k])
         copy.start()
         local.append(copy)
-        copy = remote(src, dst.at[mine], w_send.at[k], w_recv.at[k], to_c)
+        copy = remote(src, dst.at[mine], w_send.at[k], w_recv.at[k], ways.to_c)
         copy.start()
         w_copies.append(copy)
 
-    def spot(line, kind):
-        return line * 4 + kind
-
-    def tok_at(line, kind, part=None):
-        first = spot(line, kind) * count
-        if part is None:
-            return nc.at[pl.ds(first, count), pl.ds(0, width)]
-        return nc.at[pl.ds(first + part * half, half), pl.ds(0, width)]
-
-    def ag(slot, step, arr):
-        k = slot * lines + step
-        return ag_send.at[arr, k], ag_recv.at[arr, k]
-
-    def ag_copies(slot, step, src_kind, dst_kind, line, to, part=None, own=False):
-        src = tok if own else tok_at(line, src_kind, part)
-        copies = [remote(src, tok_at(line, dst_kind, part), *ag(slot, step, 0), to)]
-        if part != 1:
-            src = aux if own else aux_all.at[spot(line, src_kind)]
-            copies.append(remote(src, aux_all.at[spot(line, dst_kind)], *ag(slot, step, 1), to))
-        return copies
-
-    def send_own(u):
-        own = u == 0
-        return ag_copies(0, u, O, X, zs[u], to_b, own=own) + ag_copies(1, u, O, Y, zs[u], to_a, own=own)
-
-    def send_halves(u):
-        return ag_copies(2, u, X, D, zs[u], to_a, 0) + ag_copies(3, u, Y, D, zs[u], to_b, 1)
-
-    def start(copies):
-        for copy in copies:
-            copy.start()
-
-    def wait_recv(copies):
-        for copy in copies:
-            copy.wait_recv()
-
-    def wait_send(copies):
-        for copy in copies:
-            copy.wait_send()
-
-    up_next = device(lax.rem(z + 1, lines), a, b, c)
-    down_next = device(lax.rem(z + lines - 1, lines), a, b, c)
-
-    def chain_up(k, own=False):
-        return ag_copies(4, k, O, O, z - (k - 1), up_next, own=own)
-
-    def chain_down(k, own=False):
-        return ag_copies(5, k, O, O, z + (k - 1), down_next, own=own)
-
-    def chain_event(k):
-        @pl.when(z >= k)
-        def _():
-            wait_recv(ag_copies(4, k, O, O, z - k, up_next))
-
-            if k + 1 < lines:
-
-                @pl.when(z + 1 < lines)
-                def _():
-                    start(chain_up(k + 1))
-
-        @pl.when(z + k < lines)
-        def _():
-            wait_recv(ag_copies(5, k, O, O, z + k, down_next))
-
-            if k + 1 < lines:
-
-                @pl.when(z > 0)
-                def _():
-                    start(chain_down(k + 1))
-
-    def chain_drain(k):
-        @pl.when((z >= k - 1) & (z + 1 < lines))
-        def _():
-            wait_send(chain_up(k, own=k == 1))
-
-        @pl.when((z + k - 1 < lines) & (z > 0))
-        def _():
-            wait_send(chain_down(k, own=k == 1))
-
-    def xy_event(u):
-        wait_recv(ag_copies(0, u, O, X, zs[u], to_b))
-        wait_recv(ag_copies(1, u, O, Y, zs[u], to_a))
-        start(send_halves(u))
-
-    def diag_event(u):
-        wait_recv(ag_copies(2, u, X, D, zs[u], to_a, 0))
-        wait_recv(ag_copies(3, u, Y, D, zs[u], to_b, 1))
-
-    def sent_event(u):
-        wait_send(send_own(u))
-        wait_send(send_halves(u))
-
-    start(send_own(0))
-
-    @pl.when(z + 1 < lines)
-    def _():
-        start(chain_up(1, own=True))
-
-    @pl.when(z > 0)
-    def _():
-        start(chain_down(1, own=True))
-
-    copy = pltpu.make_async_copy(tok, tok_at(z, O), local_sem.at[3])
+    copy = pltpu.make_async_copy(tok, nc.at[rows_of(z, O, None), pl.ds(0, width)], local_sem.at[3])
     copy.start()
     local.append(copy)
-    copy = pltpu.make_async_copy(aux, aux_all.at[spot(z, O)], local_sem.at[4])
+    copy = pltpu.make_async_copy(aux, aux_chunk(z, O, None, False), local_sem.at[4])
     copy.start()
     local.append(copy)
     copy = pltpu.make_async_copy(cot, nc.at[:, pl.ds(width, width)], local_sem.at[5])
@@ -647,88 +735,42 @@
     lax.fori_loop(0, hidden // 64, zero, 0)
     dr[...] = jnp.zeros_like(dr)
 
-    def res(line, kind, part=None):
-        first = spot(line, kind) * count
-        if part is None:
-            return nc.at[pl.ds(first, count)]
-        return nc.at[pl.ds(first + part * half, half)]
-
-    def part_of(ref, u, part):
-        return ref.at[u, pl.ds(part * half, half)]
-
-    def rs(slot, u):
-        k = slot * lines + u
-        return rs_send.at[k], rs_recv.at[k]
-
-    def p_copy(u):
-        return remote(res(zs[u], D, 0), pr.at[u], *rs(0, u), to_a)
-
-    def q_copy(u):
-        return remote(res(zs[u], D, 1), qr.at[u], *rs(1, u), to_b)
-
-    def x_copy(u, part):
-        return remote(res(zs[u], X, part), part_of(xr, u, part), *rs(2 + part, u), to_b)
-
-    def y_copy(u, part):
-        return remote(res(zs[u], Y, part), part_of(yr, u, part), *rs(4 + part, u), to_a)
-
-    def z_copy(u):
-        slot = lax.rem(z - zs[u] + lines, lines) - 1
-        k = 6 * lines
-        return remote(
-            res(zs[u], O), zr.at[slot], rs_send.at[k + u], rs_recv.at[k + slot],
-            device(zs[u], a, b, c),
-        )
-
-    def add(first, rows, others):
-        def body(k, carry):
-            there = pl.ds(pl.multiple_of(k * 256, 256), 256)
-            at = pl.ds(first, rows)
-            total = nc[at, there].astype(f32)
-            for ref, u in others:
-                total = total + ref[u, :, there].astype(f32)
-            nc[at, there] = total.astype(bf16)
-            return carry
-
-        lax.fori_loop(0, 2 * width // 256, body, 0)
-
-    def rs_start(u):
-        p_copy(u).start()
-        q_copy(u).start()
-        x_copy(u, 1).start()
-        y_copy(u, 0).start()
-
-    def rs_mid(u):
-        p_copy(u).wait_recv()
-        add(spot(zs[u], X) * count, half, [(pr, u)])
-        x_copy(u, 0).start()
-        q_copy(u).wait_recv()
-        add(spot(zs[u], Y) * count + half, half, [(qr, u)])
-        y_copy(u, 1).start()
-
-    def rs_end(u):
-        for part in (0, 1):
-            x_copy(u, part).wait_recv()
-            y_copy(u, part).wait_recv()
-        add(spot(zs[u], O) * count, count, [(xr, u), (yr, u)])
-        if u > 0:
-            z_copy(u).start()
+    def cut(ref, u, part):
+        return ref.at[u] if part is None else ref.at[u, pl.ds(part * half, half)]
+
+    back = Reduce(
+        ways, lambda line, kind, part: nc.at[rows_of(line, kind, part), pl.ds(width, width)], cut,
+        pq, xr, yr, dz, lambda slot: zr.at[slot],
+        (lambda k: rs_send.at[k], lambda k: rs_recv.at[k]),
+    )
+
+    def save(u):
+        rows = pl.ds(pl.multiple_of(zs[u] * unit_rows, unit_rows), unit_rows)
+        return pltpu.make_async_copy(
+            nc.at[rows, pl.ds(0, width)], out_part.at[rows], local_sem.at[7 + u]
+        )
 
     def expand(line, columns):
         return jnp.concatenate(
-            [dot_tn(aux_all[spot(line, kind)], sel[:, columns]) for kind in range(4)], axis=0
-        )
-
-    def unit(u, carry):
-        line = pick(zs, u)
+            [dot_tn(aux_all[line * 4 + kind], sel[:, columns]) for kind in range(4)], axis=0
+        )
+
+    def at_step(s, acts_of):
+        for v, act in acts_of.items():
+            when(s == v, act)
+
+    order = [1, 2, 3, 0]
+
+    def unit(s, carry):
+        line = pick([zs[u] for u in order], s)
         rows = pl.ds(pl.multiple_of(line * unit_rows, unit_rows), unit_rows)
-
-        for v in range(lines):
-
-            @pl.when(u == v)
-            def _(v=v):
-                diag_event(v)
-
+        at_step(
+            s,
+            {
+                1: lambda: (each("diag_handed", 2), each("xy_event", 3)),
+                2: lambda: each("diag_handed", 3),
+            },
+        )
         daff[...] = jnp.zeros_like(daff)
 
         def hidden_step(i, carry):
@@ -748,125 +790,103 @@
             du[:, h] = (grad * silu).astype(bf16)
             return carry
 
-        lax.fori_loop(0, hidden // block, hidden_step, 0)
+        lax.fori_loop(0, hidden // block, hidden_step, 0, unroll=True)
         signed = expand(line, pl.ds(hidden, n_sel - hidden))
         affinity = jnp.abs(signed)
         grad_aff = jnp.where(signed > 0, daff[...], 0.0)
         total = jnp.sum(affinity * grad_aff, axis=1, keepdims=True)
         dlg[...] = (affinity * (grad_aff - total)).astype(bf16)
-
-        @pl.when(u == 0)
-        def _():
-            if lines > 2:
-                chain_event(2)
-
-        for v in range(1, lines - 1):
-
-            @pl.when(u == v)
-            def _(v=v):
-                xy_event(v + 1)
-                if v + 2 < lines:
-                    start(send_own(v + 2))
+        at_step(
+            s,
+            {
+                0: lambda: (each("chain_event", 3), each("xy_event", 2), each("send_own", 3)),
+                1: lambda: each("diag_carried", 3),
+                2: lambda: (back.carry(2), back.end(1)),
+                3: lambda: (back.carry(3), back.end(2)),
+            },
+        )
+
+        def down_step(i, carry):
+            h = pl.ds(pl.multiple_of(i * block, block), block)
+            dw[2, h, :] += dot_tn(acts[:, h], nc[rows, width : 2 * width])
+            return carry
+
+        lax.fori_loop(0, hidden // block, down_step, 0, unroll=True)
+
+        def back_step(i, carry):
+            n = pl.ds(pl.multiple_of(i * block, block), block)
+            n2 = pl.ds(pl.multiple_of(width + i * block, block), block)
+            nc[rows, n2] = (
+                dense_dot(dg[...], vg[:, n])
+                + dense_dot(du[...], vu[:, n])
+                + dense_dot(dlg[...], router_t[:, n])
+            ).astype(bf16)
+            return carry
+
+        lax.fori_loop(0, width // block, back_step, 0, unroll=True)
+        at_step(
+            s,
+            {
+                0: lambda: (each("diag_carried", 2), back.start(1)),
+                1: lambda: back.start(2),
+                2: lambda: (back.mid(2), back.start(3)),
+                3: lambda: (back.mid(3), back.start(0), back.carry(0)),
+            },
+        )
 
         def weight_step(i, carry):
             h = pl.ds(pl.multiple_of(i * block, block), block)
             x = nc[rows, 0:width]
             dw[0, h, :] += dot_tn(dg[:, h], x)
             dw[1, h, :] += dot_tn(du[:, h], x)
-            dw[2, h, :] += dot_tn(acts[:, h], nc[rows, width : 2 * width])
             return carry
 
-        lax.fori_loop(0, hidden // block, weight_step, 0)
+        lax.fori_loop(0, hidden // block, weight_step, 0, unroll=True)
         dr[...] += dot_tn(dlg[...], nc[rows, 0:width])
-
-        for v in range(lines):
-
-            @pl.when(u == v)
-            def _(v=v):
-                if v == 0:
-                    xy_event(1)
-                    if lines > 2:
-                        start(send_own(2))
-                    chain_drain(1)
-                elif v == 1:
-                    for k in range(2, lines):
-                        chain_drain(k)
-                elif v == 2:
-                    rs_mid(1)
-                sent_event(v)
-
-        def back_step(i, carry):
+        for v, u in enumerate(order):
+            when(s == v, lambda u=u: each("drain_unit", u))
+        at_step(
+            s,
+            {
+                0: lambda: (each("drain_chain", 1), each("drain_chain", 2)),
+                1: lambda: each("drain_chain", 3),
+                3: lambda: (back.mid(0), back.end(3)),
+            },
+        )
+
+        def out_step(i, carry):
             n = pl.ds(pl.multiple_of(i * block, block), block)
-            n2 = pl.ds(pl.multiple_of(width + i * block, block), block)
-            out = dense_dot(acts[...], vd[:, n])
-            back = (
-                dense_dot(dg[...], vg[:, n])
-                + dense_dot(du[...], vu[:, n])
-                + dense_dot(dlg[...], router_t[:, n])
-            )
-            nc[rows, n] = out.astype(bf16)
-            nc[rows, n2] = back.astype(bf16)
+            nc[rows, n] = dense_dot(acts[...], vd[:, n]).astype(bf16)
             return carry
 
-        lax.fori_loop(0, width // block, back_step, 0)
-
-        @pl.when(u == 0)
-        def _():
-            for k in range(3, lines):
-                chain_event(k)
-
-        for v in range(1, lines):
-
-            @pl.when(u == v)
-            def _(v=v):
-                rs_start(v)
-
+        lax.fori_loop(0, width // block, out_step, 0, unroll=True)
+        for v, u in enumerate(order):
+            when(s == v, lambda u=u: save(u).start())
         return carry
 
-    xy_event(0)
-    chain_event(1)
-    start(send_own(1))
+    each("xy_event", 0)
+    each("chain_event", 1)
+    each("send_own", 1)
+    each("diag_carried", 0)
+    each("chain_event", 2)
+    each("send_own", 2)
+    each("xy_event", 1)
     for copy in w_copies:
         copy.wait_recv()
     for copy in local:
         copy.wait()
+    each("diag_handed", 1)
     lax.fori_loop(0, lines, unit, 0)
 
     own_out = pltpu.make_async_copy(dw.at[:, mine], dw_own, local_sem.at[6])
     own_out.start()
-    sib_out = remote(dw.at[:, theirs], dw_sib, w_send.at[3], w_recv.at[3], to_c)
+    sib_out = pltpu.make_async_copy(dw.at[:, theirs], dw_sib, local_sem.at[7 + lines])
     sib_out.start()
-    rs_mid(2)
-    rs_end(1)
-    rs_start(0)
-    rs_mid(3)
-    rs_end(2)
-    rs_mid(0)
-    rs_end(3)
-    rs_end(0)
-    for slot in range(lines - 1):
-        k = 6 * lines + slot
-        remote(
-            zr.at[slot], zr.at[slot], rs_send.at[k], rs_recv.at[k], to_c
-        ).wait_recv()
-
-    def finish(k, carry):
-        there = pl.ds(pl.multiple_of(k * 128, 128), 128)
-        total = nc[pl.ds(spot(z, O) * count, count), there].astype(f32)
-        for slot in range(lines - 1):
-            total = total + zr[slot, :, there].astype(f32)
-        sums[:, there] = total
-        return carry
-
-    lax.fori_loop(0, 2 * width // 128, finish, 0)
+    back.end(0)
+    sums[...] = back.total()
+    back.drain()
     for u in range(lines):
-        p_copy(u).wait_send()
-        q_copy(u).wait_send()
-        for part in (0, 1):
-            x_copy(u, part).wait_send()
-            y_copy(u, part).wait_send()
-        if u > 0:
-            z_copy(u).wait_send()
+        save(u).wait()
     for copy in w_copies:
         copy.wait_send()
     sib_out.wait()
@@ -883,13 +903,14 @@
     return pl.pallas_call(
         functools.partial(mixture_kernel, lines),
         out_shape=(
-            jax.ShapeDtypeStruct((count, 2 * width), f32),
+            jax.ShapeDtypeStruct((count, width), f32),
+            jax.ShapeDtypeStruct((n_rows, width), bf16),
             jax.ShapeDtypeStruct((3, hc, width), f32),
             jax.ShapeDtypeStruct((3, hc, width), f32),
             jax.ShapeDtypeStruct((128, width), f32),
         ),
         in_specs=[anywhere] * 6 + [vmem] * 4,
-        out_specs=(vmem, anywhere, anywhere, vmem),
+        out_specs=(vmem, anywhere, anywhere, anywhere, vmem),
         scratch_shapes=[
             pltpu.VMEM((n_rows, 2 * width), bf16),
             pltpu.VMEM((lines * 4,) + aux.shape, bf16),
@@ -902,18 +923,18 @@
             pltpu.VMEM((4 * count, 2 * hc), bf16),
             pltpu.VMEM((4 * count, 128), f32),
             pltpu.VMEM((4 * count, 128), bf16),
-            pltpu.VMEM((lines, count // 2, 2 * width), bf16),
-            pltpu.VMEM((lines, count // 2, 2 * width), bf16),
-            pltpu.VMEM((lines, count, 2 * width), bf16),
-            pltpu.VMEM((lines, count, 2 * width), bf16),
-            pltpu.VMEM((lines - 1, count, 2 * width), bf16),
-            pltpu.SemaphoreType.DMA((2, 6 * lines)),
-            pltpu.SemaphoreType.DMA((2, 6 * lines)),
-            pltpu.SemaphoreType.DMA((7 * lines,)),
-            pltpu.SemaphoreType.DMA((7 * lines,)),
+            pltpu.VMEM((lines, count, width), bf16),
+            pltpu.VMEM((lines, count, width), bf16),
+            pltpu.VMEM((lines, count, width), bf16),
+            pltpu.VMEM((2, count, width), bf16),
+            pltpu.VMEM((lines - 1, count, width), bf16),
+            pltpu.SemaphoreType.DMA((2, 12 * lines)),
+            pltpu.SemaphoreType.DMA((2, 12 * lines)),
+            pltpu.SemaphoreType.DMA((8 * lines,)),
+            pltpu.SemaphoreType.DMA((8 * lines,)),
             pltpu.SemaphoreType.DMA((4,)),
             pltpu.SemaphoreType.DMA((4,)),
-            pltpu.SemaphoreType.DMA((7,)),
+            pltpu.SemaphoreType.DMA((8 + lines,)),
         ],
         compiler_params=pltpu.CompilerParams(
             collective_id=collective_id, has_side_effects=True, vmem_limit_bytes=62 * 2**20
@@ -922,114 +943,14 @@
     )(tok, aux, cot, *weights, sel, sel_t, router_t, ones)
 
 
-class Reduce:
-    def __init__(self, ways, chunk, cut, pq, xr, yr, zr, sems):
-        self.ways, self.chunk, self.cut = ways, chunk, cut
-        self.pq, self.xr, self.yr, self.zr = pq, xr, yr, zr
-        self.send_sem, self.recv_sem = sems
-
-    def copy(self, slot, u, src, dst, to):
-        k = slot * self.ways.lines + u
-        return remote(src, dst, self.send_sem(k), self.recv_sem(k), to)
-
-    def diag(self, part, u):
-        w = self.ways
-        return self.copy(
-            part, u, self.chunk(w.zs[u], D, part), self.cut(self.pq, u, part),
-            w.to_b if part else w.to_a,
-        )
-
-    def side_b(self, part, u):
-        w = self.ways
-        return self.copy(2 + part, u, self.chunk(w.zs[u], X, part), self.cut(self.xr, u, part), w.to_b)
-
-    def side_a(self, part, u):
-        w = self.ways
-        return self.copy(4 + part, u, self.chunk(w.zs[u], Y, part), self.cut(self.yr, u, part), w.to_a)
-
-    def along(self, u):
-        w = self.ways
-        z, a, b, c = w.spot
-        slot = lax.rem(z - w.zs[u] + w.lines, w.lines) - 1
-        k = 6 * w.lines
-        return remote(
-            self.chunk(w.zs[u], O, None), self.zr(slot), self.send_sem(k + u),
-            self.recv_sem(k + slot), device(w.zs[u], a, b, c),
-        )
-
-    def start(self, u):
-        self.diag(0, u).start()
-        self.diag(1, u).start()
-        self.side_b(1, u).start()
-        self.side_a(0, u).start()
-
-    def mid(self, u):
-        w = self.ways
-        self.diag(0, u).wait_recv()
-        accumulate(self.chunk(w.zs[u], X, 0), [self.cut(self.pq, u, 0)])
-        self.side_b(0, u).start()
-        self.diag(1, u).wait_recv()
-        accumulate(self.chunk(w.zs[u], Y, 1), [self.cut(self.pq, u, 1)])
-        self.side_a(1, u).start()
-
-    def end(self, u):
-        w = self.ways
-        for part in (0, 1):
-            self.side_b(part, u).wait_recv()
-            self.side_a(part, u).wait_recv()
-            accumulate(
-                self.chunk(w.zs[u], O, part), [self.cut(self.xr, u, part), self.cut(self.yr, u, part)]
-            )
-        if u > 0:
-            self.along(u).start()
-
-    def events(self):
-        lines = self.ways.lines
-        order = list(range(1, lines)) + [0]
-        out = []
-        for k in range(lines + 2):
-            if k < lines:
-                out.append(lambda k=k: self.start(order[k]))
-            if 1 <= k <= lines:
-                out.append(lambda k=k: self.mid(order[k - 1]))
-            if k >= 2:
-                out.append(lambda k=k: self.end(order[k - 2]))
-        return out
-
-    def total(self):
-        w = self.ways
-        sums = self.chunk(w.spot[0], O, None)[...].astype(f32)
-        for slot in range(w.lines - 1):
-            k = 6 * w.lines + slot
-            here = self.zr(slot)
-            remote(here, here, self.send_sem(k), self.recv_sem(k), w.to_c).wait_recv()
-            sums = sums + here[...].astype(f32)
-        return sums
-
-    def drain(self):
-        for u in range(self.ways.lines):
-            for part in (0, 1):
-                self.diag(part, u).wait_send()
-                self.side_b(part, u).wait_send()
-                self.side_a(part, u).wait_send()
-            if u > 0:
-                self.along(u).wait_send()
-
-
-def accumulate(dst, others):
-    total = dst[...].astype(f32)
-    for ref in others:
-        total = total + ref[...].astype(f32)
-    dst[...] = total.astype(bf16)
-
-
 def back_kernel(lines, experts, scale, *refs):
     (
-        lengths, sums, residual, cot, group, small_t, router_part, attended, q, keys, vals, normed,
-        cosine, sine, wall_in,
-        layer_out, input_grad, gq, gk, gv, go, small_out,
-        wall, part, landed, pq, xr, yr, zr, fin, fin_other,
-        s_part, s_landed, s_pq, s_xr, s_yr, s_zr,
+        lengths, dn2, residual, cot, group, small_t, router_part, attended, q, normed, cosine, sine,
+        keys, vals, wall_in, outs_in, dw_sib,
+        layer_out, input_grad, gq, gk, gv, go, small_out, dw_got,
+        wall, part, staged, landed, pq, xr, yr, dz, zr, fin, fin_other,
+        s_part, s_landed, s_pq, s_xr, s_yr, s_dz, s_zr,
+        o_part, o_pq, o_xr, o_yr, o_dz, o_zr,
         grads, low, datt, dq, dk, dv, dn_part, dn_other, dn_far, bias, rows_t,
         c_send, c_recv, r_send, r_recv, d_send, d_recv, local_sem,
     ) = refs
@@ -1039,45 +960,83 @@
     count, width = cot.shape
     half = width // 2
     heads = width // 128
-    chip_rows = pq.shape[2]
+    chip_rows = pq.shape[1]
     d_rows = chip_rows // 2
-    load = pltpu.make_async_copy(wall_in, wall, local_sem.at[0])
-    load.start()
+
+    def load(i, src, dst):
+        copy = pltpu.make_async_copy(src, dst, local_sem.at[i])
+        copy.start()
+        return copy
+
+    o_load = load(0, outs_in, o_part)
+    wo_loads = [
+        load(1 + h, wall_in.at[:, pl.ds((h * 4 + 3) * half, half)], part.at[:, pl.ds(h * half, half)])
+        for h in range(2)
+    ]
+    kv_loads = [load(3, keys, dk), load(4, vals, dv)]
+    wall_loads = [
+        load(5 + h, wall_in.at[:, pl.ds(h * 4 * half, 3 * half)], wall.at[:, pl.ds(h * 3 * half, 3 * half)])
+        for h in range(2)
+    ]
+
+    def weight(h, k):
+        return wall[:, pl.ds((h * 3 + k) * half, half)]
+
     ways.greet()
+
+    half_rows = count // 2
+
+    def o_chunk(line, kind, p):
+        first = (line * 4 + kind) * count
+        return o_part.at[pl.ds(first, count) if p is None else pl.ds(first + p * half_rows, half_rows)]
+
+    def o_cut(ref, u, p):
+        return ref.at[u] if p is None else ref.at[u, pl.ds(p * half_rows, half_rows)]
+
+    o_reduce = Reduce(
+        ways, o_chunk, o_cut, o_pq, o_xr, o_yr, o_dz, lambda slot: o_zr.at[slot],
+        (lambda i: r_send.at[3, i], lambda i: r_recv.at[3, i]),
+    )
+
+    def finish_output():
+        layer_out[...] = (residual[...] + o_reduce.total()).astype(bf16)
+
+    o_events = o_reduce.events() + [finish_output]
+    o_load.wait()
+    o_events[0]()
+    dw_copy = remote(dw_sib, dw_got, c_send.at[6], c_recv.at[6], ways.to_c)
+    dw_copy.start()
 
     res = residual[...]
     r2 = lax.rsqrt(jnp.mean(res * res, axis=-1, keepdims=True) + epsilon)
     unit_two = res * r2
-    dn2 = sums[:, width : 2 * width]
     gain_two = small_t[experts + 1 : experts + 2, :].astype(f32)
     gain_one = small_t[experts : experts + 1, :].astype(f32)
     rows_t[...] = router_part[...]
-    rows_t[experts + 1 : experts + 2, :] = jnp.sum(dn2 * unit_two, axis=0, keepdims=True)
-    scaled = dn2 * gain_two
+    rows_t[experts + 1 : experts + 2, :] = jnp.sum(dn2[...] * unit_two, axis=0, keepdims=True)
+    scaled = dn2[...] * gain_two
     back = r2 * (scaled - unit_two * jnp.mean(scaled * unit_two, axis=-1, keepdims=True))
     grads[...] = cot[...].astype(f32) + back
     low[...] = grads[...].astype(bf16)
-    layer_out[...] = (res + sums[:, 0:width]).astype(bf16)
     make_bias(bias, lengths, b * 2 + c)
 
-    cuts = [half // 256 * 128, (half // 128 - half // 256) * 128] * 2
-
-    def weight_reduce(k):
+    def weight_reduce(k, first, cols):
+        low_cols = cols // 256 * 128
+
         def span(p):
-            return (0, half) if p is None else ((0, cuts[k]) if p == 0 else (cuts[k], half - cuts[k]))
+            return (0, cols) if p is None else ((0, low_cols) if p == 0 else (low_cols, cols - low_cols))
 
         def chunk(line, kind, p):
             start, size = span(p)
             rows = pl.multiple_of(ways.chip(line, kind) * chip_rows, 16)
-            first = pl.multiple_of((c * 4 + k) * half + start, 128)
-            return part.at[pl.ds(rows, chip_rows), pl.ds(first, size)]
+            return part.at[pl.ds(rows, chip_rows), pl.ds(first + start, size)]
 
         def cut(ref, u, p):
             start, size = span(p)
-            return ref.at[k, u, :, pl.ds(start, size)]
+            return ref.at[u, :, pl.ds(first + start, size)]
 
         return Reduce(
-            ways, chunk, cut, pq, xr, yr, lambda slot: zr.at[k, slot],
+            ways, chunk, cut, pq, xr, yr, dz, lambda slot: zr.at[slot, :, pl.ds(first, cols)],
             (lambda i: r_send.at[k, i], lambda i: r_recv.at[k, i]),
         )
 
@@ -1094,24 +1053,21 @@
         return ref.at[u, pl.ds(start, size)]
 
     small_reduce = Reduce(
-        ways, small_chunk, small_cut, s_pq, s_xr, s_yr, lambda slot: s_zr.at[slot],
-        (lambda i: r_send.at[4, i], lambda i: r_recv.at[4, i]),
-    )
-    reduces = [weight_reduce(k) for k in range(4)]
+        ways, small_chunk, small_cut, s_pq, s_xr, s_yr, s_dz, lambda slot: s_zr.at[slot],
+        (lambda i: r_send.at[2, i], lambda i: r_recv.at[2, i]),
+    )
+    qkv_reduce = weight_reduce(0, 0, 3 * half)
+    wo_reduce = weight_reduce(1, 3 * half, half)
 
     def across(k):
-        cols = pl.ds(pl.multiple_of((oc * 4 + k) * half, 128), half)
-        return remote(part.at[:, cols], landed.at[k], c_send.at[k], c_recv.at[k], ways.to_c)
-
-    def own_cols(k):
-        return pl.ds(pl.multiple_of((c * 4 + k) * half, 128), half)
+        return remote(staged.at[k % 2], landed.at[k], c_send.at[k], c_recv.at[k], ways.to_c)
 
     def swapped(k):
         across(k).wait_recv()
 
         def body(i, carry):
             rows = pl.ds(pl.multiple_of(i * chip_rows, 16), chip_rows)
-            accumulate(part.at[rows, own_cols(k)], [landed.at[k, rows]])
+            accumulate(part.at[rows, pl.ds(k * half, half)], [landed.at[k, rows]])
             return carry
 
         lax.fori_loop(0, width // chip_rows, body, 0)
@@ -1123,50 +1079,65 @@
             if later:
                 later.pop(0)()
 
+    def columns(core):
+        return pl.ds(pl.multiple_of(core * half, 128), half)
+
     def weight_grad(k, left, right):
-        for h in range(2):
-            cols = pl.ds((h * 4 + k) * half, half)
-            part[:, cols] = dot_tn(left, right[:, h * half : (h + 1) * half]).astype(bf16)
+        if k < 2:
+            across(k + 2).wait_send()
+        staged[k % 2] = dot_tn(left, right[:, columns(oc)]).astype(bf16)
         across(k).start()
-        later.append(lambda: swapped(k))
-        later.extend(reduces[k].events())
-
+        part[:, pl.ds(k * half, half)] = dot_tn(left, right[:, columns(c)]).astype(bf16)
+
+    o_events[1]()
     weight_grad(3, attended[...], low)
-    load.wait()
+    for copy in wo_loads:
+        copy.wait()
     datt[...] = (
-        dot_nt(low[:, 0:half], wall[:, pl.ds(3 * half, half)])
-        + dot_nt(low[:, half:width], wall[:, pl.ds(7 * half, half)])
+        dot_nt(low[:, 0:half], part[:, 0:half]) + dot_nt(low[:, half:width], part[:, half:width])
     ).astype(bf16)
-    service()
+    wo_events = wo_reduce.events()
+    later.append(lambda: swapped(3))
+    for k in range(6):
+        later.append(o_events[k + 2])
+        later.extend(wo_events[:2] if k == 0 else [wo_events[k + 1]])
+    for copy in kv_loads:
+        copy.wait()
 
     own_rows = pl.ds(pl.multiple_of((b * 2 + c) * count, count), count)
     for h in range(heads):
         cols = pl.ds(h * 128, 128)
-        probs = softmax_rows(dot_nt(q[:, cols], keys[:, cols]) * scale + bias[...])
-        dprobs = dot_nt(datt[:, cols], vals[:, cols])
+        key, val, query = dk[:, cols], dv[:, cols], q[:, cols]
+        probs = softmax_rows(dot_nt(query, key) * scale + bias[...])
+        dprobs = dot_nt(datt[:, cols], val)
         dscores = (
             probs * (dprobs - jnp.sum(probs * dprobs, axis=-1, keepdims=True))
         ).astype(bf16)
         dq[:, cols] = turn(
-            dense_dot(dscores, keys[:, cols]) * scale, cosine[own_rows, :], -sine[own_rows, :]
+            dense_dot(dscores, key) * scale, cosine[own_rows, :], -sine[own_rows, :]
         ).astype(bf16)
-        dk[:, cols] = turn(dot_tn(dscores, q[:, cols]) * scale, cosine[...], -sine[...]).astype(bf16)
+        dk[:, cols] = turn(dot_tn(dscores, query) * scale, cosine[...], -sine[...]).astype(bf16)
         dv[:, cols] = dot_tn(probs.astype(bf16), datt[:, cols]).astype(bf16)
-        service()
+        if h in (1, 3, 4, 6, 8, 9):
+            service()
     weight_grad(2, normed[...], dv)
-    service(2)
     weight_grad(1, normed[...], dk)
-    service(2)
+    service()
     weight_grad(0, normed[own_rows, :], dq)
-    service(2)
-
+    for k in (2, 1, 0):
+        swapped(k)
+    qkv_events = qkv_reduce.events()
+    qkv_events[0]()
+    later = [later[0], later[1], qkv_events[1]] + later[2:]
+
+    for copy in wall_loads:
+        copy.wait()
     for t in range(4):
         rows = slice(t * count, (t + 1) * count)
         total = jnp.zeros((count, width), f32)
         for h in range(2):
             mine = slice(h * half, (h + 1) * half)
-            total = total + dot_nt(dk[rows, mine], wall[:, pl.ds((h * 4 + 1) * half, half)])
-            total = total + dot_nt(dv[rows, mine], wall[:, pl.ds((h * 4 + 2) * half, half)])
+            total = total + dot_nt(dk[rows, mine], weight(h, 1)) + dot_nt(dv[rows, mine], weight(h, 2))
         dn_part[t] = total.astype(bf16)
         x = group[t].astype(f32)
         unit = x * lax.rsqrt(jnp.mean(x * x, axis=-1, keepdims=True) + epsilon)
@@ -1188,7 +1159,7 @@
         copy.start()
     own = jnp.zeros((count, width), f32)
     for h in range(2):
-        own = own + dot_nt(dq[:, h * half : (h + 1) * half], wall[:, pl.ds(h * 4 * half, half)])
+        own = own + dot_nt(dq[:, h * half : (h + 1) * half], weight(h, 0))
     x = group[b * 2 + c].astype(f32)
     r1 = lax.rsqrt(jnp.mean(x * x, axis=-1, keepdims=True) + epsilon)
     unit_one = x * r1
@@ -1204,8 +1175,12 @@
     dn_copies[0].wait_recv()
     small_swap.wait()
     accumulate(s_part, [s_landed])
-    later.extend(small_reduce.events())
-    service(2)
+    service(len(later))
+    small_events = small_reduce.events()
+    for k in range(2, len(qkv_events)):
+        later.extend([small_events[k - 2], qkv_events[k]])
+    later.extend(small_events[-2:])
+    service(4)
     dn_copies[2].wait_recv()
     total = (
         own
@@ -1221,30 +1196,29 @@
 
     theirs = pl.ds(pl.multiple_of(oc * d_rows, 8), d_rows)
     mine = pl.ds(pl.multiple_of(c * d_rows, 8), d_rows)
-    fin_copies = []
-    for k in (3, 2, 1, 0):
-        fin[k] = reduces[k].total()
-        copy = remote(fin.at[k, theirs], fin_other.at[k], c_send.at[5 + k], c_recv.at[5 + k], ways.to_c)
-        copy.start()
-        fin_copies.append(copy)
+    fin[:, pl.ds(3 * half, half)] = wo_reduce.total()
+    fin[:, pl.ds(0, 3 * half)] = qkv_reduce.total()
+    fin_copy = remote(fin.at[theirs], fin_other, c_send.at[5], c_recv.at[5], ways.to_c)
+    fin_copy.start()
     s_total = small_reduce.total()
     small_out[...] = jnp.where(c == 0, s_total[:d_rows], s_total[d_rows:])
-    for k, copy in zip((3, 2, 1, 0), fin_copies):
-        copy.wait_recv()
-        out = (gq, gk, gv, go)[k]
-        out[:, pl.ds(pl.multiple_of(c * half, 128), half)] = fin[k, mine, :]
-        out[:, pl.ds(pl.multiple_of(oc * half, 128), half)] = fin_other[k]
-    for r in reduces + [small_reduce]:
+    for k, out in enumerate((gq, gk, gv, go)):
+        out[:, columns(c)] = fin[mine, pl.ds(k * half, half)]
+    fin_copy.wait_recv()
+    for k, out in enumerate((gq, gk, gv, go)):
+        out[:, columns(oc)] = fin_other[:, pl.ds(k * half, half)]
+    for r in (qkv_reduce, wo_reduce, small_reduce, o_reduce):
         r.drain()
-    for copy in dn_copies + fin_copies:
+    for copy in dn_copies + [fin_copy]:
         copy.wait_send()
-    for k in range(4):
+    dw_copy.wait()
+    for k in range(2):
         across(k).wait_send()
 
 
 def back_call(
-    lengths, sums, residual, cot, group, small_t, router_part, attended, q, keys, vals, normed,
-    cosine, sine, wall, d_rows, experts, scale, collective_id,
+    lengths, dn2, residual, cot, group, small_t, router_part, attended, q, normed, cosine, sine,
+    keys, vals, wall, outs, dw_sib, d_rows, experts, scale, collective_id,
 ):
     lines = lax.axis_size("ep") // 2
     count, width = cot.shape
@@ -1256,6 +1230,10 @@
     smem = pl.BlockSpec(memory_space=pltpu.SMEM)
     shape = jax.ShapeDtypeStruct
     dma = pltpu.SemaphoreType.DMA
+
+    def landing(rows, cols):
+        return [pltpu.VMEM((n, rows, cols), bf16) for n in (lines, lines, lines, 2, lines - 1)]
+
     return pl.pallas_call(
         functools.partial(back_kernel, lines, experts, scale),
         out_shape=(
@@ -1266,25 +1244,23 @@
             shape((d_rows, width), f32),
             shape((d_rows, width), f32),
             shape((d_rows, 128), f32),
+            shape(dw_sib.shape, f32),
         ),
-        in_specs=[smem] + [vmem] * 13 + [anywhere],
-        out_specs=(vmem,) * 7,
+        in_specs=[smem] + [vmem] * 11 + [anywhere] * 5,
+        out_specs=(vmem,) * 7 + (anywhere,),
         scratch_shapes=[
-            pltpu.VMEM(wall.shape, bf16),
-            pltpu.VMEM(wall.shape, bf16),
+            pltpu.VMEM((width, 6 * half), bf16),
+            pltpu.VMEM((width, 4 * half), bf16),
+            pltpu.VMEM((2, width, half), bf16),
             pltpu.VMEM((4, width, half), bf16),
-            pltpu.VMEM((4, lines, chip_rows, half), bf16),
-            pltpu.VMEM((4, lines, chip_rows, half), bf16),
-            pltpu.VMEM((4, lines, chip_rows, half), bf16),
-            pltpu.VMEM((4, lines - 1, chip_rows, half), bf16),
-            pltpu.VMEM((4, chip_rows, half), f32),
-            pltpu.VMEM((4, d_rows, half), f32),
+            *landing(chip_rows, 4 * half),
+            pltpu.VMEM((chip_rows, 4 * half), f32),
+            pltpu.VMEM((d_rows, 4 * half), f32),
             pltpu.VMEM((width, 128), bf16),
             pltpu.VMEM((width, 128), bf16),
-            pltpu.VMEM((lines, chip_rows, 128), bf16),
-            pltpu.VMEM((lines, chip_rows, 128), bf16),
-            pltpu.VMEM((lines, chip_rows, 128), bf16),
-            pltpu.VMEM((lines - 1, chip_rows, 128), bf16),
+            *landing(chip_rows, 128),
+            pltpu.VMEM(outs.shape, bf16),
+            *landing(count, width),
             pltpu.VMEM((count, width), f32),
             pltpu.VMEM((count, width), bf16),
             pltpu.VMEM((count, width), bf16),
@@ -1296,21 +1272,21 @@
             pltpu.VMEM((count, width), bf16),
             pltpu.VMEM((count, group_len), f32),
             pltpu.VMEM((128, width), f32),
-            dma((9,)),
-            dma((9,)),
-            dma((5, 7 * lines)),
-            dma((5, 7 * lines)),
+            dma((7,)),
+            dma((7,)),
+            dma((4, 8 * lines)),
+            dma((4, 8 * lines)),
             dma((3,)),
             dma((3,)),
-            dma((1,)),
+            dma((7,)),
         ],
         compiler_params=pltpu.CompilerParams(
-            collective_id=collective_id, has_side_effects=True, vmem_limit_bytes=62 * 2**20
+            collective_id=collective_id, has_side_effects=True, vmem_limit_bytes=63 * 2**20
         ),
         name="back",
     )(
-        lengths, sums, residual, cot, group, small_t, router_part, attended, q, keys, vals, normed,
-        cosine, sine, wall,
+        lengths, dn2, residual, cot, group, small_t, router_part, attended, q, normed, cosine, sine,
+        keys, vals, wall, outs, dw_sib,
     )
 
 
@@ -1696,7 +1672,7 @@
     sel = jnp.concatenate([sel, sel])
     ones = (jnp.arange(2 * h_core, dtype=jnp.int32) % h_core)[None, :]
     ones = ((ones >= n_routed) & (ones < hidden)).astype(f32)
-    token_sums, grads_here, grads_there, router_sum = mixture_call(
+    token_grads, out_parts, grads_here, grads_away, router_sum = mixture_call(
         normed_two,
         aux,
         cot_all,
@@ -1707,10 +1683,10 @@
         ones,
         2,
     )
-    layer_output, input_grad, grad_q, grad_k, grad_v, grad_o, small_sum = back_call(
-        seq_lengths, token_sums, residual, cotangent, group_hidden, small_t, router_sum, attended,
-        queries, key_rows, value_rows, group_normed, cos_all, sin_all, w_all, d_rows, experts,
-        attn_scale, 3,
+    layer_output, input_grad, grad_q, grad_k, grad_v, grad_o, small_sum, grads_there = back_call(
+        seq_lengths, token_grads, residual, cotangent, group_hidden, small_t, router_sum, attended,
+        queries, group_normed, cos_all, sin_all, key_rows, value_rows, w_all, out_parts,
+        grads_away, d_rows, experts, attn_scale, 3,
     )
     grad_gate, grad_up, grad_down = [(grads_here[k] + grads_there[k])[:hidden] for k in range(3)]
 

time: 492 us -> 456 us (0.927)
  Pallas kernels: 406 us -> 371 us
  waiting for transfers between devices: 0.01 us -> 7.92 us
  starting transfers between devices: 20 us -> 12.9 us
    pallas_call x1, Pallas kernels: 159 us -> 122 us  [mixture_call(): pl.pallas_call(functools.partial(mixture_kernel, lines), out_shape=(jax.S...]
    pallas_call x1, Pallas kernels: 113 us -> 127 us  [back_call(): pl.pallas_call(functools.partial(back_kernel, lines, experts, scale), out...]
    pallas_call x1, Pallas kernels: 133 us -> 122 us  [front_call(): pl.pallas_call(functools.partial(front_kernel, lines, experts, scale), ou...]
    all_to_all x1, waiting for transfers between devices: 0.01 us -> 7.92 us  [small_slice(): lax.all_to_all(shared_back, AXES, split_axis=0, concat_axis=0, tiled=True)]
    all_to_all x1, starting transfers between devices: 12.2 us -> 5.43 us  [small_slice(): lax.all_to_all(shared_back, AXES, split_axis=0, concat_axis=0, tiled=True)]
    unnamed x47 -> x49, local copies, waits for them, and re-layouts: 16.5 us -> 15.6 us
  transfers between devices with their start and end apart: 2 -> 2, of which waited for: 0 -> 1; matrix products, arithmetic and copies ran while one was open for 3% -> 3% of each run, Pallas kernels for 50% -> 27%
where the time goes in v4:
time: 456 us; the launch traced here: 452 us
  Pallas kernels  371 us (81%)
  local copies, waits for them, and re-layouts  41.3 us (9%)
  other arithmetic  18.3 us (4%)
  starting transfers between devices  12.9 us (3%)
  waiting for transfers between devices  7.92 us (2%)
    pallas_call x1, Pallas kernels, back_call(): pl.pallas_call(functools.partial(back_kernel, lines, experts, scale), out...  127 us
    pallas_call x1, Pallas kernels, front_call(): pl.pallas_call(functools.partial(front_kernel, lines, experts, scale), ou...  122 us
    pallas_call x1, Pallas kernels, mixture_call(): pl.pallas_call(functools.partial(mixture_kernel, lines), out_shape=(jax.S...  122 us
    unnamed x49, local copies, waits for them, and re-layouts  15.6 us
  transfers between devices with their start and end apart: 2, of which 1 were waited for; matrix products, arithmetic and copies ran while one was open for 3% of the time, Pallas kernels for 27%

profile of v4, /device:TPU:0, one launch (start us, length us, event | category | flops | bytes accessed | tf_op | source)
XLA Modules:
  0.0 452.5 jit_solution(12530646495330799111)
XLA Ops:
  0.6 1.5 stack.26
  2.2 1.5 stack.27
  3.7 0.0 copy-start.14
  3.8 0.0 copy-start.17
  3.8 0.1 maximum_bitcast_fusion.1
  3.9 0.0 copy-start.15
  3.9 0.3 copy.86
  4.2 0.0 copy-start.13
  4.2 1.8 reshape.160
  6.0 7.5 %all-to-all-start = ((bf16[32,2,2240]{2,1,0:T(2,128)(2,1)}), bf16[32,2,2240]{2,1,0:T(2,128)(2,1)S(1)}, u32[]{:S(2)}, u32[]{:S(2)}) async-start(bf16[32,2,2240]{2,1,0:T(2,128)(2,1)} %reshape.160), calls=%async_computation | async-start | bytes 589824 | tf_op jit(solution)/shard_map/all_to_all | solution.py:1653
  13.6 0.6 and_convert_fusion.ones
  14.2 0.1 copy.71
  14.2 0.1 copy.72
  14.4 0.1 copy.73
  14.5 0.2 fusion.9.sel_t
  14.7 0.7 fusion.14.refs_4_
  15.4 0.5 fusion.23.refs_2_
  15.9 0.7 copy.74.refs_1_
  16.7 0.1 copy.78
  16.8 122.1 %front.1 = (bf16[1280,5120]{1,0:T(8,128)(2,1)}, bf16[2048,1280]{1,0:T(8,128)(2,1)}, bf16[128,1280]{1,0:T(8,128)(2,1)}, bf16[32,128]{1,0:T(8,128)(2,1)}, bf16[128...) custom-call(s32[1,3]{1,0:T(1,128)} %refs_0_.3, ...), custom_call_target="tpu_custom_call" | custom-call | tf_op jit(solution)/shard_map/front/pallas_call | solution.py:496
  138.9 0.6 maximum_maximum_fusion.sel
  139.6 1.1 fusion.8.wd
  140.7 0.8 reshape.161
  141.6 0.1 bitcast_bitcast_fusion.1
  141.6 0.1 fusion.25
  141.7 0.2 copy.83
  141.9 0.2 copy.84
  142.0 0.8 copy-done.3
  142.8 0.3 copy-done.4
  143.1 1.7 fusion.6
  144.8 121.6 %mixture.1 = (f32[128,1280]{1,0:T(8,128)}, bf16[2048,1280]{1,0:T(8,128)(2,1)}, f32[3,512,1280]{2,1,0:T(8,128)}, f32[3,512,1280]{2,1,0:T(8,128)}, f32[128,1280]{1,0:T(8,128)}) custom-call(bf16[128,1280]{1,0:T(8,128)(2,1)} %get-tuple-element.42.tok, bf16[32,128]{1,0:T(8,128)(2,1)} %get-tuple-element.43.aux, bf16[2048,1280]{1,0:T(8,128)(2,1)} %get-tuple-element.44.cot, ...), custom_call_target="tpu_custom_call" | custom-call | tf_op jit(solution)/shard_map/mixture/pallas_call | solution.py:903
  266.4 126.8 %back.1 = (bf16[128,1280]{1,0:T(8,128)(2,1)}, f32[128,1280]{1,0:T(8,128)}, f32[40,1280]{1,0:T(8,128)}, f32[40,1280]{1,0:T(8,128)}, f32[40,1280]{1,0:T(8,128)}, /...) custom-call(s32[1,3]{1,0:T(1,128)} %refs_0_.3, f32[128,1280]{1,0:T(8,128)} %get-tuple-element.46.refs_1_, ...), custom_call_target="tpu_custom_call" | custom-call | tf_op jit(solution)/shard_map/back/pallas_call | solution.py:1237
  393.3 8.0 %slice_add_fusion = (f32[1,512,1280]{2,1,0:T(8,128)S(1)}, f32[1,512,1280]{2,1,0:T(8,128)}, f32[1,512,1280]{2,1,0:T(8,128)S(1)}) fusion(f32[3,512,1280]{2,1,0:T(8,128)} %get-tuple-element.68, f32[3,512,1280]{2,1,0:T(8,128)} %get-tuple-element.67), kind=kLoop, calls=%fused_computation.7 | loop fusion | flops 1966080 | bytes 23592960 | tf_op jit(solution)/shard_map/add | solution.py:1691
  401.3 1.5 copy-done.1
  402.8 0.7 slice.105
  403.6 1.7 stack.29
  405.2 1.7 slice.106
  406.9 2.6 stack.30
  409.5 2.6 maximum_bitcast_fusion
  412.1 4.0 copy.79
  416.1 3.5 reshape.162
  419.6 5.4 %all-to-all-start.1 = ((f32[32,1,4480]{2,1,0:T(1,128)}), f32[32,1,4480]{2,1,0:T(1,128)S(1)}, u32[]{:S(2)}, u32[]{:S(2)}) async-start(f32[32,1,4480]{2,1,0:T(1,128)} %reshape.162), calls=%async_computation.1 | async-start | bytes 1146880 | tf_op jit(solution)/shard_map/all_to_all | solution.py:1695
  425.1 3.3 slice.110
  428.4 1.5 slice.111
  430.0 1.5 slice.112
  431.5 0.7 copy.82
  432.2 0.7 slice_reduce_fusion
  432.9 0.7 slice_bitcast_fusion
  433.6 7.9 %all-to-all-done.1 = f32[32,1,4480]{2,1,0:T(1,128)S(1)} async-done(((f32[32,1,4480]{2,1,0:T(1,128)}), f32[32,1,4480]{2,1,0:T(1,128)S(1)}, u32[]{:S(2)}, u32[]{:S(2)}) %all-to-all-start.1) | async-done | bytes 573472 | tf_op jit(solution)/shard_map/all_to_all | solution.py:1695
  441.5 0.5 broadcast.137
  442.0 2.0 reduce.4
  444.0 1.0 reshape.163
  445.0 0.1 bitcast_bitcast_fusion
  445.1 0.1 fusion.24
  445.2 0.1 copy.80
  445.4 1.1 squeeze.28
  446.4 0.1 copy.81
  446.6 1.1 squeeze.29
  447.7 0.7 copy.93
  448.4 0.8 copy.94
  449.2 0.7 copy.95
  449.9 0.7 copy.96
  450.6 0.7 copy.97
  451.3 0.7 copy.98
  (34 shorter events, 0.1 us)
Async XLA Ops:
  3.7 10.4 %copy-start.14 = (bf16[40,16]{0,1:T(8,128)(2,1)S(1)}, bf16[40,16]{0,1:T(8,128)(2,1)}, u32[]{:S(2)}) copy-start(bf16[40,16]{0,1:T(8,128)(2,1)} %param.29) | copy-start | bytes 3844
  3.7 10.5 %copy-start.16 = (bf16[40]{0:T(256)(128)(2,1)S(1)}, bf16[40]{0:T(256)(128)(2,1)}, u32[]{:S(2)}) copy-start(bf16[40]{0:T(256)(128)(2,1)} %param.20) | copy-start | bytes 244
  3.8 10.6 %copy-start.17 = (bf16[40]{0:T(256)(128)(2,1)S(1)}, bf16[40]{0:T(256)(128)(2,1)}, u32[]{:S(2)}) copy-start(bf16[40]{0:T(256)(128)(2,1)} %param.25) | copy-start | bytes 244
  3.9 12.0 %copy-start.15 = (s32[128,7]{0,1:T(8,128)S(1)}, s32[128,7]{0,1:T(8,128)}, u32[]{:S(2)}) copy-start(s32[128,7]{0,1:T(8,128)} %param.19) | copy-start | bytes 10756
  4.2 135.4 %copy-start.5 = (bf16[2,224,1280]{2,1,0:T(8,128)(2,1)S(1)}, bf16[2,224,1280]{2,1,0:T(8,128)(2,1)}, u32[]{:S(2)}) copy-start(bf16[2,224,1280]{2,1,0:T(8,128)(2,1)} %param.32) | copy-start | bytes 3440644
  4.2 135.4 %copy-start.13 = (bf16[56,1280]{1,0:T(8,128)(2,1)S(1)}, bf16[56,1280]{1,0:T(8,128)(2,1)}, u32[]{:S(2)}) copy-start(bf16[56,1280]{1,0:T(8,128)(2,1)} %param.28) | copy-start | bytes 430084
  6.0 134.7 %all-to-all-start = ((bf16[32,2,2240]{2,1,0:T(2,128)(2,1)}), bf16[32,2,2240]{2,1,0:T(2,128)(2,1)S(1)}, u32[]{:S(2)}, u32[]{:S(2)}) async-start(bf16[32,2,2240]{2,1,0:T(2,128)(2,1)} %reshape.160), calls=%async_computation | async-start | bytes 589824 | tf_op jit(solution)/shard_map/all_to_all | solution.py:1653
  14.7 126.0 %copy-start.2 = (bf16[1024,128]{1,0:T(8,128)(2,1)}, bf16[1024,128]{1,0:T(8,128)(2,1)S(1)}, u32[]{:S(2)}) copy-start(bf16[1024,128]{1,0:T(8,128)(2,1)S(1)} %fusion.9.sel_t) | copy-start | bytes 786436
  141.5 1.3 copy-start.3
  141.5 1.6 copy-start.4
  401.3 1.5 copy-start.1
  419.6 21.9 %all-to-all-start.1 = ((f32[32,1,4480]{2,1,0:T(1,128)}), f32[32,1,4480]{2,1,0:T(1,128)S(1)}, u32[]{:S(2)}, u32[]{:S(2)}) async-start(f32[32,1,4480]{2,1,0:T(1,128)} %reshape.162), calls=%async_computation.1 | async-start | bytes 1146880 | tf_op jit(solution)/shard_map/all_to_all | solution.py:1695
  425.1 3.3 copy-start
  429.9 1.5 copy-start.12
  445.3 2.3 copy-start.7
  445.4 3.0 copy-start.6
  446.4 2.8 copy-start.11
  446.6 3.3 copy-start.10
  446.6 4.0 copy-start.9
  447.7 3.6 copy-start.8
